TPU v7x, 32 devices: a whole 2x2x4 slice. The times are simulated.
32 devices in a mesh: members: 2 (over y), tile: 4 (over z), group: 4 (over x, core).
Axes of the slice: x: 2, y: 2, z: 4, core: 2. Of those that a mesh axis runs over, the one named last changes fastest.
Arguments:
- theta: float32 [16, 16, 128], P('members', 'tile'), parts along dimension 0, may hold values from -6 to 6
- tracers: float32 [4, 96, 8, 16, 128], P('group', 'members', None, 'tile'), parts along dimension 1, may hold values from -6 to 6
- counts: int32 [4, 2], P('group', 'members'), parts along dimension 1, may hold values from 0 to 48, as said below
- flags: int32 [4, 96], P('group', 'members'), parts along dimension 1, may hold values 0 or 1
- kappa: float32 [4, 48], P('group'), may hold values from 0.02 to 0.2
Outputs:
- theta_out: float32 [16, 16, 128], P('members', 'tile'), parts along dimension 0
- tracers_out: float32 [4, 96, 8, 16, 128], P('group', 'members', None, 'tile'), parts along dimension 1
There are 2 independent parts, one for each index of `members`. A program takes and returns all parts, laid end to end along the dimension named above; an argument that names none is the same for every part. Nothing has to cross between parts.
Inputs may be any that keep to these rules, and one draw needn't show every extreme that they name: counts[0, 0] is 0 (the dynamics group holds no tracers); every other group has 12 to 48 live slots, and some group has exactly 48.
All inputs are finite; a program needn't handle non-finite values. No bound on the sum of `flags` on one device may be relied on, other than what follows from the above.
Results may differ from a plain program's by a relative error of at most 0.00012.
Values sent between devices are 32-bit elements; how exact they have to be, the bound alone decides.
No kernel may reach another device: no remote copies, remote signals or barrier semaphores. Data moves between devices by JAX's collectives and lax.ppermute only.
A program may use at most 64 MiB of HBM per device.

v0:
```python
import jax
import jax.numpy as jnp
from jax import lax
from jax.sharding import PartitionSpec as P

STEPS = 3
INTERVALS = 2


wind_scale = 0.3
vert_scale = 0.2
mix_base = 0.08
heat_step = 0.3


def with_halo(array, sides, width):
    for axis, dim in sides:
        size, length = (lax.axis_size(axis), array.shape[dim])
        up = [(i, (i + 1) % size) for i in range(size)]
        down = [(j, i) for i, j in up]
        last = lax.slice_in_dim(array, length - width, length, axis=dim)
        leading = lax.slice_in_dim(array, 0, width, axis=dim)
        before = lax.ppermute(last, axis, up)
        after = lax.ppermute(leading, axis, down)
        array = jnp.concatenate([before, array, after], axis=dim)
    return array


def fields(theta_ext):
    center = theta_ext[:, 1:-1, :]
    grad_x = (theta_ext[:, 2:, :] - theta_ext[:, :-2, :]) * 0.5
    pad_y = jnp.pad(center, ((0, 0), (0, 0), (1, 1)))
    grad_y = (pad_y[:, :, 2:] - pad_y[:, :, :-2]) * 0.5
    pad_z = jnp.pad(center, ((1, 1), (0, 0), (0, 0)))
    grad_z = (pad_z[2:] - pad_z[:-2]) * 0.5
    wind_x = -wind_scale * grad_y
    wind_y = wind_scale * grad_x
    wind_z = vert_scale * grad_z
    mixing = mix_base * (1.0 + 0.5 * jnp.tanh(center))
    return jnp.stack([wind_x, wind_y, wind_z, mixing])


def tendency(extended, stacked):
    center = extended[..., 1:-1, :]
    east = extended[..., 2:, :]
    west = extended[..., :-2, :]
    ndims = center.ndim
    pad_y = jnp.pad(center, [(0, 0)] * (ndims - 1) + [(1, 1)])
    north = pad_y[..., 2:]
    south = pad_y[..., :-2]
    pad_z = jnp.pad(center, [(0, 0)] * (ndims - 3) + [(1, 1), (0, 0), (0, 0)])
    upper = pad_z[..., 2:, :, :]
    lower = pad_z[..., :-2, :, :]
    advect = (
        stacked[0] * (east - west) * 0.5
        + stacked[1] * (north - south) * 0.5
        + stacked[2] * (upper - lower) * 0.5
    )
    return -advect + stacked[3] * (east + west + north + south + upper + lower - 6.0 * center)


def tracer_edges(field):
    return with_halo(field, (("tile", 2),), 1)


def per_device(theta, tracers, counts, flags, kappa):
    slots = tracers.shape[1]
    live = (jnp.arange(slots, dtype=jnp.int32) < counts[0, 0]).astype(jnp.float32)
    weight = flags[0].astype(jnp.float32) * kappa[0] * live
    state = tracers[0] * live[:, None, None, None]
    for interval in range(INTERVALS):
        theta_ext = with_halo(theta, (("tile", 1),), 1)
        stacked = fields(theta_ext)
        for _ in range(STEPS):
            first = state + tendency(tracer_edges(state), stacked)
            state = 0.5 * (state + first + tendency(tracer_edges(first), stacked))
        partial_value = jnp.einsum("t,tzxy->zxy", weight, state, precision=lax.Precision.HIGHEST)
        heating = lax.psum(partial_value, "group")
        theta = theta + heat_step * heating
    return (theta, state[None])


def solution(mesh):
    return jax.shard_map(
        per_device,
        mesh=mesh,
        in_specs=(
            P("members", "tile", None),
            P("group", "members", None, "tile", None),
            P("group", "members"),
            P("group", "members"),
            P("group", None),
        ),
        out_specs=(P("members", "tile", None), P("group", "members", None, "tile", None)),
        check_vma=False,
    )
```

profile of v0, /device:TPU:0, one launch (start us, length us, event | category | flops | bytes accessed | tf_op | source)
XLA Modules:
  0.0 191.1 jit_solution(9651993655470464608)
XLA Ops:
  0.6 0.8 fusion.32
  1.4 5.1 %collective-permute-start.2 = (f32[8,1,128]{2,1,0:T(1,128)S(1)}, f32[8,1,128]{2,1,0:T(1,128)S(1)}, u32[]{:S(2)}, u32[]{:S(2)}) collective-permute-start(f32[8,1,128]{2,1,0:T(1,128)S(1)} %get-tuple-element.47), channel_id=1, source_target_pairs={{4,0},{8,4},{12,8},{0,12},{5,1},{9,5},{13,9},{1,13},{6,2},{10,6},{... | collective-permute-start | bytes 12296 | tf_op jit(solution)/shard_map/ppermute | solution.py:24
  7.2 1.3 bitcast_multiply_fusion
  8.9 3.9 %collective-permute-start = (f32[48,8,1,128]{3,2,1,0:T(1,128)S(1)}, f32[48,8,1,128]{3,2,1,0:T(1,128)S(1)}, u32[]{:S(2)}, u32[]{:S(2)}) collective-permute-start(f32[48,8,1,128]{3,2,1,0:T(1,128)S(1)} %get-tuple-element.37), channel_id=1, source_target_pairs={{4,0},{8,4},{12,8},{0,12},{5,1},{9,5},{13,9},{1,13},{6,2},{10,6},{... | collective-permute-start | bytes 589832 | tf_op jit(solution)/shard_map/ppermute | solution.py:24
  12.9 5.7 %collective-permute-done.1 = f32[48,8,1,128]{3,2,1,0:T(1,128)S(1)} collective-permute-done((f32[48,8,1,128]{3,2,1,0:T(1,128)S(1)}, f32[48,8,1,128]{3,2,1,0:T(1,128)S(1)}, u32[]{:S(2)}, u32[]{:S(2)}) %collective-permute-start.1) | collective-permute-done | bytes 196640 | tf_op jit(solution)/shard_map/ppermute | solution.py:23
  18.6 1.0 collective-permute-done
  19.6 2.0 %add_add_fusion.10 = f32[48,8,4,128]{3,2,1,0:T(4,128)S(1)} fusion(f32[48,8,4,128]{3,2,1,0:T(4,128)S(1)} %bitcast_multiply_fusion, f32[48,8,1,128]{3,2,1,0:T(1,128)S(1)} %collective-permute-done, f32[48,8,1,128]{3,2,1,0:T(1,128)S(1)} %collective-permute-done.1, f32[8,4,128]{2,1,0:T(4,128)S(1)} %get-tuple-element.46, f32[8,4,128]{2,1,0:T(4,128)S(1)} %get-tuple-element.44, ...), kind=kLoop, calls=%fused_computation.88 | loop fusion | flops 4325376 | bytes 2031616 | tf_op jit(solution)/shard_map/add | solution.py:75
  22.0 3.5 %collective-permute-start.4 = (f32[48,8,1,128]{3,2,1,0:T(1,128)S(1)}, f32[48,8,1,128]{3,2,1,0:T(1,128)S(1)}, u32[]{:S(2)}, u32[]{:S(2)}) collective-permute-start(f32[48,8,1,128]{3,2,1,0:T(1,128)S(1)} %get-tuple-element.34), channel_id=1, source_target_pairs={{4,0},{8,4},{12,8},{0,12},{5,1},{9,5},{13,9},{1,13},{6,2},{10,6},{... | collective-permute-start | bytes 589832 | tf_op jit(solution)/shard_map/ppermute | solution.py:24
  25.5 5.8 %collective-permute-done.4 = f32[48,8,1,128]{3,2,1,0:T(1,128)S(1)} collective-permute-done((f32[48,8,1,128]{3,2,1,0:T(1,128)S(1)}, f32[48,8,1,128]{3,2,1,0:T(1,128)S(1)}, u32[]{:S(2)}, u32[]{:S(2)}) %collective-permute-start.4) | collective-permute-done | bytes 196640 | tf_op jit(solution)/shard_map/ppermute | solution.py:24
  31.3 2.6 %collective-permute-done.5 = f32[48,8,1,128]{3,2,1,0:T(1,128)S(1)} collective-permute-done((f32[48,8,1,128]{3,2,1,0:T(1,128)S(1)}, f32[48,8,1,128]{3,2,1,0:T(1,128)S(1)}, u32[]{:S(2)}, u32[]{:S(2)}) %collective-permute-start.5) | collective-permute-done | bytes 196640 | tf_op jit(solution)/shard_map/ppermute | solution.py:23
  33.8 2.3 %broadcast_multiply_fusion.4 = (f32[48,8,4,128]{3,2,1,0:T(4,128)S(1)}, f32[48,8,4,128]{3,2,1,0:T(4,128)S(1)}) fusion(f32[48,8,4,128]{3,2,1,0:T(4,128)S(1)} %add_add_fusion.10, f32[8,4,128]{2,1,0:T(4,128)S(1)} %get-tuple-element.46, f32[8,4,128]{2,1,0:T(4,128)S(1)} %get-tuple-element.44, f32[8,4,128]{2,1,0:T(4,128)S(1)} %get-tuple-element.45, ...), kind=kLoop, calls=%fused_computation.93 | loop fusion | flops 4915200 | bytes 3604672 | tf_op jit(solution)/shard_map/mul | solution.py:76
  36.5 1.5 collective-permute-start.7
  38.0 2.3 %collective-permute-start.6 = (f32[48,8,1,128]{3,2,1,0:T(1,128)S(1)}, f32[48,8,1,128]{3,2,1,0:T(1,128)S(1)}, u32[]{:S(2)}, u32[]{:S(2)}) collective-permute-start(f32[48,8,1,128]{3,2,1,0:T(1,128)S(1)} %get-tuple-element.33), channel_id=1, source_target_pairs={{4,0},{8,4},{12,8},{0,12},{5,1},{9,5},{13,9},{1,13},{6,2},{10,6},{... | collective-permute-start | bytes 589832 | tf_op jit(solution)/shard_map/ppermute | solution.py:24
  40.4 5.7 %collective-permute-done.7 = f32[48,8,1,128]{3,2,1,0:T(1,128)S(1)} collective-permute-done((f32[48,8,1,128]{3,2,1,0:T(1,128)S(1)}, f32[48,8,1,128]{3,2,1,0:T(1,128)S(1)}, u32[]{:S(2)}, u32[]{:S(2)}) %collective-permute-start.7) | collective-permute-done | bytes 196640 | tf_op jit(solution)/shard_map/ppermute | solution.py:23
  46.1 1.1 collective-permute-done.6
  47.1 2.0 %add_add_fusion.8 = f32[48,8,4,128]{3,2,1,0:T(4,128)S(1)} fusion(f32[48,8,4,128]{3,2,1,0:T(4,128)S(1)} %get-tuple-element.12, f32[48,8,4,128]{3,2,1,0:T(4,128)S(1)} %get-tuple-element.13, f32[48,8,1,128]{3,2,1,0:T(1,128)S(1)} %collective-permute-done.6, f32[48,8,1,128]{3,2,1,0:T(1,128)S(1)} %collective-permute-done.7, ...), kind=kLoop, calls=%fused_computation.86 | loop fusion | flops 4325376 | bytes 2818048 | tf_op jit(solution)/shard_map/add | solution.py:75
  49.5 2.8 %collective-permute-start.8 = (f32[48,8,1,128]{3,2,1,0:T(1,128)S(1)}, f32[48,8,1,128]{3,2,1,0:T(1,128)S(1)}, u32[]{:S(2)}, u32[]{:S(2)}) collective-permute-start(f32[48,8,1,128]{3,2,1,0:T(1,128)S(1)} %get-tuple-element.30), channel_id=1, source_target_pairs={{4,0},{8,4},{12,8},{0,12},{5,1},{9,5},{13,9},{1,13},{6,2},{10,6},{... | collective-permute-start | bytes 589832 | tf_op jit(solution)/shard_map/ppermute | solution.py:24
  52.3 5.8 %collective-permute-done.8 = f32[48,8,1,128]{3,2,1,0:T(1,128)S(1)} collective-permute-done((f32[48,8,1,128]{3,2,1,0:T(1,128)S(1)}, f32[48,8,1,128]{3,2,1,0:T(1,128)S(1)}, u32[]{:S(2)}, u32[]{:S(2)}) %collective-permute-start.8) | collective-permute-done | bytes 196640 | tf_op jit(solution)/shard_map/ppermute | solution.py:24
  58.1 2.6 %collective-permute-done.9 = f32[48,8,1,128]{3,2,1,0:T(1,128)S(1)} collective-permute-done((f32[48,8,1,128]{3,2,1,0:T(1,128)S(1)}, f32[48,8,1,128]{3,2,1,0:T(1,128)S(1)}, u32[]{:S(2)}, u32[]{:S(2)}) %collective-permute-start.9) | collective-permute-done | bytes 196640 | tf_op jit(solution)/shard_map/ppermute | solution.py:23
  60.6 2.2 %broadcast_multiply_fusion.3 = (f32[48,8,4,128]{3,2,1,0:T(4,128)S(1)}, f32[48,8,4,128]{3,2,1,0:T(4,128)S(1)}) fusion(f32[48,8,4,128]{3,2,1,0:T(4,128)S(1)} %add_add_fusion.8, f32[8,4,128]{2,1,0:T(4,128)S(1)} %get-tuple-element.46, f32[8,4,128]{2,1,0:T(4,128)S(1)} %get-tuple-element.44, f32[8,4,128]{2,1,0:T(4,128)S(1)} %get-tuple-element.45, ...), kind=kLoop, calls=%fused_computation.92 | loop fusion | flops 4915200 | bytes 3604480 | tf_op jit(solution)/shard_map/mul | solution.py:76
  63.1 1.5 collective-permute-start.11
  64.7 2.3 %collective-permute-start.10 = (f32[48,8,1,128]{3,2,1,0:T(1,128)S(1)}, f32[48,8,1,128]{3,2,1,0:T(1,128)S(1)}, u32[]{:S(2)}, u32[]{:S(2)}) collective-permute-start(f32[48,8,1,128]{3,2,1,0:T(1,128)S(1)} %get-tuple-element.29), channel_id=1, source_target_pairs={{4,0},{8,4},{12,8},{0,12},{5,1},{9,5},{13,9},{1,13},{6,2},{10,6},{... | collective-permute-start | bytes 589832 | tf_op jit(solution)/shard_map/ppermute | solution.py:24
  67.0 5.4 %collective-permute-done.11 = f32[48,8,1,128]{3,2,1,0:T(1,128)S(1)} collective-permute-done((f32[48,8,1,128]{3,2,1,0:T(1,128)S(1)}, f32[48,8,1,128]{3,2,1,0:T(1,128)S(1)}, u32[]{:S(2)}, u32[]{:S(2)}) %collective-permute-start.11) | collective-permute-done | bytes 196640 | tf_op jit(solution)/shard_map/ppermute | solution.py:23
  72.4 0.5 collective-permute-done.10
  72.9 2.0 %add_add_fusion.6 = f32[48,8,4,128]{3,2,1,0:T(4,128)S(1)} fusion(f32[48,8,4,128]{3,2,1,0:T(4,128)S(1)} %get-tuple-element.10, f32[48,8,4,128]{3,2,1,0:T(4,128)S(1)} %get-tuple-element.11, f32[48,8,1,128]{3,2,1,0:T(1,128)S(1)} %collective-permute-done.10, f32[48,8,1,128]{3,2,1,0:T(1,128)S(1)} %collective-permute-done.11, ...), kind=kLoop, calls=%fused_computation.84 | loop fusion | flops 4325376 | bytes 2818048 | tf_op jit(solution)/shard_map/add | solution.py:75
  75.2 3.2 %collective-permute-start.12 = (f32[48,8,1,128]{3,2,1,0:T(1,128)S(1)}, f32[48,8,1,128]{3,2,1,0:T(1,128)S(1)}, u32[]{:S(2)}, u32[]{:S(2)}) collective-permute-start(f32[48,8,1,128]{3,2,1,0:T(1,128)S(1)} %get-tuple-element.26), channel_id=1, source_target_pairs={{4,0},{8,4},{12,8},{0,12},{5,1},{9,5},{13,9},{1,13},{6,2},{10,6},{... | collective-permute-start | bytes 589832 | tf_op jit(solution)/shard_map/ppermute | solution.py:24
  78.4 5.8 %collective-permute-done.12 = f32[48,8,1,128]{3,2,1,0:T(1,128)S(1)} collective-permute-done((f32[48,8,1,128]{3,2,1,0:T(1,128)S(1)}, f32[48,8,1,128]{3,2,1,0:T(1,128)S(1)}, u32[]{:S(2)}, u32[]{:S(2)}) %collective-permute-start.12) | collective-permute-done | bytes 196640 | tf_op jit(solution)/shard_map/ppermute | solution.py:24
  84.3 2.6 %collective-permute-done.13 = f32[48,8,1,128]{3,2,1,0:T(1,128)S(1)} collective-permute-done((f32[48,8,1,128]{3,2,1,0:T(1,128)S(1)}, f32[48,8,1,128]{3,2,1,0:T(1,128)S(1)}, u32[]{:S(2)}, u32[]{:S(2)}) %collective-permute-start.13) | collective-permute-done | bytes 196640 | tf_op jit(solution)/shard_map/ppermute | solution.py:23
  86.8 2.2 %broadcast_multiply_fusion.2 = (f32[48,8,4,128]{3,2,1,0:T(4,128)S(1)}, f32[48,8,4,128]{3,2,1,0:T(4,128)S(1)}) fusion(f32[48,8,4,128]{3,2,1,0:T(4,128)S(1)} %add_add_fusion.6, f32[8,4,128]{2,1,0:T(4,128)S(1)} %get-tuple-element.46, f32[8,4,128]{2,1,0:T(4,128)S(1)} %get-tuple-element.44, f32[8,4,128]{2,1,0:T(4,128)S(1)} %get-tuple-element.45, ...), kind=kLoop, calls=%fused_computation.91 | loop fusion | flops 4915200 | bytes 3604480 | tf_op jit(solution)/shard_map/mul | solution.py:76
  89.7 0.9 fusion.2
  90.6 10.1 %psum.14 = f32[8,4,128]{2,1,0:T(4,128)S(1)} all-reduce(f32[8,4,128]{2,1,0:T(4,128)S(1)} %bitcast.27), channel_id=1, replica_groups=mesh['members'=2,'tile'=4,'group'=4] {'group'}, use_global_device_ids=true, to_apply=%region_0.1 | all-reduce | flops 4096 | bytes 32768 | tf_op jit(solution)/shard_map/psum | solution.py:78
  100.7 1.7 collective-permute-start.15
  102.4 2.3 %collective-permute-start.14 = (f32[48,8,1,128]{3,2,1,0:T(1,128)S(1)}, f32[48,8,1,128]{3,2,1,0:T(1,128)S(1)}, u32[]{:S(2)}, u32[]{:S(2)}) collective-permute-start(f32[48,8,1,128]{3,2,1,0:T(1,128)S(1)} %get-tuple-element.25), channel_id=1, source_target_pairs={{4,0},{8,4},{12,8},{0,12},{5,1},{9,5},{13,9},{1,13},{6,2},{10,6},{... | collective-permute-start | bytes 589832 | tf_op jit(solution)/shard_map/ppermute | solution.py:24
  105.0 1.8 collective-permute-start.17
  106.9 5.9 %collective-permute-done.16 = f32[8,1,128]{2,1,0:T(1,128)S(1)} collective-permute-done((f32[8,1,128]{2,1,0:T(1,128)S(1)}, f32[8,1,128]{2,1,0:T(1,128)S(1)}, u32[]{:S(2)}, u32[]{:S(2)}) %collective-permute-start.16) | collective-permute-done | bytes 4128 | tf_op jit(solution)/shard_map/ppermute | solution.py:24
  112.8 0.7 collective-permute-done.17
  113.6 2.0 %add_add_fusion.4 = f32[48,8,4,128]{3,2,1,0:T(4,128)S(1)} fusion(f32[48,8,4,128]{3,2,1,0:T(4,128)S(1)} %get-tuple-element.8, f32[48,8,4,128]{3,2,1,0:T(4,128)S(1)} %get-tuple-element.9, f32[48,8,1,128]{3,2,1,0:T(1,128)S(1)} %collective-permute-done.14, f32[48,8,1,128]{3,2,1,0:T(1,128)S(1)} %collective-permute-done.15, f32[8,4,128]{2,1,0:T(4,128)S(1)} %get-tuple-element.6, ...), kind=kLoop, calls=%fused_computation.82 | loop fusion | flops 4325376 | bytes 2818048 | tf_op jit(solution)/shard_map/add | solution.py:75
  115.9 1.4 collective-permute-start.18
  117.3 0.6 collective-permute-start.19
  118.0 5.7 %collective-permute-done.18 = f32[48,8,1,128]{3,2,1,0:T(1,128)S(1)} collective-permute-done((f32[48,8,1,128]{3,2,1,0:T(1,128)S(1)}, f32[48,8,1,128]{3,2,1,0:T(1,128)S(1)}, u32[]{:S(2)}, u32[]{:S(2)}) %collective-permute-start.18) | collective-permute-done | bytes 196640 | tf_op jit(solution)/shard_map/ppermute | solution.py:24
  123.7 2.1 %collective-permute-done.19 = f32[48,8,1,128]{3,2,1,0:T(1,128)S(1)} collective-permute-done((f32[48,8,1,128]{3,2,1,0:T(1,128)S(1)}, f32[48,8,1,128]{3,2,1,0:T(1,128)S(1)}, u32[]{:S(2)}, u32[]{:S(2)}) %collective-permute-start.19) | collective-permute-done | bytes 196640 | tf_op jit(solution)/shard_map/ppermute | solution.py:23
  125.8 2.2 %broadcast_multiply_fusion.1 = (f32[48,8,4,128]{3,2,1,0:T(4,128)S(1)}, f32[48,8,4,128]{3,2,1,0:T(4,128)S(1)}) fusion(f32[48,8,4,128]{3,2,1,0:T(4,128)S(1)} %add_add_fusion.4, f32[8,4,128]{2,1,0:T(4,128)S(1)} %get-tuple-element.6, f32[8,4,128]{2,1,0:T(4,128)S(1)} %get-tuple-element.39, f32[8,4,128]{2,1,0:T(4,128)S(1)} %get-tuple-element.40, ...), kind=kLoop, calls=%fused_computation.90 | loop fusion | flops 4915200 | bytes 3604480 | tf_op jit(solution)/shard_map/mul | solution.py:76
  128.3 1.1 collective-permute-start.21
  129.4 2.8 %collective-permute-start.20 = (f32[48,8,1,128]{3,2,1,0:T(1,128)S(1)}, f32[48,8,1,128]{3,2,1,0:T(1,128)S(1)}, u32[]{:S(2)}, u32[]{:S(2)}) collective-permute-start(f32[48,8,1,128]{3,2,1,0:T(1,128)S(1)} %get-tuple-element.21), channel_id=1, source_target_pairs={{4,0},{8,4},{12,8},{0,12},{5,1},{9,5},{13,9},{1,13},{6,2},{10,6},{... | collective-permute-start | bytes 589832 | tf_op jit(solution)/shard_map/ppermute | solution.py:24
  132.2 5.4 %collective-permute-done.21 = f32[48,8,1,128]{3,2,1,0:T(1,128)S(1)} collective-permute-done((f32[48,8,1,128]{3,2,1,0:T(1,128)S(1)}, f32[48,8,1,128]{3,2,1,0:T(1,128)S(1)}, u32[]{:S(2)}, u32[]{:S(2)}) %collective-permute-start.21) | collective-permute-done | bytes 196640 | tf_op jit(solution)/shard_map/ppermute | solution.py:23
  137.6 0.8 collective-permute-done.20
  138.4 2.0 %add_add_fusion.2 = f32[48,8,4,128]{3,2,1,0:T(4,128)S(1)} fusion(f32[48,8,4,128]{3,2,1,0:T(4,128)S(1)} %get-tuple-element.4, f32[48,8,4,128]{3,2,1,0:T(4,128)S(1)} %get-tuple-element.5, f32[48,8,1,128]{3,2,1,0:T(1,128)S(1)} %collective-permute-done.20, f32[48,8,1,128]{3,2,1,0:T(1,128)S(1)} %collective-permute-done.21, f32[8,4,128]{2,1,0:T(4,128)S(1)} %get-tuple-element.6, ...), kind=kLoop, calls=%fused_computation.80 | loop fusion | flops 4325376 | bytes 2818048 | tf_op jit(solution)/shard_map/add | solution.py:75
  140.8 2.6 %collective-permute-start.22 = (f32[48,8,1,128]{3,2,1,0:T(1,128)S(1)}, f32[48,8,1,128]{3,2,1,0:T(1,128)S(1)}, u32[]{:S(2)}, u32[]{:S(2)}) collective-permute-start(f32[48,8,1,128]{3,2,1,0:T(1,128)S(1)} %get-tuple-element.18), channel_id=1, source_target_pairs={{4,0},{8,4},{12,8},{0,12},{5,1},{9,5},{13,9},{1,13},{6,2},{10,6},{... | collective-permute-start | bytes 589832 | tf_op jit(solution)/shard_map/ppermute | solution.py:24
  143.4 6.1 %collective-permute-done.22 = f32[48,8,1,128]{3,2,1,0:T(1,128)S(1)} collective-permute-done((f32[48,8,1,128]{3,2,1,0:T(1,128)S(1)}, f32[48,8,1,128]{3,2,1,0:T(1,128)S(1)}, u32[]{:S(2)}, u32[]{:S(2)}) %collective-permute-start.22) | collective-permute-done | bytes 196640 | tf_op jit(solution)/shard_map/ppermute | solution.py:24
  149.5 2.6 %collective-permute-done.23 = f32[48,8,1,128]{3,2,1,0:T(1,128)S(1)} collective-permute-done((f32[48,8,1,128]{3,2,1,0:T(1,128)S(1)}, f32[48,8,1,128]{3,2,1,0:T(1,128)S(1)}, u32[]{:S(2)}, u32[]{:S(2)}) %collective-permute-start.23) | collective-permute-done | bytes 196640 | tf_op jit(solution)/shard_map/ppermute | solution.py:23
  152.1 2.2 %broadcast_multiply_fusion = (f32[48,8,4,128]{3,2,1,0:T(4,128)S(1)}, f32[48,8,4,128]{3,2,1,0:T(4,128)S(1)}) fusion(f32[48,8,4,128]{3,2,1,0:T(4,128)S(1)} %add_add_fusion.2, f32[8,4,128]{2,1,0:T(4,128)S(1)} %get-tuple-element.6, f32[8,4,128]{2,1,0:T(4,128)S(1)} %get-tuple-element.39, f32[8,4,128]{2,1,0:T(4,128)S(1)} %get-tuple-element.40, ...), kind=kLoop, calls=%fused_computation.89 | loop fusion | flops 4915200 | bytes 3604480 | tf_op jit(solution)/shard_map/mul | solution.py:76
  154.6 1.5 collective-permute-start.25
  156.1 2.3 %collective-permute-start.24 = (f32[48,8,1,128]{3,2,1,0:T(1,128)S(1)}, f32[48,8,1,128]{3,2,1,0:T(1,128)S(1)}, u32[]{:S(2)}, u32[]{:S(2)}) collective-permute-start(f32[48,8,1,128]{3,2,1,0:T(1,128)S(1)} %get-tuple-element.17), channel_id=1, source_target_pairs={{4,0},{8,4},{12,8},{0,12},{5,1},{9,5},{13,9},{1,13},{6,2},{10,6},{... | collective-permute-start | bytes 589832 | tf_op jit(solution)/shard_map/ppermute | solution.py:24
  158.5 5.3 %collective-permute-done.25 = f32[48,8,1,128]{3,2,1,0:T(1,128)S(1)} collective-permute-done((f32[48,8,1,128]{3,2,1,0:T(1,128)S(1)}, f32[48,8,1,128]{3,2,1,0:T(1,128)S(1)}, u32[]{:S(2)}, u32[]{:S(2)}) %collective-permute-start.25) | collective-permute-done | bytes 196640 | tf_op jit(solution)/shard_map/ppermute | solution.py:23
  163.7 0.4 collective-permute-done.24
  164.1 2.0 %add_add_fusion = f32[48,8,4,128]{3,2,1,0:T(4,128)S(1)} fusion(f32[48,8,4,128]{3,2,1,0:T(4,128)S(1)} %get-tuple-element.2, f32[48,8,4,128]{3,2,1,0:T(4,128)S(1)} %get-tuple-element.3, f32[48,8,1,128]{3,2,1,0:T(1,128)S(1)} %collective-permute-done.24, f32[48,8,1,128]{3,2,1,0:T(1,128)S(1)} %collective-permute-done.25, f32[8,4,128]{2,1,0:T(4,128)S(1)} %get-tuple-element.6, ...), kind=kLoop, calls=%fused_computation.78 | loop fusion | flops 4325376 | bytes 2818048 | tf_op jit(solution)/shard_map/add | solution.py:75
  166.5 2.1 %collective-permute-start.27 = (f32[48,8,1,128]{3,2,1,0:T(1,128)S(1)}, f32[48,8,1,128]{3,2,1,0:T(1,128)S(1)}, u32[]{:S(2)}, u32[]{:S(2)}) collective-permute-start(f32[48,8,1,128]{3,2,1,0:T(1,128)S(1)} %get-tuple-element.14), channel_id=1, source_target_pairs={{0,4},{4,8},{8,12},{12,0},{1,5},{5,9},{9,13},{13,1},{2,6},{6,10},{... | collective-permute-start | bytes 589832 | tf_op jit(solution)/shard_map/ppermute | solution.py:23
  168.6 1.8 collective-permute-start.26
  170.3 3.8 %collective-permute-done.27 = f32[48,8,1,128]{3,2,1,0:T(1,128)S(1)} collective-permute-done((f32[48,8,1,128]{3,2,1,0:T(1,128)S(1)}, f32[48,8,1,128]{3,2,1,0:T(1,128)S(1)}, u32[]{:S(2)}, u32[]{:S(2)}) %collective-permute-start.27) | collective-permute-done | bytes 196640 | tf_op jit(solution)/shard_map/ppermute | solution.py:23
  174.1 3.1 %collective-permute-done.26 = f32[48,8,1,128]{3,2,1,0:T(1,128)S(1)} collective-permute-done((f32[48,8,1,128]{3,2,1,0:T(1,128)S(1)}, f32[48,8,1,128]{3,2,1,0:T(1,128)S(1)}, u32[]{:S(2)}, u32[]{:S(2)}) %collective-permute-start.26) | collective-permute-done | bytes 196640 | tf_op jit(solution)/shard_map/ppermute | solution.py:24
  177.2 2.2 %add_multiply_fusion = f32[48,8,4,128]{3,2,1,0:T(4,128)S(1)} fusion(f32[48,8,4,128]{3,2,1,0:T(4,128)S(1)} %add_add_fusion, f32[48,8,1,128]{3,2,1,0:T(1,128)S(1)} %collective-permute-done.26, f32[48,8,1,128]{3,2,1,0:T(1,128)S(1)} %collective-permute-done.27, f32[8,4,128]{2,1,0:T(4,128)S(1)} %get-tuple-element.6, f32[8,4,128]{2,1,0:T(4,128)S(1)} %get-tuple-element.39, ...), kind=kLoop, calls=%fused_computation.77 | loop fusion | flops 4915200 | bytes 2818048 | tf_op jit(solution)/shard_map/mul | solution.py:76
  179.4 0.9 fusion
  180.3 10.1 %psum.15 = f32[8,4,128]{2,1,0:T(4,128)S(1)} all-reduce(f32[8,4,128]{2,1,0:T(4,128)S(1)} %bitcast.26), channel_id=1, replica_groups=mesh['members'=2,'tile'=4,'group'=4] {'group'}, use_global_device_ids=true, to_apply=%region_1.2 | all-reduce | flops 4096 | bytes 32768 | tf_op jit(solution)/shard_map/psum | solution.py:78
  190.5 0.6 multiply_add_fusion
  (38 shorter events, 4.6 us)
Async XLA Ops:
  1.4 11.4 %collective-permute-start.2 = (f32[8,1,128]{2,1,0:T(1,128)S(1)}, f32[8,1,128]{2,1,0:T(1,128)S(1)}, u32[]{:S(2)}, u32[]{:S(2)}) collective-permute-start(f32[8,1,128]{2,1,0:T(1,128)S(1)} %get-tuple-element.47), channel_id=1, source_target_pairs={{4,0},{8,4},{12,8},{0,12},{5,1},{9,5},{13,9},{1,13},{6,2},{10,6},{... | collective-permute-start | bytes 12296 | tf_op jit(solution)/shard_map/ppermute | solution.py:24
  6.5 6.3 %collective-permute-start.3 = (f32[8,1,128]{2,1,0:T(1,128)S(1)}, f32[8,1,128]{2,1,0:T(1,128)S(1)}, u32[]{:S(2)}, u32[]{:S(2)}) collective-permute-start(f32[8,1,128]{2,1,0:T(1,128)S(1)} %get-tuple-element.48), channel_id=1, source_target_pairs={{0,4},{4,8},{8,12},{12,0},{1,5},{5,9},{9,13},{13,1},{2,6},{6,10},{... | collective-permute-start | bytes 12296 | tf_op jit(solution)/shard_map/ppermute | solution.py:23
  8.5 4.3 %copy-start.2 = (f32[8,4,128]{2,1,0:T(4,128)S(1)}, f32[8,4,128]{2,1,0:T(4,128)}, u32[]{:S(2)}) copy-start(f32[8,4,128]{2,1,0:T(4,128)} %param.5) | copy-start | bytes 49156
  8.9 9.7 %collective-permute-start.1 = (f32[48,8,1,128]{3,2,1,0:T(1,128)S(1)}, f32[48,8,1,128]{3,2,1,0:T(1,128)S(1)}, u32[]{:S(2)}, u32[]{:S(2)}) collective-permute-start(f32[48,8,1,128]{3,2,1,0:T(1,128)S(1)} %get-tuple-element.36), channel_id=1, source_target_pairs={{0,4},{4,8},{8,12},{12,0},{1,5},{5,9},{9,13},{13,1},{2,6},{6,10},{... | collective-permute-start | bytes 589832 | tf_op jit(solution)/shard_map/ppermute | solution.py:23
  8.9 10.7 %collective-permute-start = (f32[48,8,1,128]{3,2,1,0:T(1,128)S(1)}, f32[48,8,1,128]{3,2,1,0:T(1,128)S(1)}, u32[]{:S(2)}, u32[]{:S(2)}) collective-permute-start(f32[48,8,1,128]{3,2,1,0:T(1,128)S(1)} %get-tuple-element.37), channel_id=1, source_target_pairs={{4,0},{8,4},{12,8},{0,12},{5,1},{9,5},{13,9},{1,13},{6,2},{10,6},{... | collective-permute-start | bytes 589832 | tf_op jit(solution)/shard_map/ppermute | solution.py:24
  21.6 12.2 %copy-start.1 = (f32[1,48,8,4,128]{4,3,2,1,0:T(4,128)S(1)}, f32[1,48,8,4,128]{4,3,2,1,0:T(4,128)}, u32[]{:S(2)}) copy-start(f32[1,48,8,4,128]{4,3,2,1,0:T(4,128)} %param.6) | copy-start | bytes 2359300
  22.0 9.3 %collective-permute-start.4 = (f32[48,8,1,128]{3,2,1,0:T(1,128)S(1)}, f32[48,8,1,128]{3,2,1,0:T(1,128)S(1)}, u32[]{:S(2)}, u32[]{:S(2)}) collective-permute-start(f32[48,8,1,128]{3,2,1,0:T(1,128)S(1)} %get-tuple-element.34), channel_id=1, source_target_pairs={{4,0},{8,4},{12,8},{0,12},{5,1},{9,5},{13,9},{1,13},{6,2},{10,6},{... | collective-permute-start | bytes 589832 | tf_op jit(solution)/shard_map/ppermute | solution.py:24
  25.5 8.4 %collective-permute-start.5 = (f32[48,8,1,128]{3,2,1,0:T(1,128)S(1)}, f32[48,8,1,128]{3,2,1,0:T(1,128)S(1)}, u32[]{:S(2)}, u32[]{:S(2)}) collective-permute-start(f32[48,8,1,128]{3,2,1,0:T(1,128)S(1)} %get-tuple-element.35), channel_id=1, source_target_pairs={{0,4},{4,8},{8,12},{12,0},{1,5},{5,9},{9,13},{13,1},{2,6},{6,10},{... | collective-permute-start | bytes 589832 | tf_op jit(solution)/shard_map/ppermute | solution.py:23
  36.5 9.6 %collective-permute-start.7 = (f32[48,8,1,128]{3,2,1,0:T(1,128)S(1)}, f32[48,8,1,128]{3,2,1,0:T(1,128)S(1)}, u32[]{:S(2)}, u32[]{:S(2)}) collective-permute-start(f32[48,8,1,128]{3,2,1,0:T(1,128)S(1)} %get-tuple-element.32), channel_id=1, source_target_pairs={{0,4},{4,8},{8,12},{12,0},{1,5},{5,9},{9,13},{13,1},{2,6},{6,10},{... | collective-permute-start | bytes 589832 | tf_op jit(solution)/shard_map/ppermute | solution.py:23
  38.0 9.1 %collective-permute-start.6 = (f32[48,8,1,128]{3,2,1,0:T(1,128)S(1)}, f32[48,8,1,128]{3,2,1,0:T(1,128)S(1)}, u32[]{:S(2)}, u32[]{:S(2)}) collective-permute-start(f32[48,8,1,128]{3,2,1,0:T(1,128)S(1)} %get-tuple-element.33), channel_id=1, source_target_pairs={{4,0},{8,4},{12,8},{0,12},{5,1},{9,5},{13,9},{1,13},{6,2},{10,6},{... | collective-permute-start | bytes 589832 | tf_op jit(solution)/shard_map/ppermute | solution.py:24
  49.5 8.6 %collective-permute-start.8 = (f32[48,8,1,128]{3,2,1,0:T(1,128)S(1)}, f32[48,8,1,128]{3,2,1,0:T(1,128)S(1)}, u32[]{:S(2)}, u32[]{:S(2)}) collective-permute-start(f32[48,8,1,128]{3,2,1,0:T(1,128)S(1)} %get-tuple-element.30), channel_id=1, source_target_pairs={{4,0},{8,4},{12,8},{0,12},{5,1},{9,5},{13,9},{1,13},{6,2},{10,6},{... | collective-permute-start | bytes 589832 | tf_op jit(solution)/shard_map/ppermute | solution.py:24
  52.3 8.4 %collective-permute-start.9 = (f32[48,8,1,128]{3,2,1,0:T(1,128)S(1)}, f32[48,8,1,128]{3,2,1,0:T(1,128)S(1)}, u32[]{:S(2)}, u32[]{:S(2)}) collective-permute-start(f32[48,8,1,128]{3,2,1,0:T(1,128)S(1)} %get-tuple-element.31), channel_id=1, source_target_pairs={{0,4},{4,8},{8,12},{12,0},{1,5},{5,9},{9,13},{13,1},{2,6},{6,10},{... | collective-permute-start | bytes 589832 | tf_op jit(solution)/shard_map/ppermute | solution.py:23
  63.1 9.2 %collective-permute-start.11 = (f32[48,8,1,128]{3,2,1,0:T(1,128)S(1)}, f32[48,8,1,128]{3,2,1,0:T(1,128)S(1)}, u32[]{:S(2)}, u32[]{:S(2)}) collective-permute-start(f32[48,8,1,128]{3,2,1,0:T(1,128)S(1)} %get-tuple-element.28), channel_id=1, source_target_pairs={{0,4},{4,8},{8,12},{12,0},{1,5},{5,9},{9,13},{13,1},{2,6},{6,10},{... | collective-permute-start | bytes 589832 | tf_op jit(solution)/shard_map/ppermute | solution.py:23
  64.7 8.2 %collective-permute-start.10 = (f32[48,8,1,128]{3,2,1,0:T(1,128)S(1)}, f32[48,8,1,128]{3,2,1,0:T(1,128)S(1)}, u32[]{:S(2)}, u32[]{:S(2)}) collective-permute-start(f32[48,8,1,128]{3,2,1,0:T(1,128)S(1)} %get-tuple-element.29), channel_id=1, source_target_pairs={{4,0},{8,4},{12,8},{0,12},{5,1},{9,5},{13,9},{1,13},{6,2},{10,6},{... | collective-permute-start | bytes 589832 | tf_op jit(solution)/shard_map/ppermute | solution.py:24
  75.2 9.0 %collective-permute-start.12 = (f32[48,8,1,128]{3,2,1,0:T(1,128)S(1)}, f32[48,8,1,128]{3,2,1,0:T(1,128)S(1)}, u32[]{:S(2)}, u32[]{:S(2)}) collective-permute-start(f32[48,8,1,128]{3,2,1,0:T(1,128)S(1)} %get-tuple-element.26), channel_id=1, source_target_pairs={{4,0},{8,4},{12,8},{0,12},{5,1},{9,5},{13,9},{1,13},{6,2},{10,6},{... | collective-permute-start | bytes 589832 | tf_op jit(solution)/shard_map/ppermute | solution.py:24
  78.4 8.4 %collective-permute-start.13 = (f32[48,8,1,128]{3,2,1,0:T(1,128)S(1)}, f32[48,8,1,128]{3,2,1,0:T(1,128)S(1)}, u32[]{:S(2)}, u32[]{:S(2)}) collective-permute-start(f32[48,8,1,128]{3,2,1,0:T(1,128)S(1)} %get-tuple-element.27), channel_id=1, source_target_pairs={{0,4},{4,8},{8,12},{12,0},{1,5},{5,9},{9,13},{13,1},{2,6},{6,10},{... | collective-permute-start | bytes 589832 | tf_op jit(solution)/shard_map/ppermute | solution.py:23
  89.0 0.7 copy-start.3
  89.0 0.7 copy-start.4
  100.7 12.8 %collective-permute-start.15 = (f32[48,8,1,128]{3,2,1,0:T(1,128)S(1)}, f32[48,8,1,128]{3,2,1,0:T(1,128)S(1)}, u32[]{:S(2)}, u32[]{:S(2)}) collective-permute-start(f32[48,8,1,128]{3,2,1,0:T(1,128)S(1)} %get-tuple-element.24), channel_id=1, source_target_pairs={{0,4},{4,8},{8,12},{12,0},{1,5},{5,9},{9,13},{13,1},{2,6},{6,10},{... | collective-permute-start | bytes 589832 | tf_op jit(solution)/shard_map/ppermute | solution.py:23
  102.4 11.1 %collective-permute-start.14 = (f32[48,8,1,128]{3,2,1,0:T(1,128)S(1)}, f32[48,8,1,128]{3,2,1,0:T(1,128)S(1)}, u32[]{:S(2)}, u32[]{:S(2)}) collective-permute-start(f32[48,8,1,128]{3,2,1,0:T(1,128)S(1)} %get-tuple-element.25), channel_id=1, source_target_pairs={{4,0},{8,4},{12,8},{0,12},{5,1},{9,5},{13,9},{1,13},{6,2},{10,6},{... | collective-permute-start | bytes 589832 | tf_op jit(solution)/shard_map/ppermute | solution.py:24
  104.8 8.0 %collective-permute-start.16 = (f32[8,1,128]{2,1,0:T(1,128)S(1)}, f32[8,1,128]{2,1,0:T(1,128)S(1)}, u32[]{:S(2)}, u32[]{:S(2)}) collective-permute-start(f32[8,1,128]{2,1,0:T(1,128)S(1)} %get-tuple-element.41), channel_id=1, source_target_pairs={{4,0},{8,4},{12,8},{0,12},{5,1},{9,5},{13,9},{1,13},{6,2},{10,6},{... | collective-permute-start | bytes 12296 | tf_op jit(solution)/shard_map/ppermute | solution.py:24
  105.0 8.4 %collective-permute-start.17 = (f32[8,1,128]{2,1,0:T(1,128)S(1)}, f32[8,1,128]{2,1,0:T(1,128)S(1)}, u32[]{:S(2)}, u32[]{:S(2)}) collective-permute-start(f32[8,1,128]{2,1,0:T(1,128)S(1)} %get-tuple-element.42), channel_id=1, source_target_pairs={{0,4},{4,8},{8,12},{12,0},{1,5},{5,9},{9,13},{13,1},{2,6},{6,10},{... | collective-permute-start | bytes 12296 | tf_op jit(solution)/shard_map/ppermute | solution.py:23
  115.9 7.8 %collective-permute-start.18 = (f32[48,8,1,128]{3,2,1,0:T(1,128)S(1)}, f32[48,8,1,128]{3,2,1,0:T(1,128)S(1)}, u32[]{:S(2)}, u32[]{:S(2)}) collective-permute-start(f32[48,8,1,128]{3,2,1,0:T(1,128)S(1)} %get-tuple-element.22), channel_id=1, source_target_pairs={{4,0},{8,4},{12,8},{0,12},{5,1},{9,5},{13,9},{1,13},{6,2},{10,6},{... | collective-permute-start | bytes 589832 | tf_op jit(solution)/shard_map/ppermute | solution.py:24
  117.3 8.5 %collective-permute-start.19 = (f32[48,8,1,128]{3,2,1,0:T(1,128)S(1)}, f32[48,8,1,128]{3,2,1,0:T(1,128)S(1)}, u32[]{:S(2)}, u32[]{:S(2)}) collective-permute-start(f32[48,8,1,128]{3,2,1,0:T(1,128)S(1)} %get-tuple-element.23), channel_id=1, source_target_pairs={{0,4},{4,8},{8,12},{12,0},{1,5},{5,9},{9,13},{13,1},{2,6},{6,10},{... | collective-permute-start | bytes 589832 | tf_op jit(solution)/shard_map/ppermute | solution.py:23
  128.3 9.3 %collective-permute-start.21 = (f32[48,8,1,128]{3,2,1,0:T(1,128)S(1)}, f32[48,8,1,128]{3,2,1,0:T(1,128)S(1)}, u32[]{:S(2)}, u32[]{:S(2)}) collective-permute-start(f32[48,8,1,128]{3,2,1,0:T(1,128)S(1)} %get-tuple-element.20), channel_id=1, source_target_pairs={{0,4},{4,8},{8,12},{12,0},{1,5},{5,9},{9,13},{13,1},{2,6},{6,10},{... | collective-permute-start | bytes 589832 | tf_op jit(solution)/shard_map/ppermute | solution.py:23
  129.4 9.0 %collective-permute-start.20 = (f32[48,8,1,128]{3,2,1,0:T(1,128)S(1)}, f32[48,8,1,128]{3,2,1,0:T(1,128)S(1)}, u32[]{:S(2)}, u32[]{:S(2)}) collective-permute-start(f32[48,8,1,128]{3,2,1,0:T(1,128)S(1)} %get-tuple-element.21), channel_id=1, source_target_pairs={{4,0},{8,4},{12,8},{0,12},{5,1},{9,5},{13,9},{1,13},{6,2},{10,6},{... | collective-permute-start | bytes 589832 | tf_op jit(solution)/shard_map/ppermute | solution.py:24
  140.8 8.7 %collective-permute-start.22 = (f32[48,8,1,128]{3,2,1,0:T(1,128)S(1)}, f32[48,8,1,128]{3,2,1,0:T(1,128)S(1)}, u32[]{:S(2)}, u32[]{:S(2)}) collective-permute-start(f32[48,8,1,128]{3,2,1,0:T(1,128)S(1)} %get-tuple-element.18), channel_id=1, source_target_pairs={{4,0},{8,4},{12,8},{0,12},{5,1},{9,5},{13,9},{1,13},{6,2},{10,6},{... | collective-permute-start | bytes 589832 | tf_op jit(solution)/shard_map/ppermute | solution.py:24
  143.4 8.7 %collective-permute-start.23 = (f32[48,8,1,128]{3,2,1,0:T(1,128)S(1)}, f32[48,8,1,128]{3,2,1,0:T(1,128)S(1)}, u32[]{:S(2)}, u32[]{:S(2)}) collective-permute-start(f32[48,8,1,128]{3,2,1,0:T(1,128)S(1)} %get-tuple-element.19), channel_id=1, source_target_pairs={{0,4},{4,8},{8,12},{12,0},{1,5},{5,9},{9,13},{13,1},{2,6},{6,10},{... | collective-permute-start | bytes 589832 | tf_op jit(solution)/shard_map/ppermute | solution.py:23
  154.6 9.1 %collective-permute-start.25 = (f32[48,8,1,128]{3,2,1,0:T(1,128)S(1)}, f32[48,8,1,128]{3,2,1,0:T(1,128)S(1)}, u32[]{:S(2)}, u32[]{:S(2)}) collective-permute-start(f32[48,8,1,128]{3,2,1,0:T(1,128)S(1)} %get-tuple-element.16), channel_id=1, source_target_pairs={{0,4},{4,8},{8,12},{12,0},{1,5},{5,9},{9,13},{13,1},{2,6},{6,10},{... | collective-permute-start | bytes 589832 | tf_op jit(solution)/shard_map/ppermute | solution.py:23
  156.1 8.0 %collective-permute-start.24 = (f32[48,8,1,128]{3,2,1,0:T(1,128)S(1)}, f32[48,8,1,128]{3,2,1,0:T(1,128)S(1)}, u32[]{:S(2)}, u32[]{:S(2)}) collective-permute-start(f32[48,8,1,128]{3,2,1,0:T(1,128)S(1)} %get-tuple-element.17), channel_id=1, source_target_pairs={{4,0},{8,4},{12,8},{0,12},{5,1},{9,5},{13,9},{1,13},{6,2},{10,6},{... | collective-permute-start | bytes 589832 | tf_op jit(solution)/shard_map/ppermute | solution.py:24
  166.5 7.7 %collective-permute-start.27 = (f32[48,8,1,128]{3,2,1,0:T(1,128)S(1)}, f32[48,8,1,128]{3,2,1,0:T(1,128)S(1)}, u32[]{:S(2)}, u32[]{:S(2)}) collective-permute-start(f32[48,8,1,128]{3,2,1,0:T(1,128)S(1)} %get-tuple-element.14), channel_id=1, source_target_pairs={{0,4},{4,8},{8,12},{12,0},{1,5},{5,9},{9,13},{13,1},{2,6},{6,10},{... | collective-permute-start | bytes 589832 | tf_op jit(solution)/shard_map/ppermute | solution.py:23
  168.6 8.6 %collective-permute-start.26 = (f32[48,8,1,128]{3,2,1,0:T(1,128)S(1)}, f32[48,8,1,128]{3,2,1,0:T(1,128)S(1)}, u32[]{:S(2)}, u32[]{:S(2)}) collective-permute-start(f32[48,8,1,128]{3,2,1,0:T(1,128)S(1)} %get-tuple-element.15), channel_id=1, source_target_pairs={{4,0},{8,4},{12,8},{0,12},{5,1},{9,5},{13,9},{1,13},{6,2},{10,6},{... | collective-permute-start | bytes 589832 | tf_op jit(solution)/shard_map/ppermute | solution.py:24
  179.4 11.7 %copy-start = (f32[48,8,4,128]{3,2,1,0:T(4,128)}, f32[48,8,4,128]{3,2,1,0:T(4,128)S(1)}, u32[]{:S(2)}) copy-start(f32[48,8,4,128]{3,2,1,0:T(4,128)S(1)} %add_multiply_fusion) | copy-start | bytes 2359300
where the time goes:
time: 191 us
  waiting for transfers between devices  86.3 us (45%)
  starting transfers between devices  48.7 us (25%)
  other arithmetic  27.5 us (14%)
  blocking collectives  20.2 us (11%)
  local copies, waits for them, and re-layouts  4.84 us (3%)
    ppermute x14, waiting for transfers between devices, with_halo(): before = lax.ppermute(last, axis, up)  44.3 us
    ppermute x14, waiting for transfers between devices, with_halo(): after = lax.ppermute(leading, axis, down)  42 us
    ppermute x14, starting transfers between devices, with_halo(): after = lax.ppermute(leading, axis, down)  36.7 us
    psum x2, blocking collectives, per_device(): heating = lax.psum(partial_value, 'group')  20.2 us
    mul x6, other arithmetic, per_device(): state = 0.5 * (state + first + tendency(tracer_edges(first), stacked))  13.2 us
    add x6, other arithmetic, per_device(): first = state + tendency(tracer_edges(state), stacked)  12.1 us
    ppermute x14, starting transfers between devices, with_halo(): before = lax.ppermute(last, axis, up)  12.1 us
  transfers between devices with their start and end apart: 28, of which 24 were waited for; matrix products, arithmetic and copies ran while one was open for 1% of the time, Pallas kernels for 0%

commit v1 on v0

v1 whole, which is shorter than its diff:
```python
import functools
import jax
import jax.numpy as jnp
from jax import lax
from jax.experimental import pallas as pl
from jax.experimental.pallas import tpu as pltpu
from jax.sharding import PartitionSpec as P

STEPS = 3
INTERVALS = 2

wind_scale = 0.3
vert_scale = 0.2
mix_base = 0.08
heat_step = 0.3

VMEM = pl.BlockSpec(memory_space=pltpu.VMEM)
SMEM = pl.BlockSpec(memory_space=pltpu.SMEM)
HBM = pl.BlockSpec(memory_space=pl.ANY)


def params():
    return pltpu.CompilerParams(vmem_limit_bytes=48 * 1024 * 1024)


def prepare(tiles, share, slots, me_ref, counts_ref, flags_ref, kappa_ref, theta_ref, tracers_ref, *outs):
    me = me_ref[0]
    count = counts_ref[0, 0]
    total = jnp.zeros(theta_ref.shape, jnp.float32)
    for step in range(tiles):
        block = lax.rem(me + step, tiles) * share
        for i in range(share):
            slot = block + i
            safe = jnp.minimum(slot, slots - 1)
            alive = slot < count
            field = tracers_ref[safe] * jnp.where(alive, 1.0, 0.0)
            weight = jnp.where(alive, flags_ref[0, safe].astype(jnp.float32) * kappa_ref[0, safe], 0.0)
            total = total + weight * field
            outs[step][i] = field
    for step in range(tiles):
        outs[step][share] = theta_ref[...]
        outs[step][share + 1] = total


def coefficients(theta_ref, coef_ref, length):
    shape = theta_ref.shape[1:]
    level = lax.broadcasted_iota(jnp.int32, shape, 0)
    place = lax.broadcasted_iota(jnp.int32, shape, 1)
    nz, ny = shape
    first_y, last_y = place > 0, place < ny - 1
    first_z, last_z = level > 0, level < nz - 1

    def body(x, carry):
        east = jnp.where(x == length - 1, 0, x + 1)
        west = jnp.where(x == 0, length - 1, x - 1)
        theta = theta_ref[x]
        grad_x = (theta_ref[east] - theta_ref[west]) * 0.5
        grad_y = (jnp.where(last_y, pltpu.roll(theta, ny - 1, 1), 0.0) - jnp.where(first_y, pltpu.roll(theta, 1, 1), 0.0)) * 0.5
        grad_z = (jnp.where(last_z, pltpu.roll(theta, nz - 1, 0), 0.0) - jnp.where(first_z, pltpu.roll(theta, 1, 0), 0.0)) * 0.5
        half_x = (-0.5 * wind_scale) * grad_y
        half_y = (0.5 * wind_scale) * grad_x
        half_z = (0.5 * vert_scale) * grad_z
        mixing = mix_base * (1.0 + 0.5 * jnp.tanh(theta))
        coef_ref[x, 0] = 1.0 - 6.0 * mixing
        coef_ref[x, 1] = mixing - half_x
        coef_ref[x, 2] = mixing + half_x
        coef_ref[x, 3] = jnp.where(last_y, mixing - half_y, 0.0)
        coef_ref[x, 4] = jnp.where(first_y, mixing + half_y, 0.0)
        coef_ref[x, 5] = jnp.where(last_z, mixing - half_z, 0.0)
        coef_ref[x, 6] = jnp.where(first_z, mixing + half_z, 0.0)
        return carry

    lax.fori_loop(0, length, body, 0, unroll=2)


def advance(coef_ref, state_ref, first_ref, length, count):
    nz, ny = state_ref.shape[-2:]

    def apply(source, x, east, west, i, coef):
        field = source[x, i]
        value = coef[0] * field + coef[1] * source[east, i] + coef[2] * source[west, i]
        value += coef[3] * pltpu.roll(field, ny - 1, 1) + coef[4] * pltpu.roll(field, 1, 1)
        value += coef[5] * pltpu.roll(field, nz - 1, 0) + coef[6] * pltpu.roll(field, 1, 0)
        return value

    def sweep(source, body_of):
        def body(x, carry):
            east = jnp.where(x == length - 1, 0, x + 1)
            west = jnp.where(x == 0, length - 1, x - 1)
            coef = [coef_ref[x, k] for k in range(7)]
            for i in range(count):
                body_of(x, i, apply(source, x, east, west, i, coef))
            return carry

        lax.fori_loop(0, length, body, 0, unroll=2)

    def put_first(x, i, value):
        first_ref[x, i] = value

    def put_state(x, i, value):
        state_ref[x, i] = state_ref[x, i] + value

    def step(_, carry):
        sweep(state_ref, put_first)
        sweep(first_ref, put_state)
        return carry

    lax.fori_loop(0, STEPS, step, 0)


def unpack(piece_ref, index, rows, nz, row):
    return piece_ref[index, pl.ds(row, nz, stride=rows), :]


def early(tiles, share, rows, nz, *refs):
    pieces, state_ref, coef_ref, theta_ref, first_ref = refs[:tiles], *refs[tiles:]
    length = tiles * rows
    for step in range(tiles):
        for row in range(rows):
            theta_ref[step * rows + row] = unpack(pieces[step], share, rows, nz, row)
            for i in range(share):
                state_ref[step * rows + row, i] = unpack(pieces[step], i, rows, nz, row)
    coefficients(theta_ref, coef_ref, length)
    advance(coef_ref, state_ref, first_ref, length, share)


def late(tiles, share, rows, nz, *refs):
    theta_in, total_in, held_ref = refs[:3]
    outs, theta_out = refs[3:3 + tiles], refs[3 + tiles]
    coef_ref, theta_ref, state_ref, first_ref, total_ref, next_ref = refs[4 + tiles:]
    length = tiles * rows
    scale = 0.5 ** STEPS
    for step in range(tiles):
        for row in range(rows):
            theta_ref[step * rows + row] = unpack(theta_in, step, rows, nz, row)
            total_ref[step * rows + row, 0] = unpack(total_in, step, rows, nz, row)
    coefficients(theta_ref, coef_ref, length)
    advance(coef_ref, total_ref, next_ref, length, 1)

    def heat(factor):
        def body(x, carry):
            theta_ref[x] = theta_ref[x] + (heat_step * factor) * total_ref[x, 0]
            return carry

        lax.fori_loop(0, length, body, 0, unroll=4)

    heat(scale)

    def copy(x, carry):
        for i in range(share):
            state_ref[x, i] = held_ref[x, i]
        state_ref[x, share] = total_ref[x, 0]
        return carry

    lax.fori_loop(0, length, copy, 0, unroll=2)
    coefficients(theta_ref, coef_ref, length)
    advance(coef_ref, state_ref, first_ref, length, share + 1)
    for step in range(tiles):
        for row in range(rows):
            x = step * rows + row
            for i in range(share):
                outs[step][i, pl.ds(row, nz, stride=rows), :] = state_ref[x, i] * (scale * scale)
            theta_out[step, pl.ds(row, nz, stride=rows), :] = theta_ref[x] + (heat_step * scale * scale) * state_ref[x, share]


def assemble(tiles, share, slots, me_ref, *refs):
    pieces, out_ref, sem = refs[:tiles], refs[tiles], refs[tiles + 1]
    me = me_ref[0]
    copies = []
    for step in range(tiles):
        block = lax.rem(me + tiles - step, tiles) * share
        copies.append(pltpu.make_async_copy(pieces[step], out_ref.at[pl.ds(block, share)], sem.at[step]))
        copies[-1].start()
    for copy in copies:
        copy.wait()


def butterfly(value, axis):
    size = lax.axis_size(axis)
    hop = 1
    while hop < size:
        value = value + lax.ppermute(value, axis, [(i, i ^ hop) for i in range(size)])
        hop *= 2
    return value


def per_device(theta, tracers, counts, flags, kappa):
    _, slots, nz, rows, ny = tracers.shape
    tiles = lax.axis_size("tile")
    share = -(-slots // tiles)
    length = tiles * rows
    me = lax.axis_index("tile").astype(jnp.int32).reshape(1)
    flat = (nz * rows, ny)
    f32 = jnp.float32
    field = lambda *lead: jax.ShapeDtypeStruct(lead, f32)

    def shift(value, step):
        return lax.ppermute(value, "tile", [(i, (i + step) % tiles) for i in range(tiles)])

    payload = pl.pallas_call(
        functools.partial(prepare, tiles, share, slots),
        out_shape=[field(share + 2, *flat)] * tiles,
        in_specs=[SMEM, SMEM, SMEM, SMEM, VMEM, VMEM],
        out_specs=[VMEM] * tiles,
        compiler_params=params(),
        name="prepare",
    )(me, counts, flags, kappa, theta.reshape(flat), tracers[0].reshape(slots, *flat))
    pieces = [payload[0]] + [shift(payload[tiles - step], tiles - step) for step in range(1, tiles)]
    total = butterfly(jnp.stack([piece[share + 1] for piece in pieces]), "group")
    grid_theta = jnp.stack([piece[share] for piece in pieces])

    held = pl.pallas_call(
        functools.partial(early, tiles, share, rows, nz),
        out_shape=field(length, share, nz, ny),
        in_specs=[VMEM] * tiles,
        out_specs=VMEM,
        scratch_shapes=[
            pltpu.VMEM((length, 7, nz, ny), f32),
            pltpu.VMEM((length, nz, ny), f32),
            pltpu.VMEM((length, share, nz, ny), f32),
        ],
        compiler_params=params(),
        name="early",
    )(*pieces)
    results = pl.pallas_call(
        functools.partial(late, tiles, share, rows, nz),
        out_shape=[field(share, *flat)] * tiles + [field(tiles, *flat)],
        in_specs=[VMEM] * 3,
        out_specs=[VMEM] * (tiles + 1),
        scratch_shapes=[
            pltpu.VMEM((length, 7, nz, ny), f32),
            pltpu.VMEM((length, nz, ny), f32),
            pltpu.VMEM((length, share + 1, nz, ny), f32),
            pltpu.VMEM((length, share + 1, nz, ny), f32),
            pltpu.VMEM((length, 1, nz, ny), f32),
            pltpu.VMEM((length, 1, nz, ny), f32),
        ],
        compiler_params=params(),
        name="late",
    )(grid_theta, total, held)
    back = [results[0]] + [shift(results[step], step) for step in range(1, tiles)]
    out = pl.pallas_call(
        functools.partial(assemble, tiles, share, slots),
        out_shape=field(tiles * share, *flat),
        in_specs=[SMEM] + [VMEM] * tiles,
        out_specs=HBM,
        scratch_shapes=[pltpu.SemaphoreType.DMA((tiles,))],
        compiler_params=params(),
        name="assemble",
    )(me, *back)
    theta_new = results[tiles][0].reshape(nz, rows, ny)
    return theta_new, out[:slots].reshape(1, slots, nz, rows, ny)


def solution(mesh):
    return jax.shard_map(
        per_device,
        mesh=mesh,
        in_specs=(
            P("members", "tile", None),
            P("group", "members", None, "tile", None),
            P("group", "members"),
            P("group", "members"),
            P("group", None),
        ),
        out_specs=(P("members", "tile", None), P("group", "members", None, "tile", None)),
        check_vma=False,
    )
```

time: 191 us -> 71 us (0.37)
  the two profiles are of different devices: /device:TPU:0 before, /device:TPU:8 now
where the time goes in v1:
time: 71 us; the launch traced here: 70.8 us
  waiting for transfers between devices  35.6 us (50%)
  Pallas kernels  19.3 us (27%)
  starting transfers between devices  11.3 us (16%)
  local copies, waits for them, and re-layouts  3.12 us (4%)
  between operations  1.37 us (2%)
    ppermute x6, waiting for transfers between devices, shift(): lax.ppermute(value, 'tile', [(i, (i + step) % tiles) for i in range(tiles)])  32.6 us
    pallas_call x1, Pallas kernels, per_device(): pl.pallas_call(functools.partial(late, tiles, share, rows, nz), out_shape...  11.2 us
    ppermute x6, starting transfers between devices, shift(): lax.ppermute(value, 'tile', [(i, (i + step) % tiles) for i in range(tiles)])  9.63 us
    pallas_call x1, Pallas kernels, per_device(): pl.pallas_call(functools.partial(early, tiles, share, rows, nz), out_shap...  6.51 us
    ppermute x2, waiting for transfers between devices, butterfly(): lax.ppermute(value, axis, [(i, i ^ hop) for i in range(size)])  3 us
    unnamed x8, local copies, waits for them, and re-layouts  2.51 us
    ppermute x2, starting transfers between devices, butterfly(): lax.ppermute(value, axis, [(i, i ^ hop) for i in range(size)])  1.63 us
  transfers between devices with their start and end apart: 8, of which 6 were waited for; matrix products, arithmetic and copies ran while one was open for 1% of the time, Pallas kernels for 9%

profile of v1, /device:TPU:8, one launch (start us, length us, event | category | flops | bytes accessed | tf_op | source)
XLA Modules:
  0.0 70.8 jit_solution(2991067285692398130)
XLA Ops:
  1.3 0.0 copy-start.2
  1.3 0.0 copy-start.3
  1.3 0.6 copy-done.2
  1.9 0.0 copy-done.3
  2.0 0.0 copy-start
  2.0 1.1 %copy-done = f32[1,48,8,4,128]{4,3,2,1,0:T(4,128)S(1)} copy-done((f32[1,48,8,4,128]{4,3,2,1,0:T(4,128)S(1)}, f32[1,48,8,4,128]{4,3,2,1,0:T(4,128)}, u32[]{:S(2)}) %copy-start) | copy-done | bytes 786456
  3.1 0.0 copy-start.1
  3.1 0.7 %copy-done.1 = f32[8,4,128]{2,1,0:T(4,128)S(1)} copy-done((f32[8,4,128]{2,1,0:T(4,128)S(1)}, f32[8,4,128]{2,1,0:T(4,128)}, u32[]{:S(2)}) %copy-start.1) | copy-done | bytes 16408
  3.8 0.7 prepare.1
  4.5 0.1 collective-permute-start
  4.6 3.0 %collective-permute-start.1 = (f32[14,32,128]{2,1,0:T(8,128)S(1)}, f32[14,32,128]{2,1,0:T(8,128)S(1)}, u32[]{:S(2)}, u32[]{:S(2)}) collective-permute-start(f32[14,32,128]{2,1,0:T(8,128)S(1)} %get-tuple-element.13), channel_id=1, source_target_pairs={{0,8},{4,12},{8,0},{12,4},{1,9},{5,13},{9,1},{13,5},{2,10},{6,14},... | collective-permute-start | bytes 688136 | tf_op jit(solution)/shard_map/ppermute | solution.py:198
  7.6 2.5 %collective-permute-start.2 = (f32[14,32,128]{2,1,0:T(8,128)S(1)}, f32[14,32,128]{2,1,0:T(8,128)S(1)}, u32[]{:S(2)}, u32[]{:S(2)}) collective-permute-start(f32[14,32,128]{2,1,0:T(8,128)S(1)} %get-tuple-element.14), channel_id=1, source_target_pairs={{0,4},{4,8},{8,12},{12,0},{1,5},{5,9},{9,13},{13,1},{2,6},{6,10},{... | collective-permute-start | bytes 688136 | tf_op jit(solution)/shard_map/ppermute | solution.py:198
  10.1 12.8 %collective-permute-done.refs_1_ = f32[14,32,128]{2,1,0:T(8,128)S(1)} collective-permute-done((f32[14,32,128]{2,1,0:T(8,128)S(1)}, f32[14,32,128]{2,1,0:T(8,128)S(1)}, u32[]{:S(2)}, u32[]{:S(2)}) %collective-permute-start) | collective-permute-done | bytes 229408 | tf_op jit(solution)/shard_map/ppermute | solution.py:198
  22.9 0.0 collective-permute-done.1.refs_2_
  22.9 4.0 %collective-permute-done.2.refs_3_ = f32[14,32,128]{2,1,0:T(8,128)S(1)} collective-permute-done((f32[14,32,128]{2,1,0:T(8,128)S(1)}, f32[14,32,128]{2,1,0:T(8,128)S(1)}, u32[]{:S(2)}, u32[]{:S(2)}) %collective-permute-start.2) | collective-permute-done | bytes 229408 | tf_op jit(solution)/shard_map/ppermute | solution.py:198
  27.0 0.1 collective-permute-start.3
  27.1 6.5 %early.1.refs_2_ = f32[16,12,8,128]{3,2,1,0:T(8,128)S(1)} custom-call(f32[14,32,128]{2,1,0:T(8,128)S(1)} %get-tuple-element.11.refs_0_, f32[14,32,128]{2,1,0:T(8,128)S(1)} %collective-permute-done.refs_1_, f32[14,32,128]{2,1,0:T(8,128)S(1)} %collective-permute-done.1.refs_2_, f32[14,32,128]{2,1,0:T(8,128)S(1)} %collective-permute-done.2.refs_3_), custom_call_target="tpu_custom_call" | custom-call | tf_op jit(solution)/shard_map/early/pallas_call | solution.py:212
  33.6 0.0 collective-permute-done.3
  33.6 1.6 %collective-permute-start.4 = (f32[4,32,128]{2,1,0:T(8,128)S(1)}, f32[4,32,128]{2,1,0:T(8,128)S(1)}, u32[]{:S(2)}, u32[]{:S(2)}) collective-permute-start(f32[4,32,128]{2,1,0:T(8,128)S(1)} %fusion), channel_id=1, source_target_pairs={{0,2},{1,3},{2,0},{3,1},{4,6},{5,7},{6,4},{7,5},{8,10},{9,11},{10,... | collective-permute-start | bytes 196616 | tf_op jit(solution)/shard_map/ppermute | solution.py:182
  35.2 3.0 %collective-permute-done.4 = f32[4,32,128]{2,1,0:T(8,128)S(1)} collective-permute-done((f32[4,32,128]{2,1,0:T(8,128)S(1)}, f32[4,32,128]{2,1,0:T(8,128)S(1)}, u32[]{:S(2)}, u32[]{:S(2)}) %collective-permute-start.4) | collective-permute-done | bytes 65568 | tf_op jit(solution)/shard_map/ppermute | solution.py:182
  38.2 11.2 %late.1 = (f32[12,32,128]{2,1,0:T(8,128)S(1)}, f32[12,32,128]{2,1,0:T(8,128)S(1)}, f32[12,32,128]{2,1,0:T(8,128)S(1)}, f32[12,32,128]{2,1,0:T(8,128)S(1)}, f32[4,32,128]{2,1,0:T(8,128)S(1)}) custom-call(f32[4,32,128]{2,1,0:T(8,128)S(1)} %pad_maximum_fusion.refs_0_, f32[4,32,128]{2,1,0:T(8,128)S(1)} %fusion.5.refs_1_, f32[16,12,8,128]{3,2,1,0:T(8,128)S(1)} %early.1.refs_2_), custom_call_target="tpu_custom_call" | custom-call | tf_op jit(solution)/shard_map/late/pallas_call | solution.py:225
  49.4 2.5 %collective-permute-start.5 = (f32[12,32,128]{2,1,0:T(8,128)S(1)}, f32[12,32,128]{2,1,0:T(8,128)S(1)}, u32[]{:S(2)}, u32[]{:S(2)}) collective-permute-start(f32[12,32,128]{2,1,0:T(8,128)S(1)} %get-tuple-element.17), channel_id=1, source_target_pairs={{0,4},{4,8},{8,12},{12,0},{1,5},{5,9},{9,13},{13,1},{2,6},{6,10},{... | collective-permute-start | bytes 589832 | tf_op jit(solution)/shard_map/ppermute | solution.py:198
  52.0 1.0 %collective-permute-start.6 = (f32[12,32,128]{2,1,0:T(8,128)S(1)}, f32[12,32,128]{2,1,0:T(8,128)S(1)}, u32[]{:S(2)}, u32[]{:S(2)}) collective-permute-start(f32[12,32,128]{2,1,0:T(8,128)S(1)} %get-tuple-element.18), channel_id=1, source_target_pairs={{0,8},{4,12},{8,0},{12,4},{1,9},{5,13},{9,1},{13,5},{2,10},{6,14},... | collective-permute-start | bytes 589832 | tf_op jit(solution)/shard_map/ppermute | solution.py:198
  53.0 0.5 collective-permute-start.7
  53.5 0.6 slice.35
  54.1 11.6 %collective-permute-done.5.refs_1_ = f32[12,32,128]{2,1,0:T(8,128)S(1)} collective-permute-done((f32[12,32,128]{2,1,0:T(8,128)S(1)}, f32[12,32,128]{2,1,0:T(8,128)S(1)}, u32[]{:S(2)}, u32[]{:S(2)}) %collective-permute-start.5) | collective-permute-done | bytes 196640 | tf_op jit(solution)/shard_map/ppermute | solution.py:198
  65.7 2.9 %collective-permute-done.6.refs_2_ = f32[12,32,128]{2,1,0:T(8,128)S(1)} collective-permute-done((f32[12,32,128]{2,1,0:T(8,128)S(1)}, f32[12,32,128]{2,1,0:T(8,128)S(1)}, u32[]{:S(2)}, u32[]{:S(2)}) %collective-permute-start.6) | collective-permute-done | bytes 196640 | tf_op jit(solution)/shard_map/ppermute | solution.py:198
  68.6 1.2 %collective-permute-done.7.refs_3_ = f32[12,32,128]{2,1,0:T(8,128)S(1)} collective-permute-done((f32[12,32,128]{2,1,0:T(8,128)S(1)}, f32[12,32,128]{2,1,0:T(8,128)S(1)}, u32[]{:S(2)}, u32[]{:S(2)}) %collective-permute-start.7) | collective-permute-done | bytes 196640 | tf_op jit(solution)/shard_map/ppermute | solution.py:198
  69.9 0.9 %assemble.1 = f32[48,32,128]{2,1,0:T(8,128)} custom-call(s32[1]{0:T(128)} %bitcast.me_ref, f32[12,32,128]{2,1,0:T(8,128)S(1)} %get-tuple-element.16.refs_0_, f32[12,32,128]{2,1,0:T(8,128)S(1)} %collective-permute-done.5.refs_1_, f32[12,32,128]{2,1,0:T(8,128)S(1)} %collective-permute-done.6.refs_2_, f32[12,32,128]{2,1,0:T(8,128)S(1)} %collective-permute-done.7.refs_3_), custom_call_target="tpu_custom_call" | custom-call | tf_op jit(solution)/shard_map/assemble/pallas_call | solution.py:242
  (8 shorter events, 0.1 us)
Async XLA Ops:
  1.3 0.7 copy-start.2
  1.3 0.7 copy-start.3
  2.0 1.1 %copy-start = (f32[1,48,8,4,128]{4,3,2,1,0:T(4,128)S(1)}, f32[1,48,8,4,128]{4,3,2,1,0:T(4,128)}, u32[]{:S(2)}) copy-start(f32[1,48,8,4,128]{4,3,2,1,0:T(4,128)} %param.6) | copy-start | bytes 2359300
  3.1 0.7 %copy-start.1 = (f32[8,4,128]{2,1,0:T(4,128)S(1)}, f32[8,4,128]{2,1,0:T(4,128)}, u32[]{:S(2)}) copy-start(f32[8,4,128]{2,1,0:T(4,128)} %param.5) | copy-start | bytes 49156
  4.5 18.4 %collective-permute-start = (f32[14,32,128]{2,1,0:T(8,128)S(1)}, f32[14,32,128]{2,1,0:T(8,128)S(1)}, u32[]{:S(2)}, u32[]{:S(2)}) collective-permute-start(f32[14,32,128]{2,1,0:T(8,128)S(1)} %get-tuple-element.12), channel_id=1, source_target_pairs={{0,12},{4,0},{8,4},{12,8},{1,13},{5,1},{9,5},{13,9},{2,14},{6,2},{... | collective-permute-start | bytes 688136 | tf_op jit(solution)/shard_map/ppermute | solution.py:198
  4.6 18.4 %collective-permute-start.1 = (f32[14,32,128]{2,1,0:T(8,128)S(1)}, f32[14,32,128]{2,1,0:T(8,128)S(1)}, u32[]{:S(2)}, u32[]{:S(2)}) collective-permute-start(f32[14,32,128]{2,1,0:T(8,128)S(1)} %get-tuple-element.13), channel_id=1, source_target_pairs={{0,8},{4,12},{8,0},{12,4},{1,9},{5,13},{9,1},{13,5},{2,10},{6,14},... | collective-permute-start | bytes 688136 | tf_op jit(solution)/shard_map/ppermute | solution.py:198
  7.6 19.4 %collective-permute-start.2 = (f32[14,32,128]{2,1,0:T(8,128)S(1)}, f32[14,32,128]{2,1,0:T(8,128)S(1)}, u32[]{:S(2)}, u32[]{:S(2)}) collective-permute-start(f32[14,32,128]{2,1,0:T(8,128)S(1)} %get-tuple-element.14), channel_id=1, source_target_pairs={{0,4},{4,8},{8,12},{12,0},{1,5},{5,9},{9,13},{13,1},{2,6},{6,10},{... | collective-permute-start | bytes 688136 | tf_op jit(solution)/shard_map/ppermute | solution.py:198
  27.0 6.6 %collective-permute-start.3 = (f32[4,32,128]{2,1,0:T(8,128)S(1)}, f32[4,32,128]{2,1,0:T(8,128)S(1)}, u32[]{:S(2)}, u32[]{:S(2)}) collective-permute-start(f32[4,32,128]{2,1,0:T(8,128)S(1)} %pad_maximum_fusion.1), channel_id=1, source_target_pairs={{0,1},{1,0},{2,3},{3,2},{4,5},{5,4},{6,7},{7,6},{8,9},{9,8},{10,11... | collective-permute-start | bytes 196616 | tf_op jit(solution)/shard_map/ppermute | solution.py:182
  33.6 4.6 %collective-permute-start.4 = (f32[4,32,128]{2,1,0:T(8,128)S(1)}, f32[4,32,128]{2,1,0:T(8,128)S(1)}, u32[]{:S(2)}, u32[]{:S(2)}) collective-permute-start(f32[4,32,128]{2,1,0:T(8,128)S(1)} %fusion), channel_id=1, source_target_pairs={{0,2},{1,3},{2,0},{3,1},{4,6},{5,7},{6,4},{7,5},{8,10},{9,11},{10,... | collective-permute-start | bytes 196616 | tf_op jit(solution)/shard_map/ppermute | solution.py:182
  49.4 16.3 %collective-permute-start.5 = (f32[12,32,128]{2,1,0:T(8,128)S(1)}, f32[12,32,128]{2,1,0:T(8,128)S(1)}, u32[]{:S(2)}, u32[]{:S(2)}) collective-permute-start(f32[12,32,128]{2,1,0:T(8,128)S(1)} %get-tuple-element.17), channel_id=1, source_target_pairs={{0,4},{4,8},{8,12},{12,0},{1,5},{5,9},{9,13},{13,1},{2,6},{6,10},{... | collective-permute-start | bytes 589832 | tf_op jit(solution)/shard_map/ppermute | solution.py:198
  52.0 16.7 %collective-permute-start.6 = (f32[12,32,128]{2,1,0:T(8,128)S(1)}, f32[12,32,128]{2,1,0:T(8,128)S(1)}, u32[]{:S(2)}, u32[]{:S(2)}) collective-permute-start(f32[12,32,128]{2,1,0:T(8,128)S(1)} %get-tuple-element.18), channel_id=1, source_target_pairs={{0,8},{4,12},{8,0},{12,4},{1,9},{5,13},{9,1},{13,5},{2,10},{6,14},... | collective-permute-start | bytes 589832 | tf_op jit(solution)/shard_map/ppermute | solution.py:198
  53.0 16.9 %collective-permute-start.7 = (f32[12,32,128]{2,1,0:T(8,128)S(1)}, f32[12,32,128]{2,1,0:T(8,128)S(1)}, u32[]{:S(2)}, u32[]{:S(2)}) collective-permute-start(f32[12,32,128]{2,1,0:T(8,128)S(1)} %get-tuple-element.19), channel_id=1, source_target_pairs={{0,12},{4,0},{8,4},{12,8},{1,13},{5,1},{9,5},{13,9},{2,14},{6,2},{... | collective-permute-start | bytes 589832 | tf_op jit(solution)/shard_map/ppermute | solution.py:198

commit v2 on v1

v2 whole, which is shorter than its diff:
```python
import functools
import jax
import jax.numpy as jnp
from jax import lax
from jax.experimental import pallas as pl
from jax.experimental.pallas import tpu as pltpu
from jax.sharding import PartitionSpec as P

STEPS = 3
INTERVALS = 2

wind_scale = 0.3
vert_scale = 0.2
mix_base = 0.08
heat_step = 0.3

UNROLL = 16
SCALE = 0.5 ** STEPS

VMEM = pl.BlockSpec(memory_space=pltpu.VMEM)
SMEM = pl.BlockSpec(memory_space=pltpu.SMEM)
HBM = pl.BlockSpec(memory_space=pltpu.HBM)


def params():
    return pltpu.CompilerParams(vmem_limit_bytes=48 * 1024 * 1024)


def cost(us):
    return pl.CostEstimate(flops=0, bytes_accessed=int(us * 1.0e3), transcendentals=0)


def prepare(tiles, parts, slots, me_ref, counts_ref, flags_hbm, kappa_hbm, theta_hbm, tracers_hbm, *refs):
    outs = refs[:tiles * len(parts)]
    flags_ref, kappa_ref, theta_ref, tracers_ref, sems = refs[tiles * len(parts):]
    copies = [
        pltpu.make_async_copy(source, target, sems.at[k])
        for k, (source, target) in enumerate(
            [(tracers_hbm, tracers_ref), (theta_hbm, theta_ref), (flags_hbm, flags_ref), (kappa_hbm, kappa_ref)]
        )
    ]
    for copy in copies:
        copy.start()
    for copy in copies:
        copy.wait()
    me = me_ref[0]
    count = counts_ref[0, 0]
    total = jnp.zeros(theta_ref.shape, jnp.float32)
    share = sum(parts)
    for step in range(tiles):
        block = lax.rem(me + step, tiles) * share
        before = 0
        for chunk, part in enumerate(parts):
            for i in range(part):
                slot = block + before + i
                safe = jnp.minimum(slot, slots - 1)
                alive = slot < count
                field = tracers_ref[safe] * jnp.where(alive, 1.0, 0.0)
                weight = jnp.where(alive, flags_ref[0, safe].astype(jnp.float32) * kappa_ref[0, safe], 0.0)
                total = total + weight * field
                outs[chunk * tiles + step][i] = field
            before += part
    for step in range(tiles):
        outs[step][parts[0]] = theta_ref[...]
        outs[step][parts[0] + 1] = total


def coefficients(theta_ref, coef_ref, length):
    shape = theta_ref.shape[1:]
    level = lax.broadcasted_iota(jnp.int32, shape, 0)
    place = lax.broadcasted_iota(jnp.int32, shape, 1)
    nz, ny = shape
    first_y, last_y = place > 0, place < ny - 1
    first_z, last_z = level > 0, level < nz - 1

    def body(x, carry):
        east = jnp.where(x == length - 1, 0, x + 1)
        west = jnp.where(x == 0, length - 1, x - 1)
        theta = theta_ref[x]
        grad_x = (theta_ref[east] - theta_ref[west]) * 0.5
        grad_y = (jnp.where(last_y, pltpu.roll(theta, ny - 1, 1), 0.0) - jnp.where(first_y, pltpu.roll(theta, 1, 1), 0.0)) * 0.5
        grad_z = (jnp.where(last_z, pltpu.roll(theta, nz - 1, 0), 0.0) - jnp.where(first_z, pltpu.roll(theta, 1, 0), 0.0)) * 0.5
        half_x = (-0.5 * wind_scale) * grad_y
        half_y = (0.5 * wind_scale) * grad_x
        half_z = (0.5 * vert_scale) * grad_z
        mixing = mix_base * (1.0 + 0.5 * jnp.tanh(theta))
        coef_ref[x, 0] = 1.0 - 6.0 * mixing
        coef_ref[x, 1] = mixing - half_x
        coef_ref[x, 2] = mixing + half_x
        coef_ref[x, 3] = jnp.where(last_y, mixing - half_y, 0.0)
        coef_ref[x, 4] = jnp.where(first_y, mixing + half_y, 0.0)
        coef_ref[x, 5] = jnp.where(last_z, mixing - half_z, 0.0)
        coef_ref[x, 6] = jnp.where(first_z, mixing + half_z, 0.0)
        return carry

    lax.fori_loop(0, length, body, 0, unroll=UNROLL)


def advance(coef_ref, state_ref, first_ref, length, count):
    nz, ny = state_ref.shape[-2:]

    def apply(source, x, east, west, i, coef):
        field = source[x, i]
        value = coef[0] * field + coef[1] * source[east, i] + coef[2] * source[west, i]
        value += coef[5] * pltpu.roll(field, nz - 1, 0) + coef[6] * pltpu.roll(field, 1, 0)
        value += coef[3] * pltpu.roll(field, ny - 1, 1) + coef[4] * pltpu.roll(field, 1, 1)
        return value

    def sweep(source, put):
        def body(x, carry):
            east = jnp.where(x == length - 1, 0, x + 1)
            west = jnp.where(x == 0, length - 1, x - 1)
            coef = [coef_ref[x, k] for k in range(7)]
            for i in range(count):
                put(x, i, apply(source, x, east, west, i, coef))
            return carry

        lax.fori_loop(0, length, body, 0, unroll=UNROLL)

    def put_first(x, i, value):
        first_ref[x, i] = value

    def put_state(x, i, value):
        state_ref[x, i] = state_ref[x, i] + value

    def step(_, carry):
        sweep(state_ref, put_first)
        sweep(first_ref, put_state)
        return carry

    lax.fori_loop(0, STEPS, step, 0)


def unpack(piece_ref, index, rows, nz, row):
    return piece_ref[index, pl.ds(row, nz, stride=rows), :]


def load(pieces, part, rows, nz, state_ref):
    for step, piece in enumerate(pieces):
        for row in range(rows):
            for i in range(part):
                state_ref[step * rows + row, i] = unpack(piece, i, rows, nz, row)


def store(outs, part, rows, nz, state_ref):
    for step, out in enumerate(outs):
        for row in range(rows):
            for i in range(part):
                out[i, pl.ds(row, nz, stride=rows), :] = state_ref[step * rows + row, i] * (SCALE * SCALE)


def early(tiles, part, rows, nz, *refs):
    pieces, (state_ref, coef_ref, theta_ref, first_ref) = refs[:tiles], refs[tiles:]
    for step in range(tiles):
        for row in range(rows):
            theta_ref[step * rows + row] = unpack(pieces[step], part, rows, nz, row)
    load(pieces, part, rows, nz, state_ref)
    coefficients(theta_ref, coef_ref, tiles * rows)
    advance(coef_ref, state_ref, first_ref, tiles * rows, part)


def dynamics(tiles, rows, nz, theta_in, total_in, coef_ref, coef_out, theta_out, state_ref, first_ref):
    length = tiles * rows
    for step in range(tiles):
        for row in range(rows):
            state_ref[step * rows + row, 0] = unpack(total_in, step, rows, nz, row)
    advance(coef_ref, state_ref, first_ref, length, 1)

    def heat(x, carry):
        theta_in[x] = theta_in[x] + (heat_step * SCALE) * state_ref[x, 0]
        return carry

    lax.fori_loop(0, length, heat, 0, unroll=UNROLL)
    coefficients(theta_in, coef_out, length)
    advance(coef_out, state_ref, first_ref, length, 1)
    for row in range(rows):
        theta_out[pl.ds(row, nz, stride=rows), :] = theta_in[row] + (heat_step * SCALE * SCALE) * state_ref[row, 0]


def dynamics_call(tiles, rows, nz, theta_pieces, total_in, coef_ref, coef_out, theta_out, state_ref, first_ref, theta_ref):
    for step in range(tiles):
        for row in range(rows):
            theta_ref[step * rows + row] = unpack(theta_pieces, step, rows, nz, row)
    dynamics(tiles, rows, nz, theta_ref, total_in, coef_ref, coef_out, theta_out, state_ref, first_ref)


def late(tiles, part, rows, nz, held_ref, coef_ref, *refs):
    outs, (state_ref, first_ref) = refs[:tiles], refs[tiles:]
    length = tiles * rows

    def copy(x, carry):
        for i in range(part):
            state_ref[x, i] = held_ref[x, i]
        return carry

    lax.fori_loop(0, length, copy, 0, unroll=UNROLL)
    advance(coef_ref, state_ref, first_ref, length, part)
    store(outs, part, rows, nz, state_ref)


def both(tiles, part, rows, nz, *refs):
    pieces, (coef_ref, next_ref) = refs[:tiles], refs[tiles:tiles + 2]
    outs, (state_ref, first_ref) = refs[tiles + 2:2 * tiles + 2], refs[2 * tiles + 2:]
    load(pieces, part, rows, nz, state_ref)
    advance(coef_ref, state_ref, first_ref, tiles * rows, part)
    advance(next_ref, state_ref, first_ref, tiles * rows, part)
    store(outs, part, rows, nz, state_ref)


def assemble(tiles, parts, me_ref, *refs):
    pieces, out_ref, sem = refs[:-2], refs[-2], refs[-1]
    me = me_ref[0]
    share = sum(parts)
    copies = []
    for step in range(tiles):
        slot = lax.rem(me + tiles - step, tiles) * share
        for chunk, part in enumerate(parts):
            copies.append(pltpu.make_async_copy(pieces[chunk * tiles + step], out_ref.at[pl.ds(slot, part)], sem.at[len(copies)]))
            copies[-1].start()
            slot = slot + part
    for copy in copies:
        copy.wait()


def butterfly(value, axis):
    size = lax.axis_size(axis)
    hop = 1
    while hop < size:
        value = value + lax.ppermute(value, axis, [(i, i ^ hop) for i in range(size)])
        hop *= 2
    return value


def per_device(theta, tracers, counts, flags, kappa):
    _, slots, nz, rows, ny = tracers.shape
    tiles = lax.axis_size("tile")
    share = max(2, -(-slots // tiles))
    parts = (share // 2, share - share // 2)
    length = tiles * rows
    me = lax.axis_index("tile").astype(jnp.int32).reshape(1)
    flat = (nz * rows, ny)
    f32 = jnp.float32
    field = lambda *lead: jax.ShapeDtypeStruct(lead, f32)
    scratch = lambda *lead: pltpu.VMEM(lead, f32)

    def shift(value, step):
        return lax.ppermute(value, "tile", [(i, (i + step) % tiles) for i in range(tiles)])

    def gather(payload):
        return [payload[0]] + [shift(payload[tiles - step], tiles - step) for step in range(1, tiles)]

    payload = pl.pallas_call(
        functools.partial(prepare, tiles, parts, slots),
        out_shape=[field(parts[0] + 2, *flat)] * tiles + [field(parts[1], *flat)] * tiles,
        in_specs=[SMEM, SMEM, HBM, HBM, HBM, HBM],
        out_specs=[VMEM] * (2 * tiles),
        scratch_shapes=[
            pltpu.SMEM(flags.shape, jnp.int32),
            pltpu.SMEM(kappa.shape, f32),
            scratch(*flat),
            scratch(slots, *flat),
            pltpu.SemaphoreType.DMA((4,)),
        ],
        compiler_params=params(),
        cost_estimate=cost(2),
        name="prepare",
    )(me, counts, flags, kappa, theta.reshape(flat), tracers[0].reshape(slots, *flat))
    one = gather(payload[:tiles])
    two = gather(payload[tiles:])
    total = butterfly(jnp.stack([piece[parts[0] + 1] for piece in one]), "group")
    grid_theta = jnp.stack([piece[parts[0]] for piece in one])

    held, coef = pl.pallas_call(
        functools.partial(early, tiles, parts[0], rows, nz),
        out_shape=[field(length, parts[0], nz, ny), field(length, 7, nz, ny)],
        in_specs=[VMEM] * tiles,
        out_specs=[VMEM] * 2,
        scratch_shapes=[scratch(length, nz, ny), scratch(length, parts[0], nz, ny)],
        compiler_params=params(),
        cost_estimate=cost(2.5),
        name="early",
    )(*one)
    next_coef, theta_new = pl.pallas_call(
        functools.partial(dynamics_call, tiles, rows, nz),
        out_shape=[field(length, 7, nz, ny), field(*flat)],
        in_specs=[VMEM] * 3,
        out_specs=[VMEM] * 2,
        scratch_shapes=[scratch(length, 1, nz, ny), scratch(length, 1, nz, ny), scratch(length, nz, ny)],
        compiler_params=params(),
        cost_estimate=cost(2.5),
        name="dynamics",
    )(grid_theta, total, coef)
    done_one = pl.pallas_call(
        functools.partial(late, tiles, parts[0], rows, nz),
        out_shape=[field(parts[0], *flat)] * tiles,
        in_specs=[VMEM] * 2,
        out_specs=[VMEM] * tiles,
        scratch_shapes=[scratch(length, parts[0], nz, ny)] * 2,
        compiler_params=params(),
        cost_estimate=cost(2),
        name="late",
    )(held, next_coef)
    done_two = pl.pallas_call(
        functools.partial(both, tiles, parts[1], rows, nz),
        out_shape=[field(parts[1], *flat)] * tiles,
        in_specs=[VMEM] * (tiles + 2),
        out_specs=[VMEM] * tiles,
        scratch_shapes=[scratch(length, parts[1], nz, ny)] * 2,
        compiler_params=params(),
        cost_estimate=cost(4),
        name="both",
    )(*two, coef, next_coef)
    back = [piece for done in (done_one, done_two) for piece in [done[0]] + [shift(done[step], step) for step in range(1, tiles)]]
    out = pl.pallas_call(
        functools.partial(assemble, tiles, parts),
        out_shape=field(tiles * share, *flat),
        in_specs=[SMEM] + [VMEM] * (2 * tiles),
        out_specs=HBM,
        scratch_shapes=[pltpu.SemaphoreType.DMA((2 * tiles,))],
        compiler_params=params(),
        cost_estimate=cost(1),
        name="assemble",
    )(me, *back)
    return theta_new.reshape(nz, rows, ny), out[:slots].reshape(1, slots, nz, rows, ny)


def solution(mesh):
    return jax.shard_map(
        per_device,
        mesh=mesh,
        in_specs=(
            P("members", "tile", None),
            P("group", "members", None, "tile", None),
            P("group", "members"),
            P("group", "members"),
            P("group", None),
        ),
        out_specs=(P("members", "tile", None), P("group", "members", None, "tile", None)),
        check_vma=False,
    )
```

time: 71 us -> 54.3 us (0.76)
  the two profiles are of different devices: /device:TPU:8 before, /device:TPU:0 now
where the time goes in v2:
time: 54.3 us; the launch traced here: 54.1 us
  starting transfers between devices  21.3 us (39%)
  waiting for transfers between devices  19.3 us (36%)
  Pallas kernels  9.51 us (18%)
  local copies, waits for them, and re-layouts  2.52 us (5%)
  between operations  1.38 us (3%)
    ppermute x12, starting transfers between devices, shift(): lax.ppermute(value, 'tile', [(i, (i + step) % tiles) for i in range(tiles)])  19.7 us
    ppermute x12, waiting for transfers between devices, shift(): lax.ppermute(value, 'tile', [(i, (i + step) % tiles) for i in range(tiles)])  16.5 us
    pallas_call x1, Pallas kernels, per_device(): pl.pallas_call(functools.partial(both, tiles, parts[1], rows, nz), out_sh...  2.9 us
    ppermute x2, waiting for transfers between devices, butterfly(): lax.ppermute(value, axis, [(i, i ^ hop) for i in range(size)])  2.77 us
    unnamed x8, local copies, waits for them, and re-layouts  2.51 us
    pallas_call x1, Pallas kernels, per_device(): pl.pallas_call(functools.partial(dynamics_call, tiles, rows, nz), out_sha...  1.84 us
    ppermute x2, starting transfers between devices, butterfly(): lax.ppermute(value, axis, [(i, i ^ hop) for i in range(size)])  1.63 us
    pallas_call x1, Pallas kernels, per_device(): pl.pallas_call(functools.partial(early, tiles, parts[0], rows, nz), out_s...  1.56 us
  transfers between devices with their start and end apart: 14, of which 5 were waited for; matrix products, arithmetic and copies ran while one was open for 0% of the time, Pallas kernels for 14%

profile of v2, /device:TPU:0, one launch (start us, length us, event | category | flops | bytes accessed | tf_op | source)
XLA Modules:
  0.0 54.1 jit_solution(9904275006159990232)
XLA Ops:
  1.3 0.0 copy-start.2
  1.3 0.0 copy-start.3
  1.3 0.6 %copy-done.2 = s32[1,48]{1,0:T(1,128)S(1)} copy-done((s32[1,48]{1,0:T(1,128)S(1)}, s32[1,48]{1,0:T(1,128)}, u32[]{:S(2)}) %copy-start.2) | copy-done | bytes 216
  1.9 0.0 copy-done.3
  2.0 0.0 copy-start
  2.0 1.1 %copy-done = f32[1,48,8,4,128]{4,3,2,1,0:T(4,128)S(1)} copy-done((f32[1,48,8,4,128]{4,3,2,1,0:T(4,128)S(1)}, f32[1,48,8,4,128]{4,3,2,1,0:T(4,128)}, u32[]{:S(2)}) %copy-start) | copy-done | bytes 786456
  3.1 0.0 copy-start.1
  3.1 0.7 %copy-done.1 = f32[8,4,128]{2,1,0:T(4,128)S(1)} copy-done((f32[8,4,128]{2,1,0:T(4,128)S(1)}, f32[8,4,128]{2,1,0:T(4,128)}, u32[]{:S(2)}) %copy-start.1) | copy-done | bytes 16408
  3.8 0.8 %prepare.1 = (f32[8,32,128]{2,1,0:T(8,128)S(1)}, f32[8,32,128]{2,1,0:T(8,128)S(1)}, f32[8,32,128]{2,1,0:T(8,128)S(1)}, f32[8,32,128]{2,1,0:T(8,128)S(1)}, f32[6,...) custom-call(s32[1]{0:T(128)} %bitcast.me_ref, ...), custom_call_target="tpu_custom_call" | custom-call | bytes 2000 | tf_op jit(solution)/shard_map/prepare/pallas_call | solution.py:252
  4.6 5.1 %collective-permute-start = (f32[8,32,128]{2,1,0:T(8,128)S(1)}, f32[8,32,128]{2,1,0:T(8,128)S(1)}, u32[]{:S(2)}, u32[]{:S(2)}) collective-permute-start(f32[8,32,128]{2,1,0:T(8,128)S(1)} %get-tuple-element.23), channel_id=1, source_target_pairs={{0,12},{4,0},{8,4},{12,8},{1,13},{5,1},{9,5},{13,9},{2,14},{6,2},{... | collective-permute-start | bytes 393224 | tf_op jit(solution)/shard_map/ppermute | solution.py:247
  9.7 0.0 collective-permute-start.1
  9.7 1.0 %collective-permute-start.2 = (f32[8,32,128]{2,1,0:T(8,128)S(1)}, f32[8,32,128]{2,1,0:T(8,128)S(1)}, u32[]{:S(2)}, u32[]{:S(2)}) collective-permute-start(f32[8,32,128]{2,1,0:T(8,128)S(1)} %get-tuple-element.25), channel_id=1, source_target_pairs={{0,4},{4,8},{8,12},{12,0},{1,5},{5,9},{9,13},{13,1},{2,6},{6,10},{... | collective-permute-start | bytes 393224 | tf_op jit(solution)/shard_map/ppermute | solution.py:247
  10.7 2.9 %collective-permute-done.refs_1_ = f32[8,32,128]{2,1,0:T(8,128)S(1)} collective-permute-done((f32[8,32,128]{2,1,0:T(8,128)S(1)}, f32[8,32,128]{2,1,0:T(8,128)S(1)}, u32[]{:S(2)}, u32[]{:S(2)}) %collective-permute-start) | collective-permute-done | bytes 131104 | tf_op jit(solution)/shard_map/ppermute | solution.py:247
  13.6 7.3 %collective-permute-done.1.refs_2_ = f32[8,32,128]{2,1,0:T(8,128)S(1)} collective-permute-done((f32[8,32,128]{2,1,0:T(8,128)S(1)}, f32[8,32,128]{2,1,0:T(8,128)S(1)}, u32[]{:S(2)}, u32[]{:S(2)}) %collective-permute-start.1) | collective-permute-done | bytes 131104 | tf_op jit(solution)/shard_map/ppermute | solution.py:247
  20.9 0.0 collective-permute-done.2.refs_3_
  20.9 0.1 collective-permute-start.3
  21.0 1.7 %collective-permute-start.8 = (f32[6,32,128]{2,1,0:T(8,128)S(1)}, f32[6,32,128]{2,1,0:T(8,128)S(1)}, u32[]{:S(2)}, u32[]{:S(2)}) collective-permute-start(f32[6,32,128]{2,1,0:T(8,128)S(1)} %get-tuple-element.35), channel_id=1, source_target_pairs={{0,12},{4,0},{8,4},{12,8},{1,13},{5,1},{9,5},{13,9},{2,14},{6,2},{... | collective-permute-start | bytes 294920 | tf_op jit(solution)/shard_map/ppermute | solution.py:247
  22.7 1.1 %collective-permute-start.9 = (f32[6,32,128]{2,1,0:T(8,128)S(1)}, f32[6,32,128]{2,1,0:T(8,128)S(1)}, u32[]{:S(2)}, u32[]{:S(2)}) collective-permute-start(f32[6,32,128]{2,1,0:T(8,128)S(1)} %get-tuple-element.36), channel_id=1, source_target_pairs={{0,8},{4,12},{8,0},{12,4},{1,9},{5,13},{9,1},{13,5},{2,10},{6,14},... | collective-permute-start | bytes 294920 | tf_op jit(solution)/shard_map/ppermute | solution.py:247
  23.8 1.9 %collective-permute-start.10 = (f32[6,32,128]{2,1,0:T(8,128)S(1)}, f32[6,32,128]{2,1,0:T(8,128)S(1)}, u32[]{:S(2)}, u32[]{:S(2)}) collective-permute-start(f32[6,32,128]{2,1,0:T(8,128)S(1)} %get-tuple-element.37), channel_id=1, source_target_pairs={{0,4},{4,8},{8,12},{12,0},{1,5},{5,9},{9,13},{13,1},{2,6},{6,10},{... | collective-permute-start | bytes 294920 | tf_op jit(solution)/shard_map/ppermute | solution.py:247
  25.7 1.6 %early.1 = (f32[16,6,8,128]{3,2,1,0:T(8,128)S(1)}, f32[16,7,8,128]{3,2,1,0:T(8,128)S(1)}) custom-call(f32[8,32,128]{2,1,0:T(8,128)S(1)} %get-tuple-element.22.refs_0_, f32[8,32,128]{2,1,0:T(8,128)S(1)} %collective-permute-done.refs_1_, f32[8,32,128]{2,1,0:T(8,128)S(1)} %collective-permute-done.1.refs_2_, f32[8,32,128]{2,1,0:T(8,128)S(1)} %collective-permute-done.2.refs_3_), custom_call_target="tpu_custom_call" | custom-call | bytes 2500 | tf_op jit(solution)/shard_map/early/pallas_call | solution.py:273
  27.3 0.0 collective-permute-done.3
  27.3 1.6 %collective-permute-start.4 = (f32[4,32,128]{2,1,0:T(8,128)S(1)}, f32[4,32,128]{2,1,0:T(8,128)S(1)}, u32[]{:S(2)}, u32[]{:S(2)}) collective-permute-start(f32[4,32,128]{2,1,0:T(8,128)S(1)} %fusion), channel_id=1, source_target_pairs={{0,2},{1,3},{2,0},{3,1},{4,6},{5,7},{6,4},{7,5},{8,10},{9,11},{10,... | collective-permute-start | bytes 196616 | tf_op jit(solution)/shard_map/ppermute | solution.py:229
  28.9 2.8 %collective-permute-done.4 = f32[4,32,128]{2,1,0:T(8,128)S(1)} collective-permute-done((f32[4,32,128]{2,1,0:T(8,128)S(1)}, f32[4,32,128]{2,1,0:T(8,128)S(1)}, u32[]{:S(2)}, u32[]{:S(2)}) %collective-permute-start.4) | collective-permute-done | bytes 65568 | tf_op jit(solution)/shard_map/ppermute | solution.py:229
  31.7 1.8 %dynamics.1 = (f32[16,7,8,128]{3,2,1,0:T(8,128)S(1)}, f32[32,128]{1,0:T(8,128)}) custom-call(f32[4,32,128]{2,1,0:T(8,128)S(1)} %pad_maximum_fusion.theta_pieces, f32[4,32,128]{2,1,0:T(8,128)S(1)} %fusion.5.total_in, f32[16,7,8,128]{3,2,1,0:T(8,128)S(1)} %get-tuple-element.26.coef_ref.refs_4_), custom_call_target="tpu_custom_call" | custom-call | bytes 2500 | tf_op jit(solution)/shard_map/dynamics/pallas_call | solution.py:283
  33.5 1.5 %late.1 = (f32[6,32,128]{2,1,0:T(8,128)S(1)}, f32[6,32,128]{2,1,0:T(8,128)S(1)}, f32[6,32,128]{2,1,0:T(8,128)S(1)}, f32[6,32,128]{2,1,0:T(8,128)S(1)}) custom-call(f32[16,6,8,128]{3,2,1,0:T(8,128)S(1)} %get-tuple-element.28.held_ref, f32[16,7,8,128]{3,2,1,0:T(8,128)S(1)} %get-tuple-element.29.coef_ref.refs_5_), custom_call_target="tpu_custom_call" | custom-call | bytes 2000 | tf_op jit(solution)/shard_map/late/pallas_call | solution.py:293
  35.0 0.5 collective-permute-start.5
  35.5 2.0 %collective-permute-start.6 = (f32[6,32,128]{2,1,0:T(8,128)S(1)}, f32[6,32,128]{2,1,0:T(8,128)S(1)}, u32[]{:S(2)}, u32[]{:S(2)}) collective-permute-start(f32[6,32,128]{2,1,0:T(8,128)S(1)} %get-tuple-element.32), channel_id=1, source_target_pairs={{0,8},{4,12},{8,0},{12,4},{1,9},{5,13},{9,1},{13,5},{2,10},{6,14},... | collective-permute-start | bytes 294920 | tf_op jit(solution)/shard_map/ppermute | solution.py:247
  37.5 0.0 collective-permute-done.8.refs_1_
  37.5 1.4 %collective-permute-start.7 = (f32[6,32,128]{2,1,0:T(8,128)S(1)}, f32[6,32,128]{2,1,0:T(8,128)S(1)}, u32[]{:S(2)}, u32[]{:S(2)}) collective-permute-start(f32[6,32,128]{2,1,0:T(8,128)S(1)} %get-tuple-element.33), channel_id=1, source_target_pairs={{0,12},{4,0},{8,4},{12,8},{1,13},{5,1},{9,5},{13,9},{2,14},{6,2},{... | collective-permute-start | bytes 294920 | tf_op jit(solution)/shard_map/ppermute | solution.py:247
  38.9 0.0 collective-permute-done.9.refs_2_
  38.9 0.0 collective-permute-done.10.refs_3_
  38.9 2.9 %both.1 = (f32[6,32,128]{2,1,0:T(8,128)S(1)}, f32[6,32,128]{2,1,0:T(8,128)S(1)}, f32[6,32,128]{2,1,0:T(8,128)S(1)}, f32[6,32,128]{2,1,0:T(8,128)S(1)}) custom-call(f32[6,32,128]{2,1,0:T(8,128)S(1)} %get-tuple-element.34.refs_0_, f32[6,32,128]{2,1,0:T(8,128)S(1)} %collective-permute-done.8.refs_1_, f32[6,32,128]{2,1,0:T(8,128)S(1)} %collective-permute-done.9.refs_2_, ...), custom_call_target="tpu_custom_call" | custom-call | bytes 4000 | tf_op jit(solution)/shard_map/both/pallas_call | solution.py:303
  41.8 0.7 %collective-permute-start.11 = (f32[6,32,128]{2,1,0:T(8,128)S(1)}, f32[6,32,128]{2,1,0:T(8,128)S(1)}, u32[]{:S(2)}, u32[]{:S(2)}) collective-permute-start(f32[6,32,128]{2,1,0:T(8,128)S(1)} %get-tuple-element.39), channel_id=1, source_target_pairs={{0,4},{4,8},{8,12},{12,0},{1,5},{5,9},{9,13},{13,1},{2,6},{6,10},{... | collective-permute-start | bytes 294920 | tf_op jit(solution)/shard_map/ppermute | solution.py:247
  42.5 1.4 %collective-permute-start.12 = (f32[6,32,128]{2,1,0:T(8,128)S(1)}, f32[6,32,128]{2,1,0:T(8,128)S(1)}, u32[]{:S(2)}, u32[]{:S(2)}) collective-permute-start(f32[6,32,128]{2,1,0:T(8,128)S(1)} %get-tuple-element.40), channel_id=1, source_target_pairs={{0,8},{4,12},{8,0},{12,4},{1,9},{5,13},{9,1},{13,5},{2,10},{6,14},... | collective-permute-start | bytes 294920 | tf_op jit(solution)/shard_map/ppermute | solution.py:247
  43.9 0.0 collective-permute-done.5.refs_1_
  43.9 2.8 %collective-permute-start.13 = (f32[6,32,128]{2,1,0:T(8,128)S(1)}, f32[6,32,128]{2,1,0:T(8,128)S(1)}, u32[]{:S(2)}, u32[]{:S(2)}) collective-permute-start(f32[6,32,128]{2,1,0:T(8,128)S(1)} %get-tuple-element.41), channel_id=1, source_target_pairs={{0,12},{4,0},{8,4},{12,8},{1,13},{5,1},{9,5},{13,9},{2,14},{6,2},{... | collective-permute-start | bytes 294920 | tf_op jit(solution)/shard_map/ppermute | solution.py:247
  46.8 0.0 collective-permute-done.6.refs_2_
  46.8 0.0 collective-permute-done.7.refs_3_
  46.8 2.2 %collective-permute-done.11.refs_5_ = f32[6,32,128]{2,1,0:T(8,128)S(1)} collective-permute-done((f32[6,32,128]{2,1,0:T(8,128)S(1)}, f32[6,32,128]{2,1,0:T(8,128)S(1)}, u32[]{:S(2)}, u32[]{:S(2)}) %collective-permute-start.11) | collective-permute-done | bytes 98336 | tf_op jit(solution)/shard_map/ppermute | solution.py:247
  49.0 4.1 %collective-permute-done.12.refs_6_ = f32[6,32,128]{2,1,0:T(8,128)S(1)} collective-permute-done((f32[6,32,128]{2,1,0:T(8,128)S(1)}, f32[6,32,128]{2,1,0:T(8,128)S(1)}, u32[]{:S(2)}, u32[]{:S(2)}) %collective-permute-start.12) | collective-permute-done | bytes 98336 | tf_op jit(solution)/shard_map/ppermute | solution.py:247
  53.1 0.0 collective-permute-done.13.refs_7_
  53.1 0.9 %assemble.1 = f32[48,32,128]{2,1,0:T(8,128)} custom-call(s32[1]{0:T(128)} %bitcast.me_ref, f32[6,32,128]{2,1,0:T(8,128)S(1)} %get-tuple-element.30.refs_0_, f32[6,32,128]{2,1,0:T(8,128)S(1)} %collective-permute-done.5.refs_1_, f32[6,32,128]{2,1,0:T(8,128)S(1)} %collective-permute-done.6.refs_2_, f32[6,32,128]{2,1,0:T(8,128)S(1)} %collective-permute-done.7.refs_3_, ...), custom_call_target="tpu_custom_call" | custom-call | bytes 1000 | tf_op jit(solution)/shard_map/assemble/pallas_call | solution.py:314
  (8 shorter events, 0.1 us)
Async XLA Ops:
  1.3 0.7 %copy-start.2 = (s32[1,48]{1,0:T(1,128)S(1)}, s32[1,48]{1,0:T(1,128)}, u32[]{:S(2)}) copy-start(s32[1,48]{1,0:T(1,128)} %flags_hbm.1) | copy-start | bytes 580
  1.3 0.7 %copy-start.3 = (f32[1,48]{1,0:T(1,128)S(1)}, f32[1,48]{1,0:T(1,128)}, u32[]{:S(2)}) copy-start(f32[1,48]{1,0:T(1,128)} %kappa_hbm.1) | copy-start | bytes 580
  2.0 1.1 %copy-start = (f32[1,48,8,4,128]{4,3,2,1,0:T(4,128)S(1)}, f32[1,48,8,4,128]{4,3,2,1,0:T(4,128)}, u32[]{:S(2)}) copy-start(f32[1,48,8,4,128]{4,3,2,1,0:T(4,128)} %param.6) | copy-start | bytes 2359300
  3.1 0.7 %copy-start.1 = (f32[8,4,128]{2,1,0:T(4,128)S(1)}, f32[8,4,128]{2,1,0:T(4,128)}, u32[]{:S(2)}) copy-start(f32[8,4,128]{2,1,0:T(4,128)} %param.5) | copy-start | bytes 49156
  4.6 9.0 %collective-permute-start = (f32[8,32,128]{2,1,0:T(8,128)S(1)}, f32[8,32,128]{2,1,0:T(8,128)S(1)}, u32[]{:S(2)}, u32[]{:S(2)}) collective-permute-start(f32[8,32,128]{2,1,0:T(8,128)S(1)} %get-tuple-element.23), channel_id=1, source_target_pairs={{0,12},{4,0},{8,4},{12,8},{1,13},{5,1},{9,5},{13,9},{2,14},{6,2},{... | collective-permute-start | bytes 393224 | tf_op jit(solution)/shard_map/ppermute | solution.py:247
  9.7 11.2 %collective-permute-start.1 = (f32[8,32,128]{2,1,0:T(8,128)S(1)}, f32[8,32,128]{2,1,0:T(8,128)S(1)}, u32[]{:S(2)}, u32[]{:S(2)}) collective-permute-start(f32[8,32,128]{2,1,0:T(8,128)S(1)} %get-tuple-element.24), channel_id=1, source_target_pairs={{0,8},{4,12},{8,0},{12,4},{1,9},{5,13},{9,1},{13,5},{2,10},{6,14},... | collective-permute-start | bytes 393224 | tf_op jit(solution)/shard_map/ppermute | solution.py:247
  9.7 11.2 %collective-permute-start.2 = (f32[8,32,128]{2,1,0:T(8,128)S(1)}, f32[8,32,128]{2,1,0:T(8,128)S(1)}, u32[]{:S(2)}, u32[]{:S(2)}) collective-permute-start(f32[8,32,128]{2,1,0:T(8,128)S(1)} %get-tuple-element.25), channel_id=1, source_target_pairs={{0,4},{4,8},{8,12},{12,0},{1,5},{5,9},{9,13},{13,1},{2,6},{6,10},{... | collective-permute-start | bytes 393224 | tf_op jit(solution)/shard_map/ppermute | solution.py:247
  20.9 6.3 %collective-permute-start.3 = (f32[4,32,128]{2,1,0:T(8,128)S(1)}, f32[4,32,128]{2,1,0:T(8,128)S(1)}, u32[]{:S(2)}, u32[]{:S(2)}) collective-permute-start(f32[4,32,128]{2,1,0:T(8,128)S(1)} %pad_maximum_fusion.1), channel_id=1, source_target_pairs={{0,1},{1,0},{2,3},{3,2},{4,5},{5,4},{6,7},{7,6},{8,9},{9,8},{10,11... | collective-permute-start | bytes 196616 | tf_op jit(solution)/shard_map/ppermute | solution.py:229
  21.0 16.5 %collective-permute-start.8 = (f32[6,32,128]{2,1,0:T(8,128)S(1)}, f32[6,32,128]{2,1,0:T(8,128)S(1)}, u32[]{:S(2)}, u32[]{:S(2)}) collective-permute-start(f32[6,32,128]{2,1,0:T(8,128)S(1)} %get-tuple-element.35), channel_id=1, source_target_pairs={{0,12},{4,0},{8,4},{12,8},{1,13},{5,1},{9,5},{13,9},{2,14},{6,2},{... | collective-permute-start | bytes 294920 | tf_op jit(solution)/shard_map/ppermute | solution.py:247
  22.7 16.2 %collective-permute-start.9 = (f32[6,32,128]{2,1,0:T(8,128)S(1)}, f32[6,32,128]{2,1,0:T(8,128)S(1)}, u32[]{:S(2)}, u32[]{:S(2)}) collective-permute-start(f32[6,32,128]{2,1,0:T(8,128)S(1)} %get-tuple-element.36), channel_id=1, source_target_pairs={{0,8},{4,12},{8,0},{12,4},{1,9},{5,13},{9,1},{13,5},{2,10},{6,14},... | collective-permute-start | bytes 294920 | tf_op jit(solution)/shard_map/ppermute | solution.py:247
  23.8 15.1 %collective-permute-start.10 = (f32[6,32,128]{2,1,0:T(8,128)S(1)}, f32[6,32,128]{2,1,0:T(8,128)S(1)}, u32[]{:S(2)}, u32[]{:S(2)}) collective-permute-start(f32[6,32,128]{2,1,0:T(8,128)S(1)} %get-tuple-element.37), channel_id=1, source_target_pairs={{0,4},{4,8},{8,12},{12,0},{1,5},{5,9},{9,13},{13,1},{2,6},{6,10},{... | collective-permute-start | bytes 294920 | tf_op jit(solution)/shard_map/ppermute | solution.py:247
  27.3 4.3 %collective-permute-start.4 = (f32[4,32,128]{2,1,0:T(8,128)S(1)}, f32[4,32,128]{2,1,0:T(8,128)S(1)}, u32[]{:S(2)}, u32[]{:S(2)}) collective-permute-start(f32[4,32,128]{2,1,0:T(8,128)S(1)} %fusion), channel_id=1, source_target_pairs={{0,2},{1,3},{2,0},{3,1},{4,6},{5,7},{6,4},{7,5},{8,10},{9,11},{10,... | collective-permute-start | bytes 196616 | tf_op jit(solution)/shard_map/ppermute | solution.py:229
  35.0 9.0 %collective-permute-start.5 = (f32[6,32,128]{2,1,0:T(8,128)S(1)}, f32[6,32,128]{2,1,0:T(8,128)S(1)}, u32[]{:S(2)}, u32[]{:S(2)}) collective-permute-start(f32[6,32,128]{2,1,0:T(8,128)S(1)} %get-tuple-element.31), channel_id=1, source_target_pairs={{0,4},{4,8},{8,12},{12,0},{1,5},{5,9},{9,13},{13,1},{2,6},{6,10},{... | collective-permute-start | bytes 294920 | tf_op jit(solution)/shard_map/ppermute | solution.py:247
  35.5 11.3 %collective-permute-start.6 = (f32[6,32,128]{2,1,0:T(8,128)S(1)}, f32[6,32,128]{2,1,0:T(8,128)S(1)}, u32[]{:S(2)}, u32[]{:S(2)}) collective-permute-start(f32[6,32,128]{2,1,0:T(8,128)S(1)} %get-tuple-element.32), channel_id=1, source_target_pairs={{0,8},{4,12},{8,0},{12,4},{1,9},{5,13},{9,1},{13,5},{2,10},{6,14},... | collective-permute-start | bytes 294920 | tf_op jit(solution)/shard_map/ppermute | solution.py:247
  37.5 9.3 %collective-permute-start.7 = (f32[6,32,128]{2,1,0:T(8,128)S(1)}, f32[6,32,128]{2,1,0:T(8,128)S(1)}, u32[]{:S(2)}, u32[]{:S(2)}) collective-permute-start(f32[6,32,128]{2,1,0:T(8,128)S(1)} %get-tuple-element.33), channel_id=1, source_target_pairs={{0,12},{4,0},{8,4},{12,8},{1,13},{5,1},{9,5},{13,9},{2,14},{6,2},{... | collective-permute-start | bytes 294920 | tf_op jit(solution)/shard_map/ppermute | solution.py:247
  41.8 7.2 %collective-permute-start.11 = (f32[6,32,128]{2,1,0:T(8,128)S(1)}, f32[6,32,128]{2,1,0:T(8,128)S(1)}, u32[]{:S(2)}, u32[]{:S(2)}) collective-permute-start(f32[6,32,128]{2,1,0:T(8,128)S(1)} %get-tuple-element.39), channel_id=1, source_target_pairs={{0,4},{4,8},{8,12},{12,0},{1,5},{5,9},{9,13},{13,1},{2,6},{6,10},{... | collective-permute-start | bytes 294920 | tf_op jit(solution)/shard_map/ppermute | solution.py:247
  42.5 10.6 %collective-permute-start.12 = (f32[6,32,128]{2,1,0:T(8,128)S(1)}, f32[6,32,128]{2,1,0:T(8,128)S(1)}, u32[]{:S(2)}, u32[]{:S(2)}) collective-permute-start(f32[6,32,128]{2,1,0:T(8,128)S(1)} %get-tuple-element.40), channel_id=1, source_target_pairs={{0,8},{4,12},{8,0},{12,4},{1,9},{5,13},{9,1},{13,5},{2,10},{6,14},... | collective-permute-start | bytes 294920 | tf_op jit(solution)/shard_map/ppermute | solution.py:247
  43.9 9.2 %collective-permute-start.13 = (f32[6,32,128]{2,1,0:T(8,128)S(1)}, f32[6,32,128]{2,1,0:T(8,128)S(1)}, u32[]{:S(2)}, u32[]{:S(2)}) collective-permute-start(f32[6,32,128]{2,1,0:T(8,128)S(1)} %get-tuple-element.41), channel_id=1, source_target_pairs={{0,12},{4,0},{8,4},{12,8},{1,13},{5,1},{9,5},{13,9},{2,14},{6,2},{... | collective-permute-start | bytes 294920 | tf_op jit(solution)/shard_map/ppermute | solution.py:247

commit v3 on v2

--- a/solution.py
+++ b/solution.py
@@ -19,50 +19,42 @@
 
 VMEM = pl.BlockSpec(memory_space=pltpu.VMEM)
 SMEM = pl.BlockSpec(memory_space=pltpu.SMEM)
-HBM = pl.BlockSpec(memory_space=pltpu.HBM)
+HBM = pl.BlockSpec(memory_space=pl.ANY)
 
 
 def params():
     return pltpu.CompilerParams(vmem_limit_bytes=48 * 1024 * 1024)
 
 
-def cost(us):
-    return pl.CostEstimate(flops=0, bytes_accessed=int(us * 1.0e3), transcendentals=0)
-
-
-def prepare(tiles, parts, slots, me_ref, counts_ref, flags_hbm, kappa_hbm, theta_hbm, tracers_hbm, *refs):
-    outs = refs[:tiles * len(parts)]
-    flags_ref, kappa_ref, theta_ref, tracers_ref, sems = refs[tiles * len(parts):]
-    copies = [
-        pltpu.make_async_copy(source, target, sems.at[k])
-        for k, (source, target) in enumerate(
-            [(tracers_hbm, tracers_ref), (theta_hbm, theta_ref), (flags_hbm, flags_ref), (kappa_hbm, kappa_ref)]
-        )
-    ]
-    for copy in copies:
-        copy.start()
-    for copy in copies:
-        copy.wait()
+def weigh(slots, counts_ref, flags_ref, kappa_ref, tracers_ref, total_ref):
+    count = counts_ref[0, 0]
+    totals = [jnp.zeros(total_ref.shape, jnp.float32)] * 4
+    for slot in range(slots):
+        weight = jnp.where(slot < count, flags_ref[0, slot].astype(jnp.float32) * kappa_ref[0, slot], 0.0)
+        totals[slot % 4] = totals[slot % 4] + weight * tracers_ref[slot]
+    total_ref[...] = (totals[0] + totals[1]) + (totals[2] + totals[3])
+
+
+def sort_slots(tiles, share, first, part, slots, me_ref, counts_ref, tracers_ref, outs):
     me = me_ref[0]
     count = counts_ref[0, 0]
-    total = jnp.zeros(theta_ref.shape, jnp.float32)
-    share = sum(parts)
-    for step in range(tiles):
-        block = lax.rem(me + step, tiles) * share
-        before = 0
-        for chunk, part in enumerate(parts):
-            for i in range(part):
-                slot = block + before + i
-                safe = jnp.minimum(slot, slots - 1)
-                alive = slot < count
-                field = tracers_ref[safe] * jnp.where(alive, 1.0, 0.0)
-                weight = jnp.where(alive, flags_ref[0, safe].astype(jnp.float32) * kappa_ref[0, safe], 0.0)
-                total = total + weight * field
-                outs[chunk * tiles + step][i] = field
-            before += part
-    for step in range(tiles):
-        outs[step][parts[0]] = theta_ref[...]
-        outs[step][parts[0] + 1] = total
+    for step in range(tiles):
+        block = lax.rem(me + step, tiles) * share + first
+        for i in range(part):
+            slot = block + i
+            safe = jnp.minimum(slot, slots - 1)
+            outs[step][i] = tracers_ref[safe] * jnp.where(slot < count, 1.0, 0.0)
+
+
+def pack_one(tiles, share, part, slots, me_ref, counts_ref, tracers_ref, theta_ref, total_ref, other_ref, *outs):
+    sort_slots(tiles, share, 0, part, slots, me_ref, counts_ref, tracers_ref, outs)
+    for out in outs:
+        out[part] = theta_ref[...]
+        out[part + 1] = total_ref[...] + other_ref[...]
+
+
+def pack_two(tiles, share, first, part, slots, me_ref, counts_ref, tracers_ref, after_ref, *outs):
+    sort_slots(tiles, share, first, part, slots, me_ref, counts_ref, tracers_ref, outs)
 
 
 def coefficients(theta_ref, coef_ref, length):
@@ -222,13 +214,8 @@
         copy.wait()
 
 
-def butterfly(value, axis):
-    size = lax.axis_size(axis)
-    hop = 1
-    while hop < size:
-        value = value + lax.ppermute(value, axis, [(i, i ^ hop) for i in range(size)])
-        hop *= 2
-    return value
+def swap(value, axis, hop):
+    return lax.ppermute(value, axis, [(i, i ^ hop) for i in range(lax.axis_size(axis))])
 
 
 def per_device(theta, tracers, counts, flags, kappa):
@@ -249,25 +236,37 @@
     def gather(payload):
         return [payload[0]] + [shift(payload[tiles - step], tiles - step) for step in range(1, tiles)]
 
-    payload = pl.pallas_call(
-        functools.partial(prepare, tiles, parts, slots),
-        out_shape=[field(parts[0] + 2, *flat)] * tiles + [field(parts[1], *flat)] * tiles,
-        in_specs=[SMEM, SMEM, HBM, HBM, HBM, HBM],
-        out_specs=[VMEM] * (2 * tiles),
-        scratch_shapes=[
-            pltpu.SMEM(flags.shape, jnp.int32),
-            pltpu.SMEM(kappa.shape, f32),
-            scratch(*flat),
-            scratch(slots, *flat),
-            pltpu.SemaphoreType.DMA((4,)),
-        ],
-        compiler_params=params(),
-        cost_estimate=cost(2),
-        name="prepare",
-    )(me, counts, flags, kappa, theta.reshape(flat), tracers[0].reshape(slots, *flat))
-    one = gather(payload[:tiles])
-    two = gather(payload[tiles:])
-    total = butterfly(jnp.stack([piece[parts[0] + 1] for piece in one]), "group")
+    tracers = tracers[0].reshape(slots, *flat)
+    theta = theta.reshape(flat)
+    total = pl.pallas_call(
+        functools.partial(weigh, slots),
+        out_shape=field(*flat),
+        in_specs=[SMEM, SMEM, SMEM, VMEM],
+        out_specs=VMEM,
+        compiler_params=params(),
+        name="weigh",
+    )(counts, flags, kappa, tracers)
+    one = gather(pl.pallas_call(
+        functools.partial(pack_one, tiles, share, parts[0], slots),
+        out_shape=[field(parts[0] + 2, *flat)] * tiles,
+        in_specs=[SMEM, SMEM] + [VMEM] * 4,
+        out_specs=[VMEM] * tiles,
+        compiler_params=params(),
+        name="pack_one",
+    )(me, counts, tracers, theta, total, swap(total, "group", 1)))
+    two = gather(pl.pallas_call(
+        functools.partial(pack_two, tiles, share, parts[0], parts[1], slots),
+        out_shape=[field(parts[1], *flat)] * tiles,
+        in_specs=[SMEM, SMEM, VMEM, HBM],
+        out_specs=[VMEM] * tiles,
+        compiler_params=params(),
+        name="pack_two",
+    )(me, counts, tracers, one[0]))
+    total = jnp.stack([piece[parts[0] + 1] for piece in one])
+    hop = 2
+    while hop < lax.axis_size("group"):
+        total = total + swap(total, "group", hop)
+        hop *= 2
     grid_theta = jnp.stack([piece[parts[0]] for piece in one])
 
     held, coef = pl.pallas_call(
@@ -277,7 +276,6 @@
         out_specs=[VMEM] * 2,
         scratch_shapes=[scratch(length, nz, ny), scratch(length, parts[0], nz, ny)],
         compiler_params=params(),
-        cost_estimate=cost(2.5),
         name="early",
     )(*one)
     next_coef, theta_new = pl.pallas_call(
@@ -287,7 +285,6 @@
         out_specs=[VMEM] * 2,
         scratch_shapes=[scratch(length, 1, nz, ny), scratch(length, 1, nz, ny), scratch(length, nz, ny)],
         compiler_params=params(),
-        cost_estimate=cost(2.5),
         name="dynamics",
     )(grid_theta, total, coef)
     done_one = pl.pallas_call(
@@ -297,7 +294,6 @@
         out_specs=[VMEM] * tiles,
         scratch_shapes=[scratch(length, parts[0], nz, ny)] * 2,
         compiler_params=params(),
-        cost_estimate=cost(2),
         name="late",
     )(held, next_coef)
     done_two = pl.pallas_call(
@@ -307,7 +303,6 @@
         out_specs=[VMEM] * tiles,
         scratch_shapes=[scratch(length, parts[1], nz, ny)] * 2,
         compiler_params=params(),
-        cost_estimate=cost(4),
         name="both",
     )(*two, coef, next_coef)
     back = [piece for done in (done_one, done_two) for piece in [done[0]] + [shift(done[step], step) for step in range(1, tiles)]]
@@ -318,7 +313,6 @@
         out_specs=HBM,
         scratch_shapes=[pltpu.SemaphoreType.DMA((2 * tiles,))],
         compiler_params=params(),
-        cost_estimate=cost(1),
         name="assemble",
     )(me, *back)
     return theta_new.reshape(nz, rows, ny), out[:slots].reshape(1, slots, nz, rows, ny)

time: 54.3 us -> 52.7 us (0.971)
  waiting for transfers between devices: 19.3 us -> 9 us
  starting transfers between devices: 21.3 us -> 30.9 us
  local copies, waits for them, and re-layouts: 2.52 us -> 1.81 us
    ppermute x12, waiting for transfers between devices: 16.5 us -> 6.97 us  [shift(): lax.ppermute(value, 'tile', [(i, (i + step) % tiles) for i in range(tiles)])]
    ppermute x12, starting transfers between devices: 19.7 us -> 28.8 us  [shift(): lax.ppermute(value, 'tile', [(i, (i + step) % tiles) for i in range(tiles)])]
    ppermute x2, waiting for transfers between devices: 2.77 us -> 2.04 us  [swap(): lax.ppermute(value, axis, [(i, i ^ hop) for i in range(lax.axis_size(axis...]
    unnamed x8 -> x10, local copies, waits for them, and re-layouts: 2.51 us -> 1.8 us
  transfers between devices with their start and end apart: 14 -> 14, of which waited for: 5 -> 6; matrix products, arithmetic and copies ran while one was open for 0% -> 0% of each run, Pallas kernels for 14% -> 15%
where the time goes in v3:
time: 52.7 us; the launch traced here: 52.6 us
  starting transfers between devices  30.9 us (59%)
  Pallas kernels  9.44 us (18%)
  waiting for transfers between devices  9 us (17%)
  local copies, waits for them, and re-layouts  1.81 us (3%)
  between operations  1.39 us (3%)
    ppermute x12, starting transfers between devices, shift(): lax.ppermute(value, 'tile', [(i, (i + step) % tiles) for i in range(tiles)])  28.8 us
    ppermute x12, waiting for transfers between devices, shift(): lax.ppermute(value, 'tile', [(i, (i + step) % tiles) for i in range(tiles)])  6.97 us
    pallas_call x1, Pallas kernels, per_device(): pl.pallas_call(functools.partial(both, tiles, parts[1], rows, nz), out_sh...  2.9 us
    ppermute x2, starting transfers between devices, swap(): lax.ppermute(value, axis, [(i, i ^ hop) for i in range(lax.axis_size(axis...  2.07 us
    ppermute x2, waiting for transfers between devices, swap(): lax.ppermute(value, axis, [(i, i ^ hop) for i in range(lax.axis_size(axis...  2.04 us
    pallas_call x1, Pallas kernels, per_device(): pl.pallas_call(functools.partial(dynamics_call, tiles, rows, nz), out_sha...  1.84 us
    unnamed x10, local copies, waits for them, and re-layouts  1.8 us
    pallas_call x1, Pallas kernels, per_device(): pl.pallas_call(functools.partial(early, tiles, parts[0], rows, nz), out_s...  1.56 us
  transfers between devices with their start and end apart: 14, of which 6 were waited for; matrix products, arithmetic and copies ran while one was open for 0% of the time, Pallas kernels for 15%

profile of v3, /device:TPU:0, one launch (start us, length us, event | category | flops | bytes accessed | tf_op | source)
XLA Modules:
  0.0 52.6 jit_solution(13913697894629382367)
XLA Ops:
  1.3 0.0 copy-start.3
  1.3 0.0 copy-start.4
  1.3 0.6 %copy-done.3 = s32[1,48]{1,0:T(1,128)S(1)} copy-done((s32[1,48]{1,0:T(1,128)S(1)}, s32[1,48]{1,0:T(1,128)}, u32[]{:S(2)}) %copy-start.3) | copy-done | bytes 216
  1.9 0.0 copy-done.4
  1.9 0.0 copy-start
  2.0 1.1 %copy-done = f32[1,48,8,4,128]{4,3,2,1,0:T(4,128)S(1)} copy-done((f32[1,48,8,4,128]{4,3,2,1,0:T(4,128)S(1)}, f32[1,48,8,4,128]{4,3,2,1,0:T(4,128)}, u32[]{:S(2)}) %copy-start) | copy-done | bytes 786456
  3.1 0.0 copy-start.1
  3.1 0.0 copy-start.2
  3.1 0.6 %weigh.1.total_ref = f32[32,128]{1,0:T(8,128)S(1)} custom-call(s32[1,1]{1,0:T(1,128)S(6)} %copy.7.counts_ref, s32[1,48]{1,0:T(1,128)S(1)} %copy-done.3, f32[1,48]{1,0:T(1,128)S(1)} %copy-done.4, f32[48,32,128]{2,1,0:T(8,128)S(1)} %bitcast.5), custom_call_target="tpu_custom_call" | custom-call | tf_op jit(solution)/shard_map/weigh/pallas_call | solution.py:241
  3.7 0.5 collective-permute-start
  4.2 0.8 %collective-permute-done.other_ref = f32[32,128]{1,0:T(8,128)S(1)} collective-permute-done((f32[32,128]{1,0:T(8,128)S(1)}, f32[32,128]{1,0:T(8,128)S(1)}, u32[]{:S(2)}, u32[]{:S(2)}) %collective-permute-start) | collective-permute-done | bytes 16416 | tf_op jit(solution)/shard_map/ppermute | solution.py:218
  5.1 0.0 copy-done.1
  5.1 0.0 copy-done.2
  5.1 3.0 %collective-permute-start.3 = (f32[8,32,128]{2,1,0:T(8,128)S(1)}, f32[8,32,128]{2,1,0:T(8,128)S(1)}, u32[]{:S(2)}, u32[]{:S(2)}) collective-permute-start(f32[8,32,128]{2,1,0:T(8,128)S(1)} %get-tuple-element.25), channel_id=1, source_target_pairs={{0,4},{4,8},{8,12},{12,0},{1,5},{5,9},{9,13},{13,1},{2,6},{6,10},{... | collective-permute-start | bytes 393224 | tf_op jit(solution)/shard_map/ppermute | solution.py:234
  8.1 2.6 %collective-permute-start.2 = (f32[8,32,128]{2,1,0:T(8,128)S(1)}, f32[8,32,128]{2,1,0:T(8,128)S(1)}, u32[]{:S(2)}, u32[]{:S(2)}) collective-permute-start(f32[8,32,128]{2,1,0:T(8,128)S(1)} %get-tuple-element.24), channel_id=1, source_target_pairs={{0,8},{4,12},{8,0},{12,4},{1,9},{5,13},{9,1},{13,5},{2,10},{6,14},... | collective-permute-start | bytes 393224 | tf_op jit(solution)/shard_map/ppermute | solution.py:234
  10.7 1.3 %collective-permute-start.1 = (f32[8,32,128]{2,1,0:T(8,128)S(1)}, f32[8,32,128]{2,1,0:T(8,128)S(1)}, u32[]{:S(2)}, u32[]{:S(2)}) collective-permute-start(f32[8,32,128]{2,1,0:T(8,128)S(1)} %get-tuple-element.23), channel_id=1, source_target_pairs={{0,12},{4,0},{8,4},{12,8},{1,13},{5,1},{9,5},{13,9},{2,14},{6,2},{... | collective-permute-start | bytes 393224 | tf_op jit(solution)/shard_map/ppermute | solution.py:234
  12.1 0.5 collective-permute-start.8
  12.6 1.7 %collective-permute-start.9 = (f32[6,32,128]{2,1,0:T(8,128)S(1)}, f32[6,32,128]{2,1,0:T(8,128)S(1)}, u32[]{:S(2)}, u32[]{:S(2)}) collective-permute-start(f32[6,32,128]{2,1,0:T(8,128)S(1)} %get-tuple-element.36), channel_id=1, source_target_pairs={{0,8},{4,12},{8,0},{12,4},{1,9},{5,13},{9,1},{13,5},{2,10},{6,14},... | collective-permute-start | bytes 294920 | tf_op jit(solution)/shard_map/ppermute | solution.py:234
  14.3 0.2 collective-permute-done.3.refs_3_
  14.5 8.6 %collective-permute-start.10 = (f32[6,32,128]{2,1,0:T(8,128)S(1)}, f32[6,32,128]{2,1,0:T(8,128)S(1)}, u32[]{:S(2)}, u32[]{:S(2)}) collective-permute-start(f32[6,32,128]{2,1,0:T(8,128)S(1)} %get-tuple-element.37), channel_id=1, source_target_pairs={{0,4},{4,8},{8,12},{12,0},{1,5},{5,9},{9,13},{13,1},{2,6},{6,10},{... | collective-permute-start | bytes 294920 | tf_op jit(solution)/shard_map/ppermute | solution.py:234
  23.2 0.0 collective-permute-done.2.refs_2_
  23.2 0.0 collective-permute-done.1.refs_1_
  23.2 1.6 %collective-permute-start.4 = (f32[4,32,128]{2,1,0:T(8,128)S(1)}, f32[4,32,128]{2,1,0:T(8,128)S(1)}, u32[]{:S(2)}, u32[]{:S(2)}) collective-permute-start(f32[4,32,128]{2,1,0:T(8,128)S(1)} %pad_maximum_fusion.1), channel_id=1, source_target_pairs={{0,2},{1,3},{2,0},{3,1},{4,6},{5,7},{6,4},{7,5},{8,10},{9,11},{10,... | collective-permute-start | bytes 196616 | tf_op jit(solution)/shard_map/ppermute | solution.py:218
  24.8 1.6 %early.1 = (f32[16,6,8,128]{3,2,1,0:T(8,128)S(1)}, f32[16,7,8,128]{3,2,1,0:T(8,128)S(1)}) custom-call(f32[8,32,128]{2,1,0:T(8,128)S(1)} %get-tuple-element.22.refs_0_.after_ref, f32[8,32,128]{2,1,0:T(8,128)S(1)} %collective-permute-done.1.refs_1_, f32[8,32,128]{2,1,0:T(8,128)S(1)} %collective-permute-done.2.refs_2_, ...), custom_call_target="tpu_custom_call" | custom-call | tf_op jit(solution)/shard_map/early/pallas_call | solution.py:272
  26.3 1.2 %collective-permute-done.4 = f32[4,32,128]{2,1,0:T(8,128)S(1)} collective-permute-done((f32[4,32,128]{2,1,0:T(8,128)S(1)}, f32[4,32,128]{2,1,0:T(8,128)S(1)}, u32[]{:S(2)}, u32[]{:S(2)}) %collective-permute-start.4) | collective-permute-done | bytes 65568 | tf_op jit(solution)/shard_map/ppermute | solution.py:218
  27.6 1.8 %dynamics.1 = (f32[16,7,8,128]{3,2,1,0:T(8,128)S(1)}, f32[32,128]{1,0:T(8,128)}) custom-call(f32[4,32,128]{2,1,0:T(8,128)S(1)} %pad_maximum_fusion.theta_pieces, f32[4,32,128]{2,1,0:T(8,128)S(1)} %fusion.total_in, f32[16,7,8,128]{3,2,1,0:T(8,128)S(1)} %get-tuple-element.26.coef_ref.refs_4_), custom_call_target="tpu_custom_call" | custom-call | tf_op jit(solution)/shard_map/dynamics/pallas_call | solution.py:281
  29.4 1.5 %late.1 = (f32[6,32,128]{2,1,0:T(8,128)S(1)}, f32[6,32,128]{2,1,0:T(8,128)S(1)}, f32[6,32,128]{2,1,0:T(8,128)S(1)}, f32[6,32,128]{2,1,0:T(8,128)S(1)}) custom-call(f32[16,6,8,128]{3,2,1,0:T(8,128)S(1)} %get-tuple-element.28.held_ref, f32[16,7,8,128]{3,2,1,0:T(8,128)S(1)} %get-tuple-element.29.coef_ref.refs_5_), custom_call_target="tpu_custom_call" | custom-call | tf_op jit(solution)/shard_map/late/pallas_call | solution.py:290
  30.9 4.2 %collective-permute-start.5 = (f32[6,32,128]{2,1,0:T(8,128)S(1)}, f32[6,32,128]{2,1,0:T(8,128)S(1)}, u32[]{:S(2)}, u32[]{:S(2)}) collective-permute-start(f32[6,32,128]{2,1,0:T(8,128)S(1)} %get-tuple-element.31), channel_id=1, source_target_pairs={{0,4},{4,8},{8,12},{12,0},{1,5},{5,9},{9,13},{13,1},{2,6},{6,10},{... | collective-permute-start | bytes 294920 | tf_op jit(solution)/shard_map/ppermute | solution.py:234
  35.0 2.4 %collective-permute-start.6 = (f32[6,32,128]{2,1,0:T(8,128)S(1)}, f32[6,32,128]{2,1,0:T(8,128)S(1)}, u32[]{:S(2)}, u32[]{:S(2)}) collective-permute-start(f32[6,32,128]{2,1,0:T(8,128)S(1)} %get-tuple-element.32), channel_id=1, source_target_pairs={{0,8},{4,12},{8,0},{12,4},{1,9},{5,13},{9,1},{13,5},{2,10},{6,14},... | collective-permute-start | bytes 294920 | tf_op jit(solution)/shard_map/ppermute | solution.py:234
  37.4 0.0 collective-permute-done.8.refs_1_
  37.4 0.0 collective-permute-start.7
  37.5 0.0 collective-permute-done.9.refs_2_
  37.5 0.0 collective-permute-done.10.refs_3_
  37.5 2.9 %both.1 = (f32[6,32,128]{2,1,0:T(8,128)S(1)}, f32[6,32,128]{2,1,0:T(8,128)S(1)}, f32[6,32,128]{2,1,0:T(8,128)S(1)}, f32[6,32,128]{2,1,0:T(8,128)S(1)}) custom-call(f32[6,32,128]{2,1,0:T(8,128)S(1)} %get-tuple-element.34.refs_0_, f32[6,32,128]{2,1,0:T(8,128)S(1)} %collective-permute-done.8.refs_1_, f32[6,32,128]{2,1,0:T(8,128)S(1)} %collective-permute-done.9.refs_2_, ...), custom_call_target="tpu_custom_call" | custom-call | tf_op jit(solution)/shard_map/both/pallas_call | solution.py:299
  40.4 2.0 %collective-permute-start.11 = (f32[6,32,128]{2,1,0:T(8,128)S(1)}, f32[6,32,128]{2,1,0:T(8,128)S(1)}, u32[]{:S(2)}, u32[]{:S(2)}) collective-permute-start(f32[6,32,128]{2,1,0:T(8,128)S(1)} %get-tuple-element.39), channel_id=1, source_target_pairs={{0,4},{4,8},{8,12},{12,0},{1,5},{5,9},{9,13},{13,1},{2,6},{6,10},{... | collective-permute-start | bytes 294920 | tf_op jit(solution)/shard_map/ppermute | solution.py:234
  42.4 0.5 %collective-permute-start.12 = (f32[6,32,128]{2,1,0:T(8,128)S(1)}, f32[6,32,128]{2,1,0:T(8,128)S(1)}, u32[]{:S(2)}, u32[]{:S(2)}) collective-permute-start(f32[6,32,128]{2,1,0:T(8,128)S(1)} %get-tuple-element.40), channel_id=1, source_target_pairs={{0,8},{4,12},{8,0},{12,4},{1,9},{5,13},{9,1},{13,5},{2,10},{6,14},... | collective-permute-start | bytes 294920 | tf_op jit(solution)/shard_map/ppermute | solution.py:234
  43.0 0.0 collective-permute-done.5.refs_1_
  43.0 1.9 %collective-permute-start.13 = (f32[6,32,128]{2,1,0:T(8,128)S(1)}, f32[6,32,128]{2,1,0:T(8,128)S(1)}, u32[]{:S(2)}, u32[]{:S(2)}) collective-permute-start(f32[6,32,128]{2,1,0:T(8,128)S(1)} %get-tuple-element.41), channel_id=1, source_target_pairs={{0,12},{4,0},{8,4},{12,8},{1,13},{5,1},{9,5},{13,9},{2,14},{6,2},{... | collective-permute-start | bytes 294920 | tf_op jit(solution)/shard_map/ppermute | solution.py:234
  44.9 0.5 collective-permute-done.6.refs_2_
  45.4 0.0 collective-permute-done.7.refs_3_
  45.4 2.1 %collective-permute-done.11.refs_5_ = f32[6,32,128]{2,1,0:T(8,128)S(1)} collective-permute-done((f32[6,32,128]{2,1,0:T(8,128)S(1)}, f32[6,32,128]{2,1,0:T(8,128)S(1)}, u32[]{:S(2)}, u32[]{:S(2)}) %collective-permute-start.11) | collective-permute-done | bytes 98336 | tf_op jit(solution)/shard_map/ppermute | solution.py:234
  47.5 4.1 %collective-permute-done.12.refs_6_ = f32[6,32,128]{2,1,0:T(8,128)S(1)} collective-permute-done((f32[6,32,128]{2,1,0:T(8,128)S(1)}, f32[6,32,128]{2,1,0:T(8,128)S(1)}, u32[]{:S(2)}, u32[]{:S(2)}) %collective-permute-start.12) | collective-permute-done | bytes 98336 | tf_op jit(solution)/shard_map/ppermute | solution.py:234
  51.6 0.0 collective-permute-done.13.refs_7_
  51.6 0.9 %assemble.1 = f32[48,32,128]{2,1,0:T(8,128)} custom-call(s32[1]{0:T(128)} %bitcast.me_ref, f32[6,32,128]{2,1,0:T(8,128)S(1)} %get-tuple-element.30.refs_0_, f32[6,32,128]{2,1,0:T(8,128)S(1)} %collective-permute-done.5.refs_1_, f32[6,32,128]{2,1,0:T(8,128)S(1)} %collective-permute-done.6.refs_2_, f32[6,32,128]{2,1,0:T(8,128)S(1)} %collective-permute-done.7.refs_3_, ...), custom_call_target="tpu_custom_call" | custom-call | tf_op jit(solution)/shard_map/assemble/pallas_call | solution.py:309
  (9 shorter events, 0.1 us)
Async XLA Ops:
  1.3 0.7 %copy-start.3 = (s32[1,48]{1,0:T(1,128)S(1)}, s32[1,48]{1,0:T(1,128)}, u32[]{:S(2)}) copy-start(s32[1,48]{1,0:T(1,128)} %flags_ref.1) | copy-start | bytes 580
  1.3 0.7 %copy-start.4 = (f32[1,48]{1,0:T(1,128)S(1)}, f32[1,48]{1,0:T(1,128)}, u32[]{:S(2)}) copy-start(f32[1,48]{1,0:T(1,128)} %kappa_ref.1) | copy-start | bytes 580
  1.9 1.1 %copy-start = (f32[1,48,8,4,128]{4,3,2,1,0:T(4,128)S(1)}, f32[1,48,8,4,128]{4,3,2,1,0:T(4,128)}, u32[]{:S(2)}) copy-start(f32[1,48,8,4,128]{4,3,2,1,0:T(4,128)} %param.6) | copy-start | bytes 2359300
  3.1 2.0 %copy-start.1 = (f32[1,48,8,4,128]{4,3,2,1,0:T(4,128)S(1)}, f32[1,48,8,4,128]{4,3,2,1,0:T(4,128)}, u32[]{:S(2)}) copy-start(f32[1,48,8,4,128]{4,3,2,1,0:T(4,128)} %param.6) | copy-start | bytes 2359300
  3.1 2.0 %copy-start.2 = (f32[8,4,128]{2,1,0:T(4,128)S(1)}, f32[8,4,128]{2,1,0:T(4,128)}, u32[]{:S(2)}) copy-start(f32[8,4,128]{2,1,0:T(4,128)} %param.5) | copy-start | bytes 49156
  3.7 1.4 %collective-permute-start = (f32[32,128]{1,0:T(8,128)S(1)}, f32[32,128]{1,0:T(8,128)S(1)}, u32[]{:S(2)}, u32[]{:S(2)}) collective-permute-start(f32[32,128]{1,0:T(8,128)S(1)} %weigh.1.total_ref), channel_id=1, source_target_pairs={{0,1},{1,0},{2,3},{3,2},{4,5},{5,4},{6,7},{7,6},{8,9},{9,8},{10,11... | collective-permute-start | bytes 49160 | tf_op jit(solution)/shard_map/ppermute | solution.py:218
  5.1 9.4 %collective-permute-start.3 = (f32[8,32,128]{2,1,0:T(8,128)S(1)}, f32[8,32,128]{2,1,0:T(8,128)S(1)}, u32[]{:S(2)}, u32[]{:S(2)}) collective-permute-start(f32[8,32,128]{2,1,0:T(8,128)S(1)} %get-tuple-element.25), channel_id=1, source_target_pairs={{0,4},{4,8},{8,12},{12,0},{1,5},{5,9},{9,13},{13,1},{2,6},{6,10},{... | collective-permute-start | bytes 393224 | tf_op jit(solution)/shard_map/ppermute | solution.py:234
  8.1 15.1 %collective-permute-start.2 = (f32[8,32,128]{2,1,0:T(8,128)S(1)}, f32[8,32,128]{2,1,0:T(8,128)S(1)}, u32[]{:S(2)}, u32[]{:S(2)}) collective-permute-start(f32[8,32,128]{2,1,0:T(8,128)S(1)} %get-tuple-element.24), channel_id=1, source_target_pairs={{0,8},{4,12},{8,0},{12,4},{1,9},{5,13},{9,1},{13,5},{2,10},{6,14},... | collective-permute-start | bytes 393224 | tf_op jit(solution)/shard_map/ppermute | solution.py:234
  10.7 12.5 %collective-permute-start.1 = (f32[8,32,128]{2,1,0:T(8,128)S(1)}, f32[8,32,128]{2,1,0:T(8,128)S(1)}, u32[]{:S(2)}, u32[]{:S(2)}) collective-permute-start(f32[8,32,128]{2,1,0:T(8,128)S(1)} %get-tuple-element.23), channel_id=1, source_target_pairs={{0,12},{4,0},{8,4},{12,8},{1,13},{5,1},{9,5},{13,9},{2,14},{6,2},{... | collective-permute-start | bytes 393224 | tf_op jit(solution)/shard_map/ppermute | solution.py:234
  12.1 25.3 %collective-permute-start.8 = (f32[6,32,128]{2,1,0:T(8,128)S(1)}, f32[6,32,128]{2,1,0:T(8,128)S(1)}, u32[]{:S(2)}, u32[]{:S(2)}) collective-permute-start(f32[6,32,128]{2,1,0:T(8,128)S(1)} %get-tuple-element.35), channel_id=1, source_target_pairs={{0,12},{4,0},{8,4},{12,8},{1,13},{5,1},{9,5},{13,9},{2,14},{6,2},{... | collective-permute-start | bytes 294920 | tf_op jit(solution)/shard_map/ppermute | solution.py:234
  12.6 24.9 %collective-permute-start.9 = (f32[6,32,128]{2,1,0:T(8,128)S(1)}, f32[6,32,128]{2,1,0:T(8,128)S(1)}, u32[]{:S(2)}, u32[]{:S(2)}) collective-permute-start(f32[6,32,128]{2,1,0:T(8,128)S(1)} %get-tuple-element.36), channel_id=1, source_target_pairs={{0,8},{4,12},{8,0},{12,4},{1,9},{5,13},{9,1},{13,5},{2,10},{6,14},... | collective-permute-start | bytes 294920 | tf_op jit(solution)/shard_map/ppermute | solution.py:234
  14.5 23.0 %collective-permute-start.10 = (f32[6,32,128]{2,1,0:T(8,128)S(1)}, f32[6,32,128]{2,1,0:T(8,128)S(1)}, u32[]{:S(2)}, u32[]{:S(2)}) collective-permute-start(f32[6,32,128]{2,1,0:T(8,128)S(1)} %get-tuple-element.37), channel_id=1, source_target_pairs={{0,4},{4,8},{8,12},{12,0},{1,5},{5,9},{9,13},{13,1},{2,6},{6,10},{... | collective-permute-start | bytes 294920 | tf_op jit(solution)/shard_map/ppermute | solution.py:234
  23.2 4.3 %collective-permute-start.4 = (f32[4,32,128]{2,1,0:T(8,128)S(1)}, f32[4,32,128]{2,1,0:T(8,128)S(1)}, u32[]{:S(2)}, u32[]{:S(2)}) collective-permute-start(f32[4,32,128]{2,1,0:T(8,128)S(1)} %pad_maximum_fusion.1), channel_id=1, source_target_pairs={{0,2},{1,3},{2,0},{3,1},{4,6},{5,7},{6,4},{7,5},{8,10},{9,11},{10,... | collective-permute-start | bytes 196616 | tf_op jit(solution)/shard_map/ppermute | solution.py:218
  30.9 12.1 %collective-permute-start.5 = (f32[6,32,128]{2,1,0:T(8,128)S(1)}, f32[6,32,128]{2,1,0:T(8,128)S(1)}, u32[]{:S(2)}, u32[]{:S(2)}) collective-permute-start(f32[6,32,128]{2,1,0:T(8,128)S(1)} %get-tuple-element.31), channel_id=1, source_target_pairs={{0,4},{4,8},{8,12},{12,0},{1,5},{5,9},{9,13},{13,1},{2,6},{6,10},{... | collective-permute-start | bytes 294920 | tf_op jit(solution)/shard_map/ppermute | solution.py:234
  35.0 10.3 %collective-permute-start.6 = (f32[6,32,128]{2,1,0:T(8,128)S(1)}, f32[6,32,128]{2,1,0:T(8,128)S(1)}, u32[]{:S(2)}, u32[]{:S(2)}) collective-permute-start(f32[6,32,128]{2,1,0:T(8,128)S(1)} %get-tuple-element.32), channel_id=1, source_target_pairs={{0,8},{4,12},{8,0},{12,4},{1,9},{5,13},{9,1},{13,5},{2,10},{6,14},... | collective-permute-start | bytes 294920 | tf_op jit(solution)/shard_map/ppermute | solution.py:234
  37.4 7.9 %collective-permute-start.7 = (f32[6,32,128]{2,1,0:T(8,128)S(1)}, f32[6,32,128]{2,1,0:T(8,128)S(1)}, u32[]{:S(2)}, u32[]{:S(2)}) collective-permute-start(f32[6,32,128]{2,1,0:T(8,128)S(1)} %get-tuple-element.33), channel_id=1, source_target_pairs={{0,12},{4,0},{8,4},{12,8},{1,13},{5,1},{9,5},{13,9},{2,14},{6,2},{... | collective-permute-start | bytes 294920 | tf_op jit(solution)/shard_map/ppermute | solution.py:234
  40.4 7.1 %collective-permute-start.11 = (f32[6,32,128]{2,1,0:T(8,128)S(1)}, f32[6,32,128]{2,1,0:T(8,128)S(1)}, u32[]{:S(2)}, u32[]{:S(2)}) collective-permute-start(f32[6,32,128]{2,1,0:T(8,128)S(1)} %get-tuple-element.39), channel_id=1, source_target_pairs={{0,4},{4,8},{8,12},{12,0},{1,5},{5,9},{9,13},{13,1},{2,6},{6,10},{... | collective-permute-start | bytes 294920 | tf_op jit(solution)/shard_map/ppermute | solution.py:234
  42.4 9.2 %collective-permute-start.12 = (f32[6,32,128]{2,1,0:T(8,128)S(1)}, f32[6,32,128]{2,1,0:T(8,128)S(1)}, u32[]{:S(2)}, u32[]{:S(2)}) collective-permute-start(f32[6,32,128]{2,1,0:T(8,128)S(1)} %get-tuple-element.40), channel_id=1, source_target_pairs={{0,8},{4,12},{8,0},{12,4},{1,9},{5,13},{9,1},{13,5},{2,10},{6,14},... | collective-permute-start | bytes 294920 | tf_op jit(solution)/shard_map/ppermute | solution.py:234
  43.0 8.7 %collective-permute-start.13 = (f32[6,32,128]{2,1,0:T(8,128)S(1)}, f32[6,32,128]{2,1,0:T(8,128)S(1)}, u32[]{:S(2)}, u32[]{:S(2)}) collective-permute-start(f32[6,32,128]{2,1,0:T(8,128)S(1)} %get-tuple-element.41), channel_id=1, source_target_pairs={{0,12},{4,0},{8,4},{12,8},{1,13},{5,1},{9,5},{13,9},{2,14},{6,2},{... | collective-permute-start | bytes 294920 | tf_op jit(solution)/shard_map/ppermute | solution.py:234

commit v4 on v3

--- a/solution.py
+++ b/solution.py
@@ -222,7 +222,7 @@
     _, slots, nz, rows, ny = tracers.shape
     tiles = lax.axis_size("tile")
     share = max(2, -(-slots // tiles))
-    parts = (share // 2, share - share // 2)
+    parts = (max(1, share // 3), share - max(1, share // 3))
     length = tiles * rows
     me = lax.axis_index("tile").astype(jnp.int32).reshape(1)
     flat = (nz * rows, ny)

time: 52.7 us -> 55.3 us (1.049)
  waiting for transfers between devices: 9 us -> 17.4 us
  starting transfers between devices: 30.9 us -> 25 us
    ppermute x12, waiting for transfers between devices: 6.97 us -> 15 us  [shift(): lax.ppermute(value, 'tile', [(i, (i + step) % tiles) for i in range(tiles)])]
    ppermute x12, starting transfers between devices: 28.8 us -> 22.9 us  [shift(): lax.ppermute(value, 'tile', [(i, (i + step) % tiles) for i in range(tiles)])]
    pallas_call x1, Pallas kernels: 2.9 us -> 3.73 us  [per_device(): pl.pallas_call(functools.partial(both, tiles, parts[1], rows, nz), out_sh...]
  transfers between devices with their start and end apart: 14 -> 14, of which waited for: 6 -> 4; matrix products, arithmetic and copies ran while one was open for 0% -> 0% of each run, Pallas kernels for 15% -> 14%
where the time goes in v4:
time: 55.3 us; the launch traced here: 55.1 us
  starting transfers between devices  25 us (45%)
  waiting for transfers between devices  17.4 us (31%)
  Pallas kernels  9.44 us (17%)
  local copies, waits for them, and re-layouts  1.81 us (3%)
  between operations  1.4 us (3%)
    ppermute x12, starting transfers between devices, shift(): lax.ppermute(value, 'tile', [(i, (i + step) % tiles) for i in range(tiles)])  22.9 us
    ppermute x12, waiting for transfers between devices, shift(): lax.ppermute(value, 'tile', [(i, (i + step) % tiles) for i in range(tiles)])  15 us
    pallas_call x1, Pallas kernels, per_device(): pl.pallas_call(functools.partial(both, tiles, parts[1], rows, nz), out_sh...  3.73 us
    ppermute x2, waiting for transfers between devices, swap(): lax.ppermute(value, axis, [(i, i ^ hop) for i in range(lax.axis_size(axis...  2.45 us
    ppermute x2, starting transfers between devices, swap(): lax.ppermute(value, axis, [(i, i ^ hop) for i in range(lax.axis_size(axis...  2.07 us
    pallas_call x1, Pallas kernels, per_device(): pl.pallas_call(functools.partial(dynamics_call, tiles, rows, nz), out_sha...  1.84 us
    unnamed x10, local copies, waits for them, and re-layouts  1.8 us
    pallas_call x1, Pallas kernels, per_device(): pl.pallas_call(functools.partial(early, tiles, parts[0], rows, nz), out_s...  1.14 us
  transfers between devices with their start and end apart: 14, of which 4 were waited for; matrix products, arithmetic and copies ran while one was open for 0% of the time, Pallas kernels for 14%

profile of v4, /device:TPU:0, one launch (start us, length us, event | category | flops | bytes accessed | tf_op | source)
XLA Modules:
  0.0 55.1 jit_solution(4234256363177230856)
XLA Ops:
  1.3 0.0 copy-start.3
  1.3 0.0 copy-start.4
  1.3 0.6 %copy-done.3 = s32[1,48]{1,0:T(1,128)S(1)} copy-done((s32[1,48]{1,0:T(1,128)S(1)}, s32[1,48]{1,0:T(1,128)}, u32[]{:S(2)}) %copy-start.3) | copy-done | bytes 216
  1.9 0.0 copy-done.4
  1.9 0.0 copy-start
  2.0 1.1 %copy-done = f32[1,48,8,4,128]{4,3,2,1,0:T(4,128)S(1)} copy-done((f32[1,48,8,4,128]{4,3,2,1,0:T(4,128)S(1)}, f32[1,48,8,4,128]{4,3,2,1,0:T(4,128)}, u32[]{:S(2)}) %copy-start) | copy-done | bytes 786456
  3.1 0.0 copy-start.1
  3.1 0.0 copy-start.2
  3.1 0.6 %weigh.1.total_ref = f32[32,128]{1,0:T(8,128)S(1)} custom-call(s32[1,1]{1,0:T(1,128)S(6)} %copy.7.counts_ref, s32[1,48]{1,0:T(1,128)S(1)} %copy-done.3, f32[1,48]{1,0:T(1,128)S(1)} %copy-done.4, f32[48,32,128]{2,1,0:T(8,128)S(1)} %bitcast.5), custom_call_target="tpu_custom_call" | custom-call | tf_op jit(solution)/shard_map/weigh/pallas_call | solution.py:241
  3.7 0.5 collective-permute-start
  4.2 0.8 %collective-permute-done.other_ref = f32[32,128]{1,0:T(8,128)S(1)} collective-permute-done((f32[32,128]{1,0:T(8,128)S(1)}, f32[32,128]{1,0:T(8,128)S(1)}, u32[]{:S(2)}, u32[]{:S(2)}) %collective-permute-start) | collective-permute-done | bytes 16416 | tf_op jit(solution)/shard_map/ppermute | solution.py:218
  5.1 0.0 copy-done.1
  5.1 0.0 copy-done.2
  5.1 5.0 %collective-permute-start.1 = (f32[6,32,128]{2,1,0:T(8,128)S(1)}, f32[6,32,128]{2,1,0:T(8,128)S(1)}, u32[]{:S(2)}, u32[]{:S(2)}) collective-permute-start(f32[6,32,128]{2,1,0:T(8,128)S(1)} %get-tuple-element.23), channel_id=1, source_target_pairs={{0,12},{4,0},{8,4},{12,8},{1,13},{5,1},{9,5},{13,9},{2,14},{6,2},{... | collective-permute-start | bytes 294920 | tf_op jit(solution)/shard_map/ppermute | solution.py:234
  10.1 0.1 pack_two.1
  10.2 0.1 collective-permute-start.2
  10.3 1.0 %collective-permute-start.3 = (f32[6,32,128]{2,1,0:T(8,128)S(1)}, f32[6,32,128]{2,1,0:T(8,128)S(1)}, u32[]{:S(2)}, u32[]{:S(2)}) collective-permute-start(f32[6,32,128]{2,1,0:T(8,128)S(1)} %get-tuple-element.25), channel_id=1, source_target_pairs={{0,4},{4,8},{8,12},{12,0},{1,5},{5,9},{9,13},{13,1},{2,6},{6,10},{... | collective-permute-start | bytes 294920 | tf_op jit(solution)/shard_map/ppermute | solution.py:234
  11.3 2.9 %collective-permute-start.8 = (f32[8,32,128]{2,1,0:T(8,128)S(1)}, f32[8,32,128]{2,1,0:T(8,128)S(1)}, u32[]{:S(2)}, u32[]{:S(2)}) collective-permute-start(f32[8,32,128]{2,1,0:T(8,128)S(1)} %get-tuple-element.35), channel_id=1, source_target_pairs={{0,12},{4,0},{8,4},{12,8},{1,13},{5,1},{9,5},{13,9},{2,14},{6,2},{... | collective-permute-start | bytes 393224 | tf_op jit(solution)/shard_map/ppermute | solution.py:234
  14.2 1.1 %collective-permute-start.9 = (f32[8,32,128]{2,1,0:T(8,128)S(1)}, f32[8,32,128]{2,1,0:T(8,128)S(1)}, u32[]{:S(2)}, u32[]{:S(2)}) collective-permute-start(f32[8,32,128]{2,1,0:T(8,128)S(1)} %get-tuple-element.36), channel_id=1, source_target_pairs={{0,8},{4,12},{8,0},{12,4},{1,9},{5,13},{9,1},{13,5},{2,10},{6,14},... | collective-permute-start | bytes 393224 | tf_op jit(solution)/shard_map/ppermute | solution.py:234
  15.2 0.0 collective-permute-done.1.refs_1_
  15.2 0.0 collective-permute-start.10
  15.2 4.8 %collective-permute-done.2.refs_2_ = f32[6,32,128]{2,1,0:T(8,128)S(1)} collective-permute-done((f32[6,32,128]{2,1,0:T(8,128)S(1)}, f32[6,32,128]{2,1,0:T(8,128)S(1)}, u32[]{:S(2)}, u32[]{:S(2)}) %collective-permute-start.2) | collective-permute-done | bytes 98336 | tf_op jit(solution)/shard_map/ppermute | solution.py:234
  20.1 0.0 collective-permute-done.3.refs_3_
  20.1 1.6 %collective-permute-start.4 = (f32[4,32,128]{2,1,0:T(8,128)S(1)}, f32[4,32,128]{2,1,0:T(8,128)S(1)}, u32[]{:S(2)}, u32[]{:S(2)}) collective-permute-start(f32[4,32,128]{2,1,0:T(8,128)S(1)} %pad_maximum_fusion.1), channel_id=1, source_target_pairs={{0,2},{1,3},{2,0},{3,1},{4,6},{5,7},{6,4},{7,5},{8,10},{9,11},{10,... | collective-permute-start | bytes 196616 | tf_op jit(solution)/shard_map/ppermute | solution.py:218
  21.6 1.1 %early.1 = (f32[16,4,8,128]{3,2,1,0:T(8,128)S(1)}, f32[16,7,8,128]{3,2,1,0:T(8,128)S(1)}) custom-call(f32[6,32,128]{2,1,0:T(8,128)S(1)} %get-tuple-element.22.refs_0_.after_ref, f32[6,32,128]{2,1,0:T(8,128)S(1)} %collective-permute-done.1.refs_1_, f32[6,32,128]{2,1,0:T(8,128)S(1)} %collective-permute-done.2.refs_2_, ...), custom_call_target="tpu_custom_call" | custom-call | tf_op jit(solution)/shard_map/early/pallas_call | solution.py:272
  22.8 1.6 %collective-permute-done.4 = f32[4,32,128]{2,1,0:T(8,128)S(1)} collective-permute-done((f32[4,32,128]{2,1,0:T(8,128)S(1)}, f32[4,32,128]{2,1,0:T(8,128)S(1)}, u32[]{:S(2)}, u32[]{:S(2)}) %collective-permute-start.4) | collective-permute-done | bytes 65568 | tf_op jit(solution)/shard_map/ppermute | solution.py:218
  24.4 1.8 %dynamics.1 = (f32[16,7,8,128]{3,2,1,0:T(8,128)S(1)}, f32[32,128]{1,0:T(8,128)}) custom-call(f32[4,32,128]{2,1,0:T(8,128)S(1)} %pad_maximum_fusion.theta_pieces, f32[4,32,128]{2,1,0:T(8,128)S(1)} %fusion.total_in, f32[16,7,8,128]{3,2,1,0:T(8,128)S(1)} %get-tuple-element.26.coef_ref.refs_4_), custom_call_target="tpu_custom_call" | custom-call | tf_op jit(solution)/shard_map/dynamics/pallas_call | solution.py:281
  26.3 1.1 %late.1 = (f32[4,32,128]{2,1,0:T(8,128)S(1)}, f32[4,32,128]{2,1,0:T(8,128)S(1)}, f32[4,32,128]{2,1,0:T(8,128)S(1)}, f32[4,32,128]{2,1,0:T(8,128)S(1)}) custom-call(f32[16,4,8,128]{3,2,1,0:T(8,128)S(1)} %get-tuple-element.28.held_ref, f32[16,7,8,128]{3,2,1,0:T(8,128)S(1)} %get-tuple-element.29.coef_ref.refs_5_), custom_call_target="tpu_custom_call" | custom-call | tf_op jit(solution)/shard_map/late/pallas_call | solution.py:290
  27.3 6.0 %collective-permute-start.5 = (f32[4,32,128]{2,1,0:T(8,128)S(1)}, f32[4,32,128]{2,1,0:T(8,128)S(1)}, u32[]{:S(2)}, u32[]{:S(2)}) collective-permute-start(f32[4,32,128]{2,1,0:T(8,128)S(1)} %get-tuple-element.31), channel_id=1, source_target_pairs={{0,4},{4,8},{8,12},{12,0},{1,5},{5,9},{9,13},{13,1},{2,6},{6,10},{... | collective-permute-start | bytes 196616 | tf_op jit(solution)/shard_map/ppermute | solution.py:234
  33.3 0.0 collective-permute-done.8.refs_1_
  33.3 0.0 collective-permute-done.9.refs_2_
  33.3 0.0 collective-permute-done.10.refs_3_
  33.3 3.7 %both.1 = (f32[8,32,128]{2,1,0:T(8,128)S(1)}, f32[8,32,128]{2,1,0:T(8,128)S(1)}, f32[8,32,128]{2,1,0:T(8,128)S(1)}, f32[8,32,128]{2,1,0:T(8,128)S(1)}) custom-call(f32[8,32,128]{2,1,0:T(8,128)S(1)} %get-tuple-element.34.refs_0_, f32[8,32,128]{2,1,0:T(8,128)S(1)} %collective-permute-done.8.refs_1_, f32[8,32,128]{2,1,0:T(8,128)S(1)} %collective-permute-done.9.refs_2_, ...), custom_call_target="tpu_custom_call" | custom-call | tf_op jit(solution)/shard_map/both/pallas_call | solution.py:299
  37.1 2.5 %collective-permute-start.11 = (f32[8,32,128]{2,1,0:T(8,128)S(1)}, f32[8,32,128]{2,1,0:T(8,128)S(1)}, u32[]{:S(2)}, u32[]{:S(2)}) collective-permute-start(f32[8,32,128]{2,1,0:T(8,128)S(1)} %get-tuple-element.39), channel_id=1, source_target_pairs={{0,4},{4,8},{8,12},{12,0},{1,5},{5,9},{9,13},{13,1},{2,6},{6,10},{... | collective-permute-start | bytes 393224 | tf_op jit(solution)/shard_map/ppermute | solution.py:234
  39.6 0.0 collective-permute-start.12
  39.6 2.4 %collective-permute-start.13 = (f32[8,32,128]{2,1,0:T(8,128)S(1)}, f32[8,32,128]{2,1,0:T(8,128)S(1)}, u32[]{:S(2)}, u32[]{:S(2)}) collective-permute-start(f32[8,32,128]{2,1,0:T(8,128)S(1)} %get-tuple-element.41), channel_id=1, source_target_pairs={{0,12},{4,0},{8,4},{12,8},{1,13},{5,1},{9,5},{13,9},{2,14},{6,2},{... | collective-permute-start | bytes 393224 | tf_op jit(solution)/shard_map/ppermute | solution.py:234
  42.1 0.9 %collective-permute-start.6 = (f32[4,32,128]{2,1,0:T(8,128)S(1)}, f32[4,32,128]{2,1,0:T(8,128)S(1)}, u32[]{:S(2)}, u32[]{:S(2)}) collective-permute-start(f32[4,32,128]{2,1,0:T(8,128)S(1)} %get-tuple-element.32), channel_id=1, source_target_pairs={{0,8},{4,12},{8,0},{12,4},{1,9},{5,13},{9,1},{13,5},{2,10},{6,14},... | collective-permute-start | bytes 196616 | tf_op jit(solution)/shard_map/ppermute | solution.py:234
  43.0 0.0 collective-permute-done.5.refs_1_
  43.0 1.0 %collective-permute-start.7 = (f32[4,32,128]{2,1,0:T(8,128)S(1)}, f32[4,32,128]{2,1,0:T(8,128)S(1)}, u32[]{:S(2)}, u32[]{:S(2)}) collective-permute-start(f32[4,32,128]{2,1,0:T(8,128)S(1)} %get-tuple-element.33), channel_id=1, source_target_pairs={{0,12},{4,0},{8,4},{12,8},{1,13},{5,1},{9,5},{13,9},{2,14},{6,2},{... | collective-permute-start | bytes 196616 | tf_op jit(solution)/shard_map/ppermute | solution.py:234
  44.0 10.1 %collective-permute-done.6.refs_2_ = f32[4,32,128]{2,1,0:T(8,128)S(1)} collective-permute-done((f32[4,32,128]{2,1,0:T(8,128)S(1)}, f32[4,32,128]{2,1,0:T(8,128)S(1)}, u32[]{:S(2)}, u32[]{:S(2)}) %collective-permute-start.6) | collective-permute-done | bytes 65568 | tf_op jit(solution)/shard_map/ppermute | solution.py:234
  54.1 0.0 collective-permute-done.7.refs_3_
  54.1 0.0 collective-permute-done.11.refs_5_
  54.1 0.0 collective-permute-done.12.refs_6_
  54.2 0.0 collective-permute-done.13.refs_7_
  54.2 0.9 %assemble.1 = f32[48,32,128]{2,1,0:T(8,128)} custom-call(s32[1]{0:T(128)} %bitcast.me_ref, f32[4,32,128]{2,1,0:T(8,128)S(1)} %get-tuple-element.30.refs_0_, f32[4,32,128]{2,1,0:T(8,128)S(1)} %collective-permute-done.5.refs_1_, f32[4,32,128]{2,1,0:T(8,128)S(1)} %collective-permute-done.6.refs_2_, f32[4,32,128]{2,1,0:T(8,128)S(1)} %collective-permute-done.7.refs_3_, ...), custom_call_target="tpu_custom_call" | custom-call | tf_op jit(solution)/shard_map/assemble/pallas_call | solution.py:309
  (8 shorter events, 0.1 us)
Async XLA Ops:
  1.3 0.7 %copy-start.3 = (s32[1,48]{1,0:T(1,128)S(1)}, s32[1,48]{1,0:T(1,128)}, u32[]{:S(2)}) copy-start(s32[1,48]{1,0:T(1,128)} %flags_ref.1) | copy-start | bytes 580
  1.3 0.7 %copy-start.4 = (f32[1,48]{1,0:T(1,128)S(1)}, f32[1,48]{1,0:T(1,128)}, u32[]{:S(2)}) copy-start(f32[1,48]{1,0:T(1,128)} %kappa_ref.1) | copy-start | bytes 580
  1.9 1.1 %copy-start = (f32[1,48,8,4,128]{4,3,2,1,0:T(4,128)S(1)}, f32[1,48,8,4,128]{4,3,2,1,0:T(4,128)}, u32[]{:S(2)}) copy-start(f32[1,48,8,4,128]{4,3,2,1,0:T(4,128)} %param.6) | copy-start | bytes 2359300
  3.1 2.0 %copy-start.1 = (f32[1,48,8,4,128]{4,3,2,1,0:T(4,128)S(1)}, f32[1,48,8,4,128]{4,3,2,1,0:T(4,128)}, u32[]{:S(2)}) copy-start(f32[1,48,8,4,128]{4,3,2,1,0:T(4,128)} %param.6) | copy-start | bytes 2359300
  3.1 2.0 %copy-start.2 = (f32[8,4,128]{2,1,0:T(4,128)S(1)}, f32[8,4,128]{2,1,0:T(4,128)}, u32[]{:S(2)}) copy-start(f32[8,4,128]{2,1,0:T(4,128)} %param.5) | copy-start | bytes 49156
  3.7 1.4 %collective-permute-start = (f32[32,128]{1,0:T(8,128)S(1)}, f32[32,128]{1,0:T(8,128)S(1)}, u32[]{:S(2)}, u32[]{:S(2)}) collective-permute-start(f32[32,128]{1,0:T(8,128)S(1)} %weigh.1.total_ref), channel_id=1, source_target_pairs={{0,1},{1,0},{2,3},{3,2},{4,5},{5,4},{6,7},{7,6},{8,9},{9,8},{10,11... | collective-permute-start | bytes 49160 | tf_op jit(solution)/shard_map/ppermute | solution.py:218
  5.1 10.1 %collective-permute-start.1 = (f32[6,32,128]{2,1,0:T(8,128)S(1)}, f32[6,32,128]{2,1,0:T(8,128)S(1)}, u32[]{:S(2)}, u32[]{:S(2)}) collective-permute-start(f32[6,32,128]{2,1,0:T(8,128)S(1)} %get-tuple-element.23), channel_id=1, source_target_pairs={{0,12},{4,0},{8,4},{12,8},{1,13},{5,1},{9,5},{13,9},{2,14},{6,2},{... | collective-permute-start | bytes 294920 | tf_op jit(solution)/shard_map/ppermute | solution.py:234
  10.2 9.9 %collective-permute-start.2 = (f32[6,32,128]{2,1,0:T(8,128)S(1)}, f32[6,32,128]{2,1,0:T(8,128)S(1)}, u32[]{:S(2)}, u32[]{:S(2)}) collective-permute-start(f32[6,32,128]{2,1,0:T(8,128)S(1)} %get-tuple-element.24), channel_id=1, source_target_pairs={{0,8},{4,12},{8,0},{12,4},{1,9},{5,13},{9,1},{13,5},{2,10},{6,14},... | collective-permute-start | bytes 294920 | tf_op jit(solution)/shard_map/ppermute | solution.py:234
  10.3 9.8 %collective-permute-start.3 = (f32[6,32,128]{2,1,0:T(8,128)S(1)}, f32[6,32,128]{2,1,0:T(8,128)S(1)}, u32[]{:S(2)}, u32[]{:S(2)}) collective-permute-start(f32[6,32,128]{2,1,0:T(8,128)S(1)} %get-tuple-element.25), channel_id=1, source_target_pairs={{0,4},{4,8},{8,12},{12,0},{1,5},{5,9},{9,13},{13,1},{2,6},{6,10},{... | collective-permute-start | bytes 294920 | tf_op jit(solution)/shard_map/ppermute | solution.py:234
  11.3 22.1 %collective-permute-start.8 = (f32[8,32,128]{2,1,0:T(8,128)S(1)}, f32[8,32,128]{2,1,0:T(8,128)S(1)}, u32[]{:S(2)}, u32[]{:S(2)}) collective-permute-start(f32[8,32,128]{2,1,0:T(8,128)S(1)} %get-tuple-element.35), channel_id=1, source_target_pairs={{0,12},{4,0},{8,4},{12,8},{1,13},{5,1},{9,5},{13,9},{2,14},{6,2},{... | collective-permute-start | bytes 393224 | tf_op jit(solution)/shard_map/ppermute | solution.py:234
  14.2 19.2 %collective-permute-start.9 = (f32[8,32,128]{2,1,0:T(8,128)S(1)}, f32[8,32,128]{2,1,0:T(8,128)S(1)}, u32[]{:S(2)}, u32[]{:S(2)}) collective-permute-start(f32[8,32,128]{2,1,0:T(8,128)S(1)} %get-tuple-element.36), channel_id=1, source_target_pairs={{0,8},{4,12},{8,0},{12,4},{1,9},{5,13},{9,1},{13,5},{2,10},{6,14},... | collective-permute-start | bytes 393224 | tf_op jit(solution)/shard_map/ppermute | solution.py:234
  15.2 18.1 %collective-permute-start.10 = (f32[8,32,128]{2,1,0:T(8,128)S(1)}, f32[8,32,128]{2,1,0:T(8,128)S(1)}, u32[]{:S(2)}, u32[]{:S(2)}) collective-permute-start(f32[8,32,128]{2,1,0:T(8,128)S(1)} %get-tuple-element.37), channel_id=1, source_target_pairs={{0,4},{4,8},{8,12},{12,0},{1,5},{5,9},{9,13},{13,1},{2,6},{6,10},{... | collective-permute-start | bytes 393224 | tf_op jit(solution)/shard_map/ppermute | solution.py:234
  20.1 4.3 %collective-permute-start.4 = (f32[4,32,128]{2,1,0:T(8,128)S(1)}, f32[4,32,128]{2,1,0:T(8,128)S(1)}, u32[]{:S(2)}, u32[]{:S(2)}) collective-permute-start(f32[4,32,128]{2,1,0:T(8,128)S(1)} %pad_maximum_fusion.1), channel_id=1, source_target_pairs={{0,2},{1,3},{2,0},{3,1},{4,6},{5,7},{6,4},{7,5},{8,10},{9,11},{10,... | collective-permute-start | bytes 196616 | tf_op jit(solution)/shard_map/ppermute | solution.py:218
  27.3 15.7 %collective-permute-start.5 = (f32[4,32,128]{2,1,0:T(8,128)S(1)}, f32[4,32,128]{2,1,0:T(8,128)S(1)}, u32[]{:S(2)}, u32[]{:S(2)}) collective-permute-start(f32[4,32,128]{2,1,0:T(8,128)S(1)} %get-tuple-element.31), channel_id=1, source_target_pairs={{0,4},{4,8},{8,12},{12,0},{1,5},{5,9},{9,13},{13,1},{2,6},{6,10},{... | collective-permute-start | bytes 196616 | tf_op jit(solution)/shard_map/ppermute | solution.py:234
  37.1 17.1 %collective-permute-start.11 = (f32[8,32,128]{2,1,0:T(8,128)S(1)}, f32[8,32,128]{2,1,0:T(8,128)S(1)}, u32[]{:S(2)}, u32[]{:S(2)}) collective-permute-start(f32[8,32,128]{2,1,0:T(8,128)S(1)} %get-tuple-element.39), channel_id=1, source_target_pairs={{0,4},{4,8},{8,12},{12,0},{1,5},{5,9},{9,13},{13,1},{2,6},{6,10},{... | collective-permute-start | bytes 393224 | tf_op jit(solution)/shard_map/ppermute | solution.py:234
  39.6 14.5 %collective-permute-start.12 = (f32[8,32,128]{2,1,0:T(8,128)S(1)}, f32[8,32,128]{2,1,0:T(8,128)S(1)}, u32[]{:S(2)}, u32[]{:S(2)}) collective-permute-start(f32[8,32,128]{2,1,0:T(8,128)S(1)} %get-tuple-element.40), channel_id=1, source_target_pairs={{0,8},{4,12},{8,0},{12,4},{1,9},{5,13},{9,1},{13,5},{2,10},{6,14},... | collective-permute-start | bytes 393224 | tf_op jit(solution)/shard_map/ppermute | solution.py:234
  39.6 14.5 %collective-permute-start.13 = (f32[8,32,128]{2,1,0:T(8,128)S(1)}, f32[8,32,128]{2,1,0:T(8,128)S(1)}, u32[]{:S(2)}, u32[]{:S(2)}) collective-permute-start(f32[8,32,128]{2,1,0:T(8,128)S(1)} %get-tuple-element.41), channel_id=1, source_target_pairs={{0,12},{4,0},{8,4},{12,8},{1,13},{5,1},{9,5},{13,9},{2,14},{6,2},{... | collective-permute-start | bytes 393224 | tf_op jit(solution)/shard_map/ppermute | solution.py:234
  42.1 12.1 %collective-permute-start.6 = (f32[4,32,128]{2,1,0:T(8,128)S(1)}, f32[4,32,128]{2,1,0:T(8,128)S(1)}, u32[]{:S(2)}, u32[]{:S(2)}) collective-permute-start(f32[4,32,128]{2,1,0:T(8,128)S(1)} %get-tuple-element.32), channel_id=1, source_target_pairs={{0,8},{4,12},{8,0},{12,4},{1,9},{5,13},{9,1},{13,5},{2,10},{6,14},... | collective-permute-start | bytes 196616 | tf_op jit(solution)/shard_map/ppermute | solution.py:234
  43.0 11.2 %collective-permute-start.7 = (f32[4,32,128]{2,1,0:T(8,128)S(1)}, f32[4,32,128]{2,1,0:T(8,128)S(1)}, u32[]{:S(2)}, u32[]{:S(2)}) collective-permute-start(f32[4,32,128]{2,1,0:T(8,128)S(1)} %get-tuple-element.33), channel_id=1, source_target_pairs={{0,12},{4,0},{8,4},{12,8},{1,13},{5,1},{9,5},{13,9},{2,14},{6,2},{... | collective-permute-start | bytes 196616 | tf_op jit(solution)/shard_map/ppermute | solution.py:234

commit v5 on v3

--- a/solution.py
+++ b/solution.py
@@ -44,13 +44,6 @@
             slot = block + i
             safe = jnp.minimum(slot, slots - 1)
             outs[step][i] = tracers_ref[safe] * jnp.where(slot < count, 1.0, 0.0)
-
-
-def pack_one(tiles, share, part, slots, me_ref, counts_ref, tracers_ref, theta_ref, total_ref, other_ref, *outs):
-    sort_slots(tiles, share, 0, part, slots, me_ref, counts_ref, tracers_ref, outs)
-    for out in outs:
-        out[part] = theta_ref[...]
-        out[part + 1] = total_ref[...] + other_ref[...]
 
 
 def pack_two(tiles, share, first, part, slots, me_ref, counts_ref, tracers_ref, after_ref, *outs):
@@ -141,53 +134,25 @@
                 out[i, pl.ds(row, nz, stride=rows), :] = state_ref[step * rows + row, i] * (SCALE * SCALE)
 
 
-def early(tiles, part, rows, nz, *refs):
-    pieces, (state_ref, coef_ref, theta_ref, first_ref) = refs[:tiles], refs[tiles:]
-    for step in range(tiles):
-        for row in range(rows):
-            theta_ref[step * rows + row] = unpack(pieces[step], part, rows, nz, row)
-    load(pieces, part, rows, nz, state_ref)
-    coefficients(theta_ref, coef_ref, tiles * rows)
-    advance(coef_ref, state_ref, first_ref, tiles * rows, part)
-
-
-def dynamics(tiles, rows, nz, theta_in, total_in, coef_ref, coef_out, theta_out, state_ref, first_ref):
+def dynamics(tiles, rows, nz, *refs):
+    pieces, (coef_ref, next_ref, theta_out, theta_ref, state_ref, first_ref) = refs[:tiles], refs[tiles:]
     length = tiles * rows
     for step in range(tiles):
         for row in range(rows):
-            state_ref[step * rows + row, 0] = unpack(total_in, step, rows, nz, row)
+            theta_ref[step * rows + row] = unpack(pieces[step], 0, rows, nz, row)
+            state_ref[step * rows + row, 0] = unpack(pieces[step], 1, rows, nz, row)
+    coefficients(theta_ref, coef_ref, length)
     advance(coef_ref, state_ref, first_ref, length, 1)
 
     def heat(x, carry):
-        theta_in[x] = theta_in[x] + (heat_step * SCALE) * state_ref[x, 0]
+        theta_ref[x] = theta_ref[x] + (heat_step * SCALE) * state_ref[x, 0]
         return carry
 
     lax.fori_loop(0, length, heat, 0, unroll=UNROLL)
-    coefficients(theta_in, coef_out, length)
-    advance(coef_out, state_ref, first_ref, length, 1)
+    coefficients(theta_ref, next_ref, length)
+    advance(next_ref, state_ref, first_ref, length, 1)
     for row in range(rows):
-        theta_out[pl.ds(row, nz, stride=rows), :] = theta_in[row] + (heat_step * SCALE * SCALE) * state_ref[row, 0]
-
-
-def dynamics_call(tiles, rows, nz, theta_pieces, total_in, coef_ref, coef_out, theta_out, state_ref, first_ref, theta_ref):
-    for step in range(tiles):
-        for row in range(rows):
-            theta_ref[step * rows + row] = unpack(theta_pieces, step, rows, nz, row)
-    dynamics(tiles, rows, nz, theta_ref, total_in, coef_ref, coef_out, theta_out, state_ref, first_ref)
-
-
-def late(tiles, part, rows, nz, held_ref, coef_ref, *refs):
-    outs, (state_ref, first_ref) = refs[:tiles], refs[tiles:]
-    length = tiles * rows
-
-    def copy(x, carry):
-        for i in range(part):
-            state_ref[x, i] = held_ref[x, i]
-        return carry
-
-    lax.fori_loop(0, length, copy, 0, unroll=UNROLL)
-    advance(coef_ref, state_ref, first_ref, length, part)
-    store(outs, part, rows, nz, state_ref)
+        theta_out[pl.ds(row, nz, stride=rows), :] = theta_ref[row] + (heat_step * SCALE * SCALE) * state_ref[row, 0]
 
 
 def both(tiles, part, rows, nz, *refs):
@@ -246,65 +211,49 @@
         compiler_params=params(),
         name="weigh",
     )(counts, flags, kappa, tracers)
-    one = gather(pl.pallas_call(
-        functools.partial(pack_one, tiles, share, parts[0], slots),
-        out_shape=[field(parts[0] + 2, *flat)] * tiles,
-        in_specs=[SMEM, SMEM] + [VMEM] * 4,
-        out_specs=[VMEM] * tiles,
-        compiler_params=params(),
-        name="pack_one",
-    )(me, counts, tracers, theta, total, swap(total, "group", 1)))
-    two = gather(pl.pallas_call(
-        functools.partial(pack_two, tiles, share, parts[0], parts[1], slots),
-        out_shape=[field(parts[1], *flat)] * tiles,
-        in_specs=[SMEM, SMEM, VMEM, HBM],
-        out_specs=[VMEM] * tiles,
-        compiler_params=params(),
-        name="pack_two",
-    )(me, counts, tracers, one[0]))
-    total = jnp.stack([piece[parts[0] + 1] for piece in one])
-    hop = 2
+    hop = 1
     while hop < lax.axis_size("group"):
         total = total + swap(total, "group", hop)
         hop *= 2
-    grid_theta = jnp.stack([piece[parts[0]] for piece in one])
-
-    held, coef = pl.pallas_call(
-        functools.partial(early, tiles, parts[0], rows, nz),
-        out_shape=[field(length, parts[0], nz, ny), field(length, 7, nz, ny)],
+    small = jnp.stack([theta, total])
+    small = [small] + [shift(small, tiles - step) for step in range(1, tiles)]
+
+    def pack(before, part, after):
+        return pl.pallas_call(
+            functools.partial(pack_two, tiles, share, before, part, slots),
+            out_shape=[field(part, *flat)] * tiles,
+            in_specs=[SMEM, SMEM, VMEM, HBM],
+            out_specs=[VMEM] * tiles,
+            compiler_params=params(),
+            name="pack",
+        )(me, counts, tracers, after)
+
+    payload = pack(0, parts[0], me)
+    one = gather(payload)
+    two = gather(pack(parts[0], parts[1], payload[0]))
+    coef, next_coef, theta_new = pl.pallas_call(
+        functools.partial(dynamics, tiles, rows, nz),
+        out_shape=[field(length, 7, nz, ny), field(length, 7, nz, ny), field(*flat)],
         in_specs=[VMEM] * tiles,
-        out_specs=[VMEM] * 2,
-        scratch_shapes=[scratch(length, nz, ny), scratch(length, parts[0], nz, ny)],
-        compiler_params=params(),
-        name="early",
-    )(*one)
-    next_coef, theta_new = pl.pallas_call(
-        functools.partial(dynamics_call, tiles, rows, nz),
-        out_shape=[field(length, 7, nz, ny), field(*flat)],
-        in_specs=[VMEM] * 3,
-        out_specs=[VMEM] * 2,
-        scratch_shapes=[scratch(length, 1, nz, ny), scratch(length, 1, nz, ny), scratch(length, nz, ny)],
+        out_specs=[VMEM] * 3,
+        scratch_shapes=[scratch(length, nz, ny), scratch(length, 1, nz, ny), scratch(length, 1, nz, ny)],
         compiler_params=params(),
         name="dynamics",
-    )(grid_theta, total, coef)
-    done_one = pl.pallas_call(
-        functools.partial(late, tiles, parts[0], rows, nz),
-        out_shape=[field(parts[0], *flat)] * tiles,
-        in_specs=[VMEM] * 2,
-        out_specs=[VMEM] * tiles,
-        scratch_shapes=[scratch(length, parts[0], nz, ny)] * 2,
-        compiler_params=params(),
-        name="late",
-    )(held, next_coef)
-    done_two = pl.pallas_call(
-        functools.partial(both, tiles, parts[1], rows, nz),
-        out_shape=[field(parts[1], *flat)] * tiles,
-        in_specs=[VMEM] * (tiles + 2),
-        out_specs=[VMEM] * tiles,
-        scratch_shapes=[scratch(length, parts[1], nz, ny)] * 2,
-        compiler_params=params(),
-        name="both",
-    )(*two, coef, next_coef)
+    )(*small)
+
+    def work(pieces, part):
+        return pl.pallas_call(
+            functools.partial(both, tiles, part, rows, nz),
+            out_shape=[field(part, *flat)] * tiles,
+            in_specs=[VMEM] * (tiles + 2),
+            out_specs=[VMEM] * tiles,
+            scratch_shapes=[scratch(length, part, nz, ny)] * 2,
+            compiler_params=params(),
+            name="both",
+        )(*pieces, coef, next_coef)
+
+    done_one = work(one, parts[0])
+    done_two = work(two, parts[1])
     back = [piece for done in (done_one, done_two) for piece in [done[0]] + [shift(done[step], step) for step in range(1, tiles)]]
     out = pl.pallas_call(
         functools.partial(assemble, tiles, parts),

time: 52.7 us -> 51.7 us (0.981)
  starting transfers between devices: 30.9 us -> 29.6 us
    ppermute x12 -> x15, starting transfers between devices: 28.8 us -> 26.2 us  [shift(): lax.ppermute(value, 'tile', [(i, (i + step) % tiles) for i in range(tiles)])]
    ppermute x12 -> x15, waiting for transfers between devices: 6.97 us -> 8.49 us  [shift(): lax.ppermute(value, 'tile', [(i, (i + step) % tiles) for i in range(tiles)])]
    ppermute x2, starting transfers between devices: 2.07 us -> 3.35 us  [swap(): lax.ppermute(value, axis, [(i, i ^ hop) for i in range(lax.axis_size(axis...]
    ppermute x2, waiting for transfers between devices: 2.04 us -> 0.84 us  [swap(): lax.ppermute(value, axis, [(i, i ^ hop) for i in range(lax.axis_size(axis...]
    pallas_call x6 -> x5, Pallas kernels: 7.87 us -> 7.82 us  [the longest x2 5.8 us: work(): pl.pallas_call(functools.partial(both, tiles, part, rows, nz), out_shape=...]
  transfers between devices with their start and end apart: 14 -> 17, of which waited for: 6 -> 5; matrix products, arithmetic and copies ran while one was open for 0% -> 0% of each run, Pallas kernels for 15% -> 15%
where the time goes in v5:
time: 51.7 us; the launch traced here: 51.5 us
  starting transfers between devices  29.6 us (57%)
  Pallas kernels  9.39 us (18%)
  waiting for transfers between devices  9.33 us (18%)
  local copies, waits for them, and re-layouts  1.8 us (3%)
  between operations  1.38 us (3%)
    ppermute x15, starting transfers between devices, shift(): lax.ppermute(value, 'tile', [(i, (i + step) % tiles) for i in range(tiles)])  26.2 us
    ppermute x15, waiting for transfers between devices, shift(): lax.ppermute(value, 'tile', [(i, (i + step) % tiles) for i in range(tiles)])  8.49 us
    pallas_call x2, Pallas kernels, work(): pl.pallas_call(functools.partial(both, tiles, part, rows, nz), out_shape=...  5.8 us
    ppermute x2, starting transfers between devices, swap(): lax.ppermute(value, axis, [(i, i ^ hop) for i in range(lax.axis_size(axis...  3.35 us
    pallas_call x1, Pallas kernels, per_device(): pl.pallas_call(functools.partial(dynamics, tiles, rows, nz), out_shape=[f...  1.93 us
    unnamed x10, local copies, waits for them, and re-layouts  1.8 us
  transfers between devices with their start and end apart: 17, of which 5 were waited for; matrix products, arithmetic and copies ran while one was open for 0% of the time, Pallas kernels for 15%

profile of v5, /device:TPU:0, one launch (start us, length us, event | category | flops | bytes accessed | tf_op | source)
XLA Modules:
  0.0 51.5 jit_solution(18359906676017891440)
XLA Ops:
  1.3 0.0 copy-start.2
  1.3 0.0 copy-start.3
  1.3 0.6 %copy-done.2 = s32[1,48]{1,0:T(1,128)S(1)} copy-done((s32[1,48]{1,0:T(1,128)S(1)}, s32[1,48]{1,0:T(1,128)}, u32[]{:S(2)}) %copy-start.2) | copy-done | bytes 216
  1.9 0.0 copy-done.3
  1.9 0.0 copy-start
  2.0 1.1 %copy-done = f32[1,48,8,4,128]{4,3,2,1,0:T(4,128)S(1)} copy-done((f32[1,48,8,4,128]{4,3,2,1,0:T(4,128)S(1)}, f32[1,48,8,4,128]{4,3,2,1,0:T(4,128)}, u32[]{:S(2)}) %copy-start) | copy-done | bytes 786456
  3.1 0.0 copy-start.1
  3.1 0.6 %weigh.1 = f32[32,128]{1,0:T(8,128)S(1)} custom-call(s32[1,1]{1,0:T(1,128)S(6)} %copy.7.counts_ref, s32[1,48]{1,0:T(1,128)S(1)} %copy-done.2, f32[1,48]{1,0:T(1,128)S(1)} %copy-done.3, f32[48,32,128]{2,1,0:T(8,128)S(1)} %bitcast.7), custom_call_target="tpu_custom_call" | custom-call | tf_op jit(solution)/shard_map/weigh/pallas_call | solution.py:206
  3.7 0.5 %collective-permute-start = (f32[32,128]{1,0:T(8,128)S(1)}, f32[32,128]{1,0:T(8,128)S(1)}, u32[]{:S(2)}, u32[]{:S(2)}) collective-permute-start(f32[32,128]{1,0:T(8,128)S(1)} %weigh.1), channel_id=1, source_target_pairs={{0,1},{1,0},{2,3},{3,2},{4,5},{5,4},{6,7},{7,6},{8,9},{9,8},{10,11... | collective-permute-start | bytes 49160 | tf_op jit(solution)/shard_map/ppermute | solution.py:183
  4.2 0.8 %collective-permute-done = f32[32,128]{1,0:T(8,128)S(1)} collective-permute-done((f32[32,128]{1,0:T(8,128)S(1)}, f32[32,128]{1,0:T(8,128)S(1)}, u32[]{:S(2)}, u32[]{:S(2)}) %collective-permute-start) | collective-permute-done | bytes 16416 | tf_op jit(solution)/shard_map/ppermute | solution.py:183
  5.1 2.8 %collective-permute-start.1 = (f32[32,128]{1,0:T(8,128)S(1)}, f32[32,128]{1,0:T(8,128)S(1)}, u32[]{:S(2)}, u32[]{:S(2)}) collective-permute-start(f32[32,128]{1,0:T(8,128)S(1)} %add.6), channel_id=1, source_target_pairs={{0,2},{1,3},{2,0},{3,1},{4,6},{5,7},{6,4},{7,5},{8,10},{9,11},{10,... | collective-permute-start | bytes 49160 | tf_op jit(solution)/shard_map/ppermute | solution.py:183
  7.9 0.0 copy-done.1
  8.0 3.7 %collective-permute-start.5 = (f32[6,32,128]{2,1,0:T(8,128)S(1)}, f32[6,32,128]{2,1,0:T(8,128)S(1)}, u32[]{:S(2)}, u32[]{:S(2)}) collective-permute-start(f32[6,32,128]{2,1,0:T(8,128)S(1)} %get-tuple-element.23), channel_id=1, source_target_pairs={{0,12},{4,0},{8,4},{12,8},{1,13},{5,1},{9,5},{13,9},{2,14},{6,2},{... | collective-permute-start | bytes 294920 | tf_op jit(solution)/shard_map/ppermute | solution.py:199
  11.6 0.0 collective-permute-start.6
  11.6 0.0 copy-start.4
  11.6 1.0 %collective-permute-start.7 = (f32[6,32,128]{2,1,0:T(8,128)S(1)}, f32[6,32,128]{2,1,0:T(8,128)S(1)}, u32[]{:S(2)}, u32[]{:S(2)}) collective-permute-start(f32[6,32,128]{2,1,0:T(8,128)S(1)} %get-tuple-element.25), channel_id=1, source_target_pairs={{0,4},{4,8},{8,12},{12,0},{1,5},{5,9},{9,13},{13,1},{2,6},{6,10},{... | collective-permute-start | bytes 294920 | tf_op jit(solution)/shard_map/ppermute | solution.py:199
  12.6 0.0 collective-permute-done.1
  12.7 0.0 copy-done.4
  12.7 2.9 %collective-permute-start.2 = (f32[2,32,128]{2,1,0:T(8,128)S(1)}, f32[2,32,128]{2,1,0:T(8,128)S(1)}, u32[]{:S(2)}, u32[]{:S(2)}) collective-permute-start(f32[2,32,128]{2,1,0:T(8,128)S(1)} %pad_maximum_fusion.refs_0_), channel_id=1, source_target_pairs={{0,12},{4,0},{8,4},{12,8},{1,13},{5,1},{9,5},{13,9},{2,14},{6,2},{... | collective-permute-start | bytes 98312 | tf_op jit(solution)/shard_map/ppermute | solution.py:199
  15.5 1.1 %collective-permute-start.3 = (f32[2,32,128]{2,1,0:T(8,128)S(1)}, f32[2,32,128]{2,1,0:T(8,128)S(1)}, u32[]{:S(2)}, u32[]{:S(2)}) collective-permute-start(f32[2,32,128]{2,1,0:T(8,128)S(1)} %pad_maximum_fusion.refs_0_), channel_id=1, source_target_pairs={{0,8},{4,12},{8,0},{12,4},{1,9},{5,13},{9,1},{13,5},{2,10},{6,14},... | collective-permute-start | bytes 98312 | tf_op jit(solution)/shard_map/ppermute | solution.py:199
  16.7 2.4 %collective-permute-done.2.refs_1_ = f32[2,32,128]{2,1,0:T(8,128)S(1)} collective-permute-done((f32[2,32,128]{2,1,0:T(8,128)S(1)}, f32[2,32,128]{2,1,0:T(8,128)S(1)}, u32[]{:S(2)}, u32[]{:S(2)}) %collective-permute-start.2) | collective-permute-done | bytes 32800 | tf_op jit(solution)/shard_map/ppermute | solution.py:199
  19.0 3.7 %collective-permute-start.4 = (f32[2,32,128]{2,1,0:T(8,128)S(1)}, f32[2,32,128]{2,1,0:T(8,128)S(1)}, u32[]{:S(2)}, u32[]{:S(2)}) collective-permute-start(f32[2,32,128]{2,1,0:T(8,128)S(1)} %pad_maximum_fusion.refs_0_), channel_id=1, source_target_pairs={{0,4},{4,8},{8,12},{12,0},{1,5},{5,9},{9,13},{13,1},{2,6},{6,10},{... | collective-permute-start | bytes 98312 | tf_op jit(solution)/shard_map/ppermute | solution.py:199
  22.8 0.0 collective-permute-done.3.refs_2_
  22.8 3.2 %collective-permute-start.11 = (f32[6,32,128]{2,1,0:T(8,128)S(1)}, f32[6,32,128]{2,1,0:T(8,128)S(1)}, u32[]{:S(2)}, u32[]{:S(2)}) collective-permute-start(f32[6,32,128]{2,1,0:T(8,128)S(1)} %get-tuple-element.33), channel_id=1, source_target_pairs={{0,12},{4,0},{8,4},{12,8},{1,13},{5,1},{9,5},{13,9},{2,14},{6,2},{... | collective-permute-start | bytes 294920 | tf_op jit(solution)/shard_map/ppermute | solution.py:199
  26.1 0.0 collective-permute-done.4.refs_3_
  26.1 0.1 collective-permute-start.12
  26.1 1.9 %dynamics.1 = (f32[16,7,8,128]{3,2,1,0:T(8,128)S(1)}, f32[16,7,8,128]{3,2,1,0:T(8,128)S(1)}, f32[32,128]{1,0:T(8,128)}) custom-call(f32[2,32,128]{2,1,0:T(8,128)S(1)} %pad_maximum_fusion.refs_0_, f32[2,32,128]{2,1,0:T(8,128)S(1)} %collective-permute-done.2.refs_1_, f32[2,32,128]{2,1,0:T(8,128)S(1)} %collective-permute-done.3.refs_2_, ...), custom_call_target="tpu_custom_call" | custom-call | tf_op jit(solution)/shard_map/dynamics/pallas_call | solution.py:234
  28.1 0.0 collective-permute-done.5.refs_1_
  28.1 1.7 %collective-permute-start.13 = (f32[6,32,128]{2,1,0:T(8,128)S(1)}, f32[6,32,128]{2,1,0:T(8,128)S(1)}, u32[]{:S(2)}, u32[]{:S(2)}) collective-permute-start(f32[6,32,128]{2,1,0:T(8,128)S(1)} %get-tuple-element.35), channel_id=1, source_target_pairs={{0,4},{4,8},{8,12},{12,0},{1,5},{5,9},{9,13},{13,1},{2,6},{6,10},{... | collective-permute-start | bytes 294920 | tf_op jit(solution)/shard_map/ppermute | solution.py:199
  29.7 0.0 collective-permute-done.6.refs_2_
  29.7 0.0 collective-permute-done.7.refs_3_
  29.7 2.9 %both.2 = (f32[6,32,128]{2,1,0:T(8,128)S(1)}, f32[6,32,128]{2,1,0:T(8,128)S(1)}, f32[6,32,128]{2,1,0:T(8,128)S(1)}, f32[6,32,128]{2,1,0:T(8,128)S(1)}) custom-call(f32[6,32,128]{2,1,0:T(8,128)S(1)} %get-tuple-element.22.refs_0_.after_ref, f32[6,32,128]{2,1,0:T(8,128)S(1)} %collective-permute-done.5.refs_1_, ...), custom_call_target="tpu_custom_call" | custom-call | tf_op jit(solution)/shard_map/both/pallas_call | solution.py:245
  32.6 1.8 %collective-permute-start.8 = (f32[6,32,128]{2,1,0:T(8,128)S(1)}, f32[6,32,128]{2,1,0:T(8,128)S(1)}, u32[]{:S(2)}, u32[]{:S(2)}) collective-permute-start(f32[6,32,128]{2,1,0:T(8,128)S(1)} %get-tuple-element.29), channel_id=1, source_target_pairs={{0,4},{4,8},{8,12},{12,0},{1,5},{5,9},{9,13},{13,1},{2,6},{6,10},{... | collective-permute-start | bytes 294920 | tf_op jit(solution)/shard_map/ppermute | solution.py:199
  34.5 1.0 %collective-permute-start.9 = (f32[6,32,128]{2,1,0:T(8,128)S(1)}, f32[6,32,128]{2,1,0:T(8,128)S(1)}, u32[]{:S(2)}, u32[]{:S(2)}) collective-permute-start(f32[6,32,128]{2,1,0:T(8,128)S(1)} %get-tuple-element.30), channel_id=1, source_target_pairs={{0,8},{4,12},{8,0},{12,4},{1,9},{5,13},{9,1},{13,5},{2,10},{6,14},... | collective-permute-start | bytes 294920 | tf_op jit(solution)/shard_map/ppermute | solution.py:199
  35.4 0.0 collective-permute-done.11.refs_1_
  35.4 2.0 %collective-permute-start.10 = (f32[6,32,128]{2,1,0:T(8,128)S(1)}, f32[6,32,128]{2,1,0:T(8,128)S(1)}, u32[]{:S(2)}, u32[]{:S(2)}) collective-permute-start(f32[6,32,128]{2,1,0:T(8,128)S(1)} %get-tuple-element.31), channel_id=1, source_target_pairs={{0,12},{4,0},{8,4},{12,8},{1,13},{5,1},{9,5},{13,9},{2,14},{6,2},{... | collective-permute-start | bytes 294920 | tf_op jit(solution)/shard_map/ppermute | solution.py:199
  37.4 0.0 collective-permute-done.12.refs_2_
  37.4 0.0 collective-permute-done.13.refs_3_
  37.4 2.9 %both.3 = (f32[6,32,128]{2,1,0:T(8,128)S(1)}, f32[6,32,128]{2,1,0:T(8,128)S(1)}, f32[6,32,128]{2,1,0:T(8,128)S(1)}, f32[6,32,128]{2,1,0:T(8,128)S(1)}) custom-call(f32[6,32,128]{2,1,0:T(8,128)S(1)} %get-tuple-element.32.refs_0_, f32[6,32,128]{2,1,0:T(8,128)S(1)} %collective-permute-done.11.refs_1_, f32[6,32,128]{2,1,0:T(8,128)S(1)} %collective-permute-done.12.refs_2_, ...), custom_call_target="tpu_custom_call" | custom-call | tf_op jit(solution)/shard_map/both/pallas_call | solution.py:245
  40.4 0.1 collective-permute-start.14
  40.4 2.0 %collective-permute-start.15 = (f32[6,32,128]{2,1,0:T(8,128)S(1)}, f32[6,32,128]{2,1,0:T(8,128)S(1)}, u32[]{:S(2)}, u32[]{:S(2)}) collective-permute-start(f32[6,32,128]{2,1,0:T(8,128)S(1)} %get-tuple-element.38), channel_id=1, source_target_pairs={{0,8},{4,12},{8,0},{12,4},{1,9},{5,13},{9,1},{13,5},{2,10},{6,14},... | collective-permute-start | bytes 294920 | tf_op jit(solution)/shard_map/ppermute | solution.py:199
  42.4 0.0 collective-permute-done.8.refs_1_
  42.4 2.1 %collective-permute-start.16 = (f32[6,32,128]{2,1,0:T(8,128)S(1)}, f32[6,32,128]{2,1,0:T(8,128)S(1)}, u32[]{:S(2)}, u32[]{:S(2)}) collective-permute-start(f32[6,32,128]{2,1,0:T(8,128)S(1)} %get-tuple-element.39), channel_id=1, source_target_pairs={{0,12},{4,0},{8,4},{12,8},{1,13},{5,1},{9,5},{13,9},{2,14},{6,2},{... | collective-permute-start | bytes 294920 | tf_op jit(solution)/shard_map/ppermute | solution.py:199
  44.5 0.1 collective-permute-done.9.refs_2_
  44.5 0.0 collective-permute-done.10.refs_3_
  44.6 2.4 %collective-permute-done.14.refs_5_ = f32[6,32,128]{2,1,0:T(8,128)S(1)} collective-permute-done((f32[6,32,128]{2,1,0:T(8,128)S(1)}, f32[6,32,128]{2,1,0:T(8,128)S(1)}, u32[]{:S(2)}, u32[]{:S(2)}) %collective-permute-start.14) | collective-permute-done | bytes 98336 | tf_op jit(solution)/shard_map/ppermute | solution.py:199
  47.0 3.5 %collective-permute-done.15.refs_6_ = f32[6,32,128]{2,1,0:T(8,128)S(1)} collective-permute-done((f32[6,32,128]{2,1,0:T(8,128)S(1)}, f32[6,32,128]{2,1,0:T(8,128)S(1)}, u32[]{:S(2)}, u32[]{:S(2)}) %collective-permute-start.15) | collective-permute-done | bytes 98336 | tf_op jit(solution)/shard_map/ppermute | solution.py:199
  50.5 0.0 collective-permute-done.16.refs_7_
  50.5 0.9 %assemble.1 = f32[48,32,128]{2,1,0:T(8,128)} custom-call(s32[1]{0:T(128)} %bitcast.4.me_ref.after_ref, f32[6,32,128]{2,1,0:T(8,128)S(1)} %get-tuple-element.28.refs_0_, f32[6,32,128]{2,1,0:T(8,128)S(1)} %collective-permute-done.8.refs_1_, f32[6,32,128]{2,1,0:T(8,128)S(1)} %collective-permute-done.9.refs_2_, ...), custom_call_target="tpu_custom_call" | custom-call | tf_op jit(solution)/shard_map/assemble/pallas_call | solution.py:258
  (5 shorter events, 0.1 us)
Async XLA Ops:
  1.3 0.7 %copy-start.2 = (s32[1,48]{1,0:T(1,128)S(1)}, s32[1,48]{1,0:T(1,128)}, u32[]{:S(2)}) copy-start(s32[1,48]{1,0:T(1,128)} %flags_ref.1) | copy-start | bytes 580
  1.3 0.7 %copy-start.3 = (f32[1,48]{1,0:T(1,128)S(1)}, f32[1,48]{1,0:T(1,128)}, u32[]{:S(2)}) copy-start(f32[1,48]{1,0:T(1,128)} %kappa_ref.1) | copy-start | bytes 580
  1.9 1.1 %copy-start = (f32[1,48,8,4,128]{4,3,2,1,0:T(4,128)S(1)}, f32[1,48,8,4,128]{4,3,2,1,0:T(4,128)}, u32[]{:S(2)}) copy-start(f32[1,48,8,4,128]{4,3,2,1,0:T(4,128)} %param.6) | copy-start | bytes 2359300
  3.1 4.8 %copy-start.1 = (f32[1,48,8,4,128]{4,3,2,1,0:T(4,128)S(1)}, f32[1,48,8,4,128]{4,3,2,1,0:T(4,128)}, u32[]{:S(2)}) copy-start(f32[1,48,8,4,128]{4,3,2,1,0:T(4,128)} %param.6) | copy-start | bytes 2359300
  3.7 1.4 %collective-permute-start = (f32[32,128]{1,0:T(8,128)S(1)}, f32[32,128]{1,0:T(8,128)S(1)}, u32[]{:S(2)}, u32[]{:S(2)}) collective-permute-start(f32[32,128]{1,0:T(8,128)S(1)} %weigh.1), channel_id=1, source_target_pairs={{0,1},{1,0},{2,3},{3,2},{4,5},{5,4},{6,7},{7,6},{8,9},{9,8},{10,11... | collective-permute-start | bytes 49160 | tf_op jit(solution)/shard_map/ppermute | solution.py:183
  5.1 7.6 %collective-permute-start.1 = (f32[32,128]{1,0:T(8,128)S(1)}, f32[32,128]{1,0:T(8,128)S(1)}, u32[]{:S(2)}, u32[]{:S(2)}) collective-permute-start(f32[32,128]{1,0:T(8,128)S(1)} %add.6), channel_id=1, source_target_pairs={{0,2},{1,3},{2,0},{3,1},{4,6},{5,7},{6,4},{7,5},{8,10},{9,11},{10,... | collective-permute-start | bytes 49160 | tf_op jit(solution)/shard_map/ppermute | solution.py:183
  8.0 20.1 %collective-permute-start.5 = (f32[6,32,128]{2,1,0:T(8,128)S(1)}, f32[6,32,128]{2,1,0:T(8,128)S(1)}, u32[]{:S(2)}, u32[]{:S(2)}) collective-permute-start(f32[6,32,128]{2,1,0:T(8,128)S(1)} %get-tuple-element.23), channel_id=1, source_target_pairs={{0,12},{4,0},{8,4},{12,8},{1,13},{5,1},{9,5},{13,9},{2,14},{6,2},{... | collective-permute-start | bytes 294920 | tf_op jit(solution)/shard_map/ppermute | solution.py:199
  11.6 18.1 %collective-permute-start.6 = (f32[6,32,128]{2,1,0:T(8,128)S(1)}, f32[6,32,128]{2,1,0:T(8,128)S(1)}, u32[]{:S(2)}, u32[]{:S(2)}) collective-permute-start(f32[6,32,128]{2,1,0:T(8,128)S(1)} %get-tuple-element.24), channel_id=1, source_target_pairs={{0,8},{4,12},{8,0},{12,4},{1,9},{5,13},{9,1},{13,5},{2,10},{6,14},... | collective-permute-start | bytes 294920 | tf_op jit(solution)/shard_map/ppermute | solution.py:199
  11.6 1.0 %copy-start.4 = (f32[8,4,128]{2,1,0:T(4,128)S(1)}, f32[8,4,128]{2,1,0:T(4,128)}, u32[]{:S(2)}) copy-start(f32[8,4,128]{2,1,0:T(4,128)} %param.5) | copy-start | bytes 49156
  11.6 18.1 %collective-permute-start.7 = (f32[6,32,128]{2,1,0:T(8,128)S(1)}, f32[6,32,128]{2,1,0:T(8,128)S(1)}, u32[]{:S(2)}, u32[]{:S(2)}) collective-permute-start(f32[6,32,128]{2,1,0:T(8,128)S(1)} %get-tuple-element.25), channel_id=1, source_target_pairs={{0,4},{4,8},{8,12},{12,0},{1,5},{5,9},{9,13},{13,1},{2,6},{6,10},{... | collective-permute-start | bytes 294920 | tf_op jit(solution)/shard_map/ppermute | solution.py:199
  12.7 6.4 %collective-permute-start.2 = (f32[2,32,128]{2,1,0:T(8,128)S(1)}, f32[2,32,128]{2,1,0:T(8,128)S(1)}, u32[]{:S(2)}, u32[]{:S(2)}) collective-permute-start(f32[2,32,128]{2,1,0:T(8,128)S(1)} %pad_maximum_fusion.refs_0_), channel_id=1, source_target_pairs={{0,12},{4,0},{8,4},{12,8},{1,13},{5,1},{9,5},{13,9},{2,14},{6,2},{... | collective-permute-start | bytes 98312 | tf_op jit(solution)/shard_map/ppermute | solution.py:199
  15.5 7.3 %collective-permute-start.3 = (f32[2,32,128]{2,1,0:T(8,128)S(1)}, f32[2,32,128]{2,1,0:T(8,128)S(1)}, u32[]{:S(2)}, u32[]{:S(2)}) collective-permute-start(f32[2,32,128]{2,1,0:T(8,128)S(1)} %pad_maximum_fusion.refs_0_), channel_id=1, source_target_pairs={{0,8},{4,12},{8,0},{12,4},{1,9},{5,13},{9,1},{13,5},{2,10},{6,14},... | collective-permute-start | bytes 98312 | tf_op jit(solution)/shard_map/ppermute | solution.py:199
  19.0 7.0 %collective-permute-start.4 = (f32[2,32,128]{2,1,0:T(8,128)S(1)}, f32[2,32,128]{2,1,0:T(8,128)S(1)}, u32[]{:S(2)}, u32[]{:S(2)}) collective-permute-start(f32[2,32,128]{2,1,0:T(8,128)S(1)} %pad_maximum_fusion.refs_0_), channel_id=1, source_target_pairs={{0,4},{4,8},{8,12},{12,0},{1,5},{5,9},{9,13},{13,1},{2,6},{6,10},{... | collective-permute-start | bytes 98312 | tf_op jit(solution)/shard_map/ppermute | solution.py:199
  22.8 12.6 %collective-permute-start.11 = (f32[6,32,128]{2,1,0:T(8,128)S(1)}, f32[6,32,128]{2,1,0:T(8,128)S(1)}, u32[]{:S(2)}, u32[]{:S(2)}) collective-permute-start(f32[6,32,128]{2,1,0:T(8,128)S(1)} %get-tuple-element.33), channel_id=1, source_target_pairs={{0,12},{4,0},{8,4},{12,8},{1,13},{5,1},{9,5},{13,9},{2,14},{6,2},{... | collective-permute-start | bytes 294920 | tf_op jit(solution)/shard_map/ppermute | solution.py:199
  26.1 11.4 %collective-permute-start.12 = (f32[6,32,128]{2,1,0:T(8,128)S(1)}, f32[6,32,128]{2,1,0:T(8,128)S(1)}, u32[]{:S(2)}, u32[]{:S(2)}) collective-permute-start(f32[6,32,128]{2,1,0:T(8,128)S(1)} %get-tuple-element.34), channel_id=1, source_target_pairs={{0,8},{4,12},{8,0},{12,4},{1,9},{5,13},{9,1},{13,5},{2,10},{6,14},... | collective-permute-start | bytes 294920 | tf_op jit(solution)/shard_map/ppermute | solution.py:199
  28.1 9.4 %collective-permute-start.13 = (f32[6,32,128]{2,1,0:T(8,128)S(1)}, f32[6,32,128]{2,1,0:T(8,128)S(1)}, u32[]{:S(2)}, u32[]{:S(2)}) collective-permute-start(f32[6,32,128]{2,1,0:T(8,128)S(1)} %get-tuple-element.35), channel_id=1, source_target_pairs={{0,4},{4,8},{8,12},{12,0},{1,5},{5,9},{9,13},{13,1},{2,6},{6,10},{... | collective-permute-start | bytes 294920 | tf_op jit(solution)/shard_map/ppermute | solution.py:199
  32.6 9.7 %collective-permute-start.8 = (f32[6,32,128]{2,1,0:T(8,128)S(1)}, f32[6,32,128]{2,1,0:T(8,128)S(1)}, u32[]{:S(2)}, u32[]{:S(2)}) collective-permute-start(f32[6,32,128]{2,1,0:T(8,128)S(1)} %get-tuple-element.29), channel_id=1, source_target_pairs={{0,4},{4,8},{8,12},{12,0},{1,5},{5,9},{9,13},{13,1},{2,6},{6,10},{... | collective-permute-start | bytes 294920 | tf_op jit(solution)/shard_map/ppermute | solution.py:199
  34.5 10.1 %collective-permute-start.9 = (f32[6,32,128]{2,1,0:T(8,128)S(1)}, f32[6,32,128]{2,1,0:T(8,128)S(1)}, u32[]{:S(2)}, u32[]{:S(2)}) collective-permute-start(f32[6,32,128]{2,1,0:T(8,128)S(1)} %get-tuple-element.30), channel_id=1, source_target_pairs={{0,8},{4,12},{8,0},{12,4},{1,9},{5,13},{9,1},{13,5},{2,10},{6,14},... | collective-permute-start | bytes 294920 | tf_op jit(solution)/shard_map/ppermute | solution.py:199
  35.4 9.1 %collective-permute-start.10 = (f32[6,32,128]{2,1,0:T(8,128)S(1)}, f32[6,32,128]{2,1,0:T(8,128)S(1)}, u32[]{:S(2)}, u32[]{:S(2)}) collective-permute-start(f32[6,32,128]{2,1,0:T(8,128)S(1)} %get-tuple-element.31), channel_id=1, source_target_pairs={{0,12},{4,0},{8,4},{12,8},{1,13},{5,1},{9,5},{13,9},{2,14},{6,2},{... | collective-permute-start | bytes 294920 | tf_op jit(solution)/shard_map/ppermute | solution.py:199
  40.4 6.6 %collective-permute-start.14 = (f32[6,32,128]{2,1,0:T(8,128)S(1)}, f32[6,32,128]{2,1,0:T(8,128)S(1)}, u32[]{:S(2)}, u32[]{:S(2)}) collective-permute-start(f32[6,32,128]{2,1,0:T(8,128)S(1)} %get-tuple-element.37), channel_id=1, source_target_pairs={{0,4},{4,8},{8,12},{12,0},{1,5},{5,9},{9,13},{13,1},{2,6},{6,10},{... | collective-permute-start | bytes 294920 | tf_op jit(solution)/shard_map/ppermute | solution.py:199
  40.4 10.1 %collective-permute-start.15 = (f32[6,32,128]{2,1,0:T(8,128)S(1)}, f32[6,32,128]{2,1,0:T(8,128)S(1)}, u32[]{:S(2)}, u32[]{:S(2)}) collective-permute-start(f32[6,32,128]{2,1,0:T(8,128)S(1)} %get-tuple-element.38), channel_id=1, source_target_pairs={{0,8},{4,12},{8,0},{12,4},{1,9},{5,13},{9,1},{13,5},{2,10},{6,14},... | collective-permute-start | bytes 294920 | tf_op jit(solution)/shard_map/ppermute | solution.py:199
  42.4 8.2 %collective-permute-start.16 = (f32[6,32,128]{2,1,0:T(8,128)S(1)}, f32[6,32,128]{2,1,0:T(8,128)S(1)}, u32[]{:S(2)}, u32[]{:S(2)}) collective-permute-start(f32[6,32,128]{2,1,0:T(8,128)S(1)} %get-tuple-element.39), channel_id=1, source_target_pairs={{0,12},{4,0},{8,4},{12,8},{1,13},{5,1},{9,5},{13,9},{2,14},{6,2},{... | collective-permute-start | bytes 294920 | tf_op jit(solution)/shard_map/ppermute | solution.py:199

commit v6 on v5

--- a/solution.py
+++ b/solution.py
@@ -208,13 +208,10 @@
         out_shape=field(*flat),
         in_specs=[SMEM, SMEM, SMEM, VMEM],
         out_specs=VMEM,
-        compiler_params=params(),
+        compiler_params=pltpu.CompilerParams(vmem_limit_bytes=63 * 1024 * 1024),
         name="weigh",
     )(counts, flags, kappa, tracers)
-    hop = 1
-    while hop < lax.axis_size("group"):
-        total = total + swap(total, "group", hop)
-        hop *= 2
+    total = sum((swap(total, "group", hop) for hop in range(1, lax.axis_size("group"))), total)
     small = jnp.stack([theta, total])
     small = [small] + [shift(small, tiles - step) for step in range(1, tiles)]
 

time: 51.7 us -> 50.5 us (0.977)
  local copies, waits for them, and re-layouts: 1.8 us -> 0.01 us
  Pallas kernels: 9.39 us -> 10.6 us
  waiting for transfers between devices: 9.33 us -> 8.66 us
    unnamed x10 -> x6, local copies, waits for them, and re-layouts: 1.8 us -> 0.01 us
    pallas_call x1, Pallas kernels: 0.63 us -> 1.85 us  [per_device(): pl.pallas_call(functools.partial(weigh, slots), out_shape=field(*flat), i...]
    ppermute x2 -> x3, waiting for transfers between devices: 0.84 us -> 0.01 us  [swap(): lax.ppermute(value, axis, [(i, i ^ hop) for i in range(lax.axis_size(axis...]
    ppermute x2 -> x3, starting transfers between devices: 3.35 us -> 3.06 us  [swap(): lax.ppermute(value, axis, [(i, i ^ hop) for i in range(lax.axis_size(axis...]
  transfers between devices with their start and end apart: 17 -> 18, of which waited for: 5 -> 4; matrix products, arithmetic and copies ran while one was open for 0% -> 0% of each run, Pallas kernels for 15% -> 16%
where the time goes in v6:
time: 50.5 us; the launch traced here: 50.4 us
  starting transfers between devices  29.6 us (59%)
  Pallas kernels  10.6 us (21%)
  waiting for transfers between devices  8.66 us (17%)
  between operations  1.45 us (3%)
    ppermute x15, starting transfers between devices, shift(): lax.ppermute(value, 'tile', [(i, (i + step) % tiles) for i in range(tiles)])  26.6 us
    ppermute x15, waiting for transfers between devices, shift(): lax.ppermute(value, 'tile', [(i, (i + step) % tiles) for i in range(tiles)])  8.65 us
    pallas_call x2, Pallas kernels, work(): pl.pallas_call(functools.partial(both, tiles, part, rows, nz), out_shape=...  5.8 us
    ppermute x3, starting transfers between devices, swap(): lax.ppermute(value, axis, [(i, i ^ hop) for i in range(lax.axis_size(axis...  3.06 us
    pallas_call x1, Pallas kernels, per_device(): pl.pallas_call(functools.partial(dynamics, tiles, rows, nz), out_shape=[f...  1.93 us
    pallas_call x1, Pallas kernels, per_device(): pl.pallas_call(functools.partial(weigh, slots), out_shape=field(*flat), i...  1.85 us
  transfers between devices with their start and end apart: 18, of which 4 were waited for; matrix products, arithmetic and copies ran while one was open for 0% of the time, Pallas kernels for 16%

profile of v6, /device:TPU:0, one launch (start us, length us, event | category | flops | bytes accessed | tf_op | source)
XLA Modules:
  0.0 50.4 jit_solution(1042378467464058592)
XLA Ops:
  0.6 0.0 copy-start
  1.4 1.8 %weigh.1 = f32[32,128]{1,0:T(8,128)} custom-call(s32[1,1]{1,0:T(1,128)S(6)} %copy.7.counts_ref, s32[1,48]{1,0:T(1,128)} %flags_ref.1, f32[1,48]{1,0:T(1,128)} %kappa_ref.1, f32[48,32,128]{2,1,0:T(8,128)} %bitcast.7), custom_call_target="tpu_custom_call" | custom-call | tf_op jit(solution)/shard_map/weigh/pallas_call | solution.py:206
  3.2 2.4 %collective-permute-start.2 = (f32[32,128]{1,0:T(8,128)}, f32[32,128]{1,0:T(8,128)S(1)}, u32[]{:S(2)}, u32[]{:S(2)}) collective-permute-start(f32[32,128]{1,0:T(8,128)} %weigh.1), channel_id=1, source_target_pairs={{0,3},{1,2},{2,1},{3,0},{4,7},{5,6},{6,5},{7,4},{8,11},{9,10},{10,... | collective-permute-start | bytes 49160 | tf_op jit(solution)/shard_map/ppermute | solution.py:183
  5.6 0.6 %collective-permute-start.1 = (f32[32,128]{1,0:T(8,128)}, f32[32,128]{1,0:T(8,128)S(1)}, u32[]{:S(2)}, u32[]{:S(2)}) collective-permute-start(f32[32,128]{1,0:T(8,128)} %weigh.1), channel_id=1, source_target_pairs={{0,2},{1,3},{2,0},{3,1},{4,6},{5,7},{6,4},{7,5},{8,10},{9,11},{10,... | collective-permute-start | bytes 49160 | tf_op jit(solution)/shard_map/ppermute | solution.py:183
  6.2 0.1 collective-permute-start
  6.3 0.0 copy-done
  6.3 0.0 copy-start.1
  6.3 3.9 %collective-permute-start.6 = (f32[6,32,128]{2,1,0:T(8,128)S(1)}, f32[6,32,128]{2,1,0:T(8,128)S(1)}, u32[]{:S(2)}, u32[]{:S(2)}) collective-permute-start(f32[6,32,128]{2,1,0:T(8,128)S(1)} %get-tuple-element.23), channel_id=1, source_target_pairs={{0,12},{4,0},{8,4},{12,8},{1,13},{5,1},{9,5},{13,9},{2,14},{6,2},{... | collective-permute-start | bytes 294920 | tf_op jit(solution)/shard_map/ppermute | solution.py:199
  10.2 0.0 collective-permute-start.7
  10.2 0.0 collective-permute-done.2
  10.2 0.0 copy-start.2
  10.2 1.0 %collective-permute-start.8 = (f32[6,32,128]{2,1,0:T(8,128)S(1)}, f32[6,32,128]{2,1,0:T(8,128)S(1)}, u32[]{:S(2)}, u32[]{:S(2)}) collective-permute-start(f32[6,32,128]{2,1,0:T(8,128)S(1)} %get-tuple-element.25), channel_id=1, source_target_pairs={{0,4},{4,8},{8,12},{12,0},{1,5},{5,9},{9,13},{13,1},{2,6},{6,10},{... | collective-permute-start | bytes 294920 | tf_op jit(solution)/shard_map/ppermute | solution.py:199
  11.2 0.0 collective-permute-done.1
  11.2 0.0 collective-permute-done
  11.2 0.0 copy-done.1
  11.3 0.0 copy-done.2
  11.3 2.9 %collective-permute-start.3 = (f32[2,32,128]{2,1,0:T(8,128)S(1)}, f32[2,32,128]{2,1,0:T(8,128)S(1)}, u32[]{:S(2)}, u32[]{:S(2)}) collective-permute-start(f32[2,32,128]{2,1,0:T(8,128)S(1)} %pad_maximum_fusion.refs_0_), channel_id=1, source_target_pairs={{0,12},{4,0},{8,4},{12,8},{1,13},{5,1},{9,5},{13,9},{2,14},{6,2},{... | collective-permute-start | bytes 98312 | tf_op jit(solution)/shard_map/ppermute | solution.py:199
  14.2 1.1 %collective-permute-start.4 = (f32[2,32,128]{2,1,0:T(8,128)S(1)}, f32[2,32,128]{2,1,0:T(8,128)S(1)}, u32[]{:S(2)}, u32[]{:S(2)}) collective-permute-start(f32[2,32,128]{2,1,0:T(8,128)S(1)} %pad_maximum_fusion.refs_0_), channel_id=1, source_target_pairs={{0,8},{4,12},{8,0},{12,4},{1,9},{5,13},{9,1},{13,5},{2,10},{6,14},... | collective-permute-start | bytes 98312 | tf_op jit(solution)/shard_map/ppermute | solution.py:199
  15.3 2.6 %collective-permute-done.3.refs_1_ = f32[2,32,128]{2,1,0:T(8,128)S(1)} collective-permute-done((f32[2,32,128]{2,1,0:T(8,128)S(1)}, f32[2,32,128]{2,1,0:T(8,128)S(1)}, u32[]{:S(2)}, u32[]{:S(2)}) %collective-permute-start.3) | collective-permute-done | bytes 32800 | tf_op jit(solution)/shard_map/ppermute | solution.py:199
  17.9 3.9 %collective-permute-start.5 = (f32[2,32,128]{2,1,0:T(8,128)S(1)}, f32[2,32,128]{2,1,0:T(8,128)S(1)}, u32[]{:S(2)}, u32[]{:S(2)}) collective-permute-start(f32[2,32,128]{2,1,0:T(8,128)S(1)} %pad_maximum_fusion.refs_0_), channel_id=1, source_target_pairs={{0,4},{4,8},{8,12},{12,0},{1,5},{5,9},{9,13},{13,1},{2,6},{6,10},{... | collective-permute-start | bytes 98312 | tf_op jit(solution)/shard_map/ppermute | solution.py:199
  21.9 0.0 collective-permute-done.4.refs_2_
  21.9 3.1 %collective-permute-start.12 = (f32[6,32,128]{2,1,0:T(8,128)S(1)}, f32[6,32,128]{2,1,0:T(8,128)S(1)}, u32[]{:S(2)}, u32[]{:S(2)}) collective-permute-start(f32[6,32,128]{2,1,0:T(8,128)S(1)} %get-tuple-element.33), channel_id=1, source_target_pairs={{0,12},{4,0},{8,4},{12,8},{1,13},{5,1},{9,5},{13,9},{2,14},{6,2},{... | collective-permute-start | bytes 294920 | tf_op jit(solution)/shard_map/ppermute | solution.py:199
  24.9 0.0 collective-permute-done.5.refs_3_
  24.9 0.2 collective-permute-start.13
  25.2 1.9 %dynamics.1 = (f32[16,7,8,128]{3,2,1,0:T(8,128)S(1)}, f32[16,7,8,128]{3,2,1,0:T(8,128)S(1)}, f32[32,128]{1,0:T(8,128)}) custom-call(f32[2,32,128]{2,1,0:T(8,128)S(1)} %pad_maximum_fusion.refs_0_, f32[2,32,128]{2,1,0:T(8,128)S(1)} %collective-permute-done.3.refs_1_, f32[2,32,128]{2,1,0:T(8,128)S(1)} %collective-permute-done.4.refs_2_, ...), custom_call_target="tpu_custom_call" | custom-call | tf_op jit(solution)/shard_map/dynamics/pallas_call | solution.py:231
  27.1 0.0 collective-permute-done.6.refs_1_
  27.1 1.6 %collective-permute-start.14 = (f32[6,32,128]{2,1,0:T(8,128)S(1)}, f32[6,32,128]{2,1,0:T(8,128)S(1)}, u32[]{:S(2)}, u32[]{:S(2)}) collective-permute-start(f32[6,32,128]{2,1,0:T(8,128)S(1)} %get-tuple-element.35), channel_id=1, source_target_pairs={{0,4},{4,8},{8,12},{12,0},{1,5},{5,9},{9,13},{13,1},{2,6},{6,10},{... | collective-permute-start | bytes 294920 | tf_op jit(solution)/shard_map/ppermute | solution.py:199
  28.7 0.0 collective-permute-done.7.refs_2_
  28.7 0.0 collective-permute-done.8.refs_3_
  28.7 2.9 %both.2 = (f32[6,32,128]{2,1,0:T(8,128)S(1)}, f32[6,32,128]{2,1,0:T(8,128)S(1)}, f32[6,32,128]{2,1,0:T(8,128)S(1)}, f32[6,32,128]{2,1,0:T(8,128)S(1)}) custom-call(f32[6,32,128]{2,1,0:T(8,128)S(1)} %get-tuple-element.22.refs_0_.after_ref, f32[6,32,128]{2,1,0:T(8,128)S(1)} %collective-permute-done.6.refs_1_, ...), custom_call_target="tpu_custom_call" | custom-call | tf_op jit(solution)/shard_map/both/pallas_call | solution.py:242
  31.6 1.7 %collective-permute-start.9 = (f32[6,32,128]{2,1,0:T(8,128)S(1)}, f32[6,32,128]{2,1,0:T(8,128)S(1)}, u32[]{:S(2)}, u32[]{:S(2)}) collective-permute-start(f32[6,32,128]{2,1,0:T(8,128)S(1)} %get-tuple-element.29), channel_id=1, source_target_pairs={{0,4},{4,8},{8,12},{12,0},{1,5},{5,9},{9,13},{13,1},{2,6},{6,10},{... | collective-permute-start | bytes 294920 | tf_op jit(solution)/shard_map/ppermute | solution.py:199
  33.3 1.1 %collective-permute-start.10 = (f32[6,32,128]{2,1,0:T(8,128)S(1)}, f32[6,32,128]{2,1,0:T(8,128)S(1)}, u32[]{:S(2)}, u32[]{:S(2)}) collective-permute-start(f32[6,32,128]{2,1,0:T(8,128)S(1)} %get-tuple-element.30), channel_id=1, source_target_pairs={{0,8},{4,12},{8,0},{12,4},{1,9},{5,13},{9,1},{13,5},{2,10},{6,14},... | collective-permute-start | bytes 294920 | tf_op jit(solution)/shard_map/ppermute | solution.py:199
  34.5 0.0 collective-permute-done.12.refs_1_
  34.5 2.0 %collective-permute-start.11 = (f32[6,32,128]{2,1,0:T(8,128)S(1)}, f32[6,32,128]{2,1,0:T(8,128)S(1)}, u32[]{:S(2)}, u32[]{:S(2)}) collective-permute-start(f32[6,32,128]{2,1,0:T(8,128)S(1)} %get-tuple-element.31), channel_id=1, source_target_pairs={{0,12},{4,0},{8,4},{12,8},{1,13},{5,1},{9,5},{13,9},{2,14},{6,2},{... | collective-permute-start | bytes 294920 | tf_op jit(solution)/shard_map/ppermute | solution.py:199
  36.5 0.0 collective-permute-done.13.refs_2_
  36.5 0.0 collective-permute-done.14.refs_3_
  36.5 2.9 %both.3 = (f32[6,32,128]{2,1,0:T(8,128)S(1)}, f32[6,32,128]{2,1,0:T(8,128)S(1)}, f32[6,32,128]{2,1,0:T(8,128)S(1)}, f32[6,32,128]{2,1,0:T(8,128)S(1)}) custom-call(f32[6,32,128]{2,1,0:T(8,128)S(1)} %get-tuple-element.32.refs_0_, f32[6,32,128]{2,1,0:T(8,128)S(1)} %collective-permute-done.12.refs_1_, f32[6,32,128]{2,1,0:T(8,128)S(1)} %collective-permute-done.13.refs_2_, ...), custom_call_target="tpu_custom_call" | custom-call | tf_op jit(solution)/shard_map/both/pallas_call | solution.py:242
  39.4 0.1 collective-permute-start.15
  39.5 1.8 %collective-permute-start.16 = (f32[6,32,128]{2,1,0:T(8,128)S(1)}, f32[6,32,128]{2,1,0:T(8,128)S(1)}, u32[]{:S(2)}, u32[]{:S(2)}) collective-permute-start(f32[6,32,128]{2,1,0:T(8,128)S(1)} %get-tuple-element.38), channel_id=1, source_target_pairs={{0,8},{4,12},{8,0},{12,4},{1,9},{5,13},{9,1},{13,5},{2,10},{6,14},... | collective-permute-start | bytes 294920 | tf_op jit(solution)/shard_map/ppermute | solution.py:199
  41.3 0.0 collective-permute-done.9.refs_1_
  41.3 2.2 %collective-permute-start.17 = (f32[6,32,128]{2,1,0:T(8,128)S(1)}, f32[6,32,128]{2,1,0:T(8,128)S(1)}, u32[]{:S(2)}, u32[]{:S(2)}) collective-permute-start(f32[6,32,128]{2,1,0:T(8,128)S(1)} %get-tuple-element.39), channel_id=1, source_target_pairs={{0,12},{4,0},{8,4},{12,8},{1,13},{5,1},{9,5},{13,9},{2,14},{6,2},{... | collective-permute-start | bytes 294920 | tf_op jit(solution)/shard_map/ppermute | solution.py:199
  43.4 0.1 collective-permute-done.10.refs_2_
  43.5 0.0 collective-permute-done.11.refs_3_
  43.5 2.5 %collective-permute-done.15.refs_5_ = f32[6,32,128]{2,1,0:T(8,128)S(1)} collective-permute-done((f32[6,32,128]{2,1,0:T(8,128)S(1)}, f32[6,32,128]{2,1,0:T(8,128)S(1)}, u32[]{:S(2)}, u32[]{:S(2)}) %collective-permute-start.15) | collective-permute-done | bytes 98336 | tf_op jit(solution)/shard_map/ppermute | solution.py:199
  46.0 3.4 %collective-permute-done.16.refs_6_ = f32[6,32,128]{2,1,0:T(8,128)S(1)} collective-permute-done((f32[6,32,128]{2,1,0:T(8,128)S(1)}, f32[6,32,128]{2,1,0:T(8,128)S(1)}, u32[]{:S(2)}, u32[]{:S(2)}) %collective-permute-start.16) | collective-permute-done | bytes 98336 | tf_op jit(solution)/shard_map/ppermute | solution.py:199
  49.4 0.0 collective-permute-done.17.refs_7_
  49.4 0.9 %assemble.1 = f32[48,32,128]{2,1,0:T(8,128)} custom-call(s32[1]{0:T(128)} %bitcast.4.me_ref.after_ref, f32[6,32,128]{2,1,0:T(8,128)S(1)} %get-tuple-element.28.refs_0_, f32[6,32,128]{2,1,0:T(8,128)S(1)} %collective-permute-done.9.refs_1_, f32[6,32,128]{2,1,0:T(8,128)S(1)} %collective-permute-done.10.refs_2_, ...), custom_call_target="tpu_custom_call" | custom-call | tf_op jit(solution)/shard_map/assemble/pallas_call | solution.py:255
  (4 shorter events, 0.1 us)
Async XLA Ops:
  0.6 5.6 %copy-start = (f32[1,48,8,4,128]{4,3,2,1,0:T(4,128)S(1)}, f32[1,48,8,4,128]{4,3,2,1,0:T(4,128)}, u32[]{:S(2)}) copy-start(f32[1,48,8,4,128]{4,3,2,1,0:T(4,128)} %param.6) | copy-start | bytes 2359300
  3.2 7.0 %collective-permute-start.2 = (f32[32,128]{1,0:T(8,128)}, f32[32,128]{1,0:T(8,128)S(1)}, u32[]{:S(2)}, u32[]{:S(2)}) collective-permute-start(f32[32,128]{1,0:T(8,128)} %weigh.1), channel_id=1, source_target_pairs={{0,3},{1,2},{2,1},{3,0},{4,7},{5,6},{6,5},{7,4},{8,11},{9,10},{10,... | collective-permute-start | bytes 49160 | tf_op jit(solution)/shard_map/ppermute | solution.py:183
  5.6 5.7 %collective-permute-start.1 = (f32[32,128]{1,0:T(8,128)}, f32[32,128]{1,0:T(8,128)S(1)}, u32[]{:S(2)}, u32[]{:S(2)}) collective-permute-start(f32[32,128]{1,0:T(8,128)} %weigh.1), channel_id=1, source_target_pairs={{0,2},{1,3},{2,0},{3,1},{4,6},{5,7},{6,4},{7,5},{8,10},{9,11},{10,... | collective-permute-start | bytes 49160 | tf_op jit(solution)/shard_map/ppermute | solution.py:183
  6.2 5.1 %collective-permute-start = (f32[32,128]{1,0:T(8,128)}, f32[32,128]{1,0:T(8,128)S(1)}, u32[]{:S(2)}, u32[]{:S(2)}) collective-permute-start(f32[32,128]{1,0:T(8,128)} %weigh.1), channel_id=1, source_target_pairs={{0,1},{1,0},{2,3},{3,2},{4,5},{5,4},{6,7},{7,6},{8,9},{9,8},{10,11... | collective-permute-start | bytes 49160 | tf_op jit(solution)/shard_map/ppermute | solution.py:183
  6.3 5.0 %copy-start.1 = (f32[32,128]{1,0:T(8,128)S(1)}, f32[32,128]{1,0:T(8,128)}, u32[]{:S(2)}) copy-start(f32[32,128]{1,0:T(8,128)} %weigh.1) | copy-start | bytes 49156
  6.3 20.8 %collective-permute-start.6 = (f32[6,32,128]{2,1,0:T(8,128)S(1)}, f32[6,32,128]{2,1,0:T(8,128)S(1)}, u32[]{:S(2)}, u32[]{:S(2)}) collective-permute-start(f32[6,32,128]{2,1,0:T(8,128)S(1)} %get-tuple-element.23), channel_id=1, source_target_pairs={{0,12},{4,0},{8,4},{12,8},{1,13},{5,1},{9,5},{13,9},{2,14},{6,2},{... | collective-permute-start | bytes 294920 | tf_op jit(solution)/shard_map/ppermute | solution.py:199
  10.2 18.5 %collective-permute-start.7 = (f32[6,32,128]{2,1,0:T(8,128)S(1)}, f32[6,32,128]{2,1,0:T(8,128)S(1)}, u32[]{:S(2)}, u32[]{:S(2)}) collective-permute-start(f32[6,32,128]{2,1,0:T(8,128)S(1)} %get-tuple-element.24), channel_id=1, source_target_pairs={{0,8},{4,12},{8,0},{12,4},{1,9},{5,13},{9,1},{13,5},{2,10},{6,14},... | collective-permute-start | bytes 294920 | tf_op jit(solution)/shard_map/ppermute | solution.py:199
  10.2 1.0 %copy-start.2 = (f32[8,4,128]{2,1,0:T(4,128)S(1)}, f32[8,4,128]{2,1,0:T(4,128)}, u32[]{:S(2)}) copy-start(f32[8,4,128]{2,1,0:T(4,128)} %param.5) | copy-start | bytes 49156
  10.2 18.5 %collective-permute-start.8 = (f32[6,32,128]{2,1,0:T(8,128)S(1)}, f32[6,32,128]{2,1,0:T(8,128)S(1)}, u32[]{:S(2)}, u32[]{:S(2)}) collective-permute-start(f32[6,32,128]{2,1,0:T(8,128)S(1)} %get-tuple-element.25), channel_id=1, source_target_pairs={{0,4},{4,8},{8,12},{12,0},{1,5},{5,9},{9,13},{13,1},{2,6},{6,10},{... | collective-permute-start | bytes 294920 | tf_op jit(solution)/shard_map/ppermute | solution.py:199
  11.3 6.6 %collective-permute-start.3 = (f32[2,32,128]{2,1,0:T(8,128)S(1)}, f32[2,32,128]{2,1,0:T(8,128)S(1)}, u32[]{:S(2)}, u32[]{:S(2)}) collective-permute-start(f32[2,32,128]{2,1,0:T(8,128)S(1)} %pad_maximum_fusion.refs_0_), channel_id=1, source_target_pairs={{0,12},{4,0},{8,4},{12,8},{1,13},{5,1},{9,5},{13,9},{2,14},{6,2},{... | collective-permute-start | bytes 98312 | tf_op jit(solution)/shard_map/ppermute | solution.py:199
  14.2 7.7 %collective-permute-start.4 = (f32[2,32,128]{2,1,0:T(8,128)S(1)}, f32[2,32,128]{2,1,0:T(8,128)S(1)}, u32[]{:S(2)}, u32[]{:S(2)}) collective-permute-start(f32[2,32,128]{2,1,0:T(8,128)S(1)} %pad_maximum_fusion.refs_0_), channel_id=1, source_target_pairs={{0,8},{4,12},{8,0},{12,4},{1,9},{5,13},{9,1},{13,5},{2,10},{6,14},... | collective-permute-start | bytes 98312 | tf_op jit(solution)/shard_map/ppermute | solution.py:199
  17.9 7.0 %collective-permute-start.5 = (f32[2,32,128]{2,1,0:T(8,128)S(1)}, f32[2,32,128]{2,1,0:T(8,128)S(1)}, u32[]{:S(2)}, u32[]{:S(2)}) collective-permute-start(f32[2,32,128]{2,1,0:T(8,128)S(1)} %pad_maximum_fusion.refs_0_), channel_id=1, source_target_pairs={{0,4},{4,8},{8,12},{12,0},{1,5},{5,9},{9,13},{13,1},{2,6},{6,10},{... | collective-permute-start | bytes 98312 | tf_op jit(solution)/shard_map/ppermute | solution.py:199
  21.9 12.6 %collective-permute-start.12 = (f32[6,32,128]{2,1,0:T(8,128)S(1)}, f32[6,32,128]{2,1,0:T(8,128)S(1)}, u32[]{:S(2)}, u32[]{:S(2)}) collective-permute-start(f32[6,32,128]{2,1,0:T(8,128)S(1)} %get-tuple-element.33), channel_id=1, source_target_pairs={{0,12},{4,0},{8,4},{12,8},{1,13},{5,1},{9,5},{13,9},{2,14},{6,2},{... | collective-permute-start | bytes 294920 | tf_op jit(solution)/shard_map/ppermute | solution.py:199
  24.9 11.5 %collective-permute-start.13 = (f32[6,32,128]{2,1,0:T(8,128)S(1)}, f32[6,32,128]{2,1,0:T(8,128)S(1)}, u32[]{:S(2)}, u32[]{:S(2)}) collective-permute-start(f32[6,32,128]{2,1,0:T(8,128)S(1)} %get-tuple-element.34), channel_id=1, source_target_pairs={{0,8},{4,12},{8,0},{12,4},{1,9},{5,13},{9,1},{13,5},{2,10},{6,14},... | collective-permute-start | bytes 294920 | tf_op jit(solution)/shard_map/ppermute | solution.py:199
  27.1 9.4 %collective-permute-start.14 = (f32[6,32,128]{2,1,0:T(8,128)S(1)}, f32[6,32,128]{2,1,0:T(8,128)S(1)}, u32[]{:S(2)}, u32[]{:S(2)}) collective-permute-start(f32[6,32,128]{2,1,0:T(8,128)S(1)} %get-tuple-element.35), channel_id=1, source_target_pairs={{0,4},{4,8},{8,12},{12,0},{1,5},{5,9},{9,13},{13,1},{2,6},{6,10},{... | collective-permute-start | bytes 294920 | tf_op jit(solution)/shard_map/ppermute | solution.py:199
  31.6 9.6 %collective-permute-start.9 = (f32[6,32,128]{2,1,0:T(8,128)S(1)}, f32[6,32,128]{2,1,0:T(8,128)S(1)}, u32[]{:S(2)}, u32[]{:S(2)}) collective-permute-start(f32[6,32,128]{2,1,0:T(8,128)S(1)} %get-tuple-element.29), channel_id=1, source_target_pairs={{0,4},{4,8},{8,12},{12,0},{1,5},{5,9},{9,13},{13,1},{2,6},{6,10},{... | collective-permute-start | bytes 294920 | tf_op jit(solution)/shard_map/ppermute | solution.py:199
  33.3 10.2 %collective-permute-start.10 = (f32[6,32,128]{2,1,0:T(8,128)S(1)}, f32[6,32,128]{2,1,0:T(8,128)S(1)}, u32[]{:S(2)}, u32[]{:S(2)}) collective-permute-start(f32[6,32,128]{2,1,0:T(8,128)S(1)} %get-tuple-element.30), channel_id=1, source_target_pairs={{0,8},{4,12},{8,0},{12,4},{1,9},{5,13},{9,1},{13,5},{2,10},{6,14},... | collective-permute-start | bytes 294920 | tf_op jit(solution)/shard_map/ppermute | solution.py:199
  34.5 9.1 %collective-permute-start.11 = (f32[6,32,128]{2,1,0:T(8,128)S(1)}, f32[6,32,128]{2,1,0:T(8,128)S(1)}, u32[]{:S(2)}, u32[]{:S(2)}) collective-permute-start(f32[6,32,128]{2,1,0:T(8,128)S(1)} %get-tuple-element.31), channel_id=1, source_target_pairs={{0,12},{4,0},{8,4},{12,8},{1,13},{5,1},{9,5},{13,9},{2,14},{6,2},{... | collective-permute-start | bytes 294920 | tf_op jit(solution)/shard_map/ppermute | solution.py:199
  39.4 6.6 %collective-permute-start.15 = (f32[6,32,128]{2,1,0:T(8,128)S(1)}, f32[6,32,128]{2,1,0:T(8,128)S(1)}, u32[]{:S(2)}, u32[]{:S(2)}) collective-permute-start(f32[6,32,128]{2,1,0:T(8,128)S(1)} %get-tuple-element.37), channel_id=1, source_target_pairs={{0,4},{4,8},{8,12},{12,0},{1,5},{5,9},{9,13},{13,1},{2,6},{6,10},{... | collective-permute-start | bytes 294920 | tf_op jit(solution)/shard_map/ppermute | solution.py:199
  39.5 9.9 %collective-permute-start.16 = (f32[6,32,128]{2,1,0:T(8,128)S(1)}, f32[6,32,128]{2,1,0:T(8,128)S(1)}, u32[]{:S(2)}, u32[]{:S(2)}) collective-permute-start(f32[6,32,128]{2,1,0:T(8,128)S(1)} %get-tuple-element.38), channel_id=1, source_target_pairs={{0,8},{4,12},{8,0},{12,4},{1,9},{5,13},{9,1},{13,5},{2,10},{6,14},... | collective-permute-start | bytes 294920 | tf_op jit(solution)/shard_map/ppermute | solution.py:199
  41.3 8.2 %collective-permute-start.17 = (f32[6,32,128]{2,1,0:T(8,128)S(1)}, f32[6,32,128]{2,1,0:T(8,128)S(1)}, u32[]{:S(2)}, u32[]{:S(2)}) collective-permute-start(f32[6,32,128]{2,1,0:T(8,128)S(1)} %get-tuple-element.39), channel_id=1, source_target_pairs={{0,12},{4,0},{8,4},{12,8},{1,13},{5,1},{9,5},{13,9},{2,14},{6,2},{... | collective-permute-start | bytes 294920 | tf_op jit(solution)/shard_map/ppermute | solution.py:199

commit v7 on v6

--- a/solution.py
+++ b/solution.py
@@ -135,7 +135,7 @@
 
 
 def dynamics(tiles, rows, nz, *refs):
-    pieces, (coef_ref, next_ref, theta_out, theta_ref, state_ref, first_ref) = refs[:tiles], refs[tiles:]
+    pieces, (coef_ref, next_ref, theta_ref, state_ref, first_ref) = refs[:tiles], refs[tiles:]
     length = tiles * rows
     for step in range(tiles):
         for row in range(rows):
@@ -150,6 +150,16 @@
 
     lax.fori_loop(0, length, heat, 0, unroll=UNROLL)
     coefficients(theta_ref, next_ref, length)
+
+
+def finish(rows, nz, theta_ref, total_ref, next_ref, after_ref, theta_out, state_ref, first_ref):
+    length = total_ref.shape[0]
+
+    def copy(x, carry):
+        state_ref[x, 0] = total_ref[x, 0]
+        return carry
+
+    lax.fori_loop(0, length, copy, 0, unroll=UNROLL)
     advance(next_ref, state_ref, first_ref, length, 1)
     for row in range(rows):
         theta_out[pl.ds(row, nz, stride=rows), :] = theta_ref[row] + (heat_step * SCALE * SCALE) * state_ref[row, 0]
@@ -187,7 +197,8 @@
     _, slots, nz, rows, ny = tracers.shape
     tiles = lax.axis_size("tile")
     share = max(2, -(-slots // tiles))
-    parts = (share // 2, share - share // 2)
+    first = max(1, share * 6 // 12)
+    parts = (first, share - first)
     length = tiles * rows
     me = lax.axis_index("tile").astype(jnp.int32).reshape(1)
     flat = (nz * rows, ny)
@@ -227,13 +238,13 @@
 
     payload = pack(0, parts[0], me)
     one = gather(payload)
-    two = gather(pack(parts[0], parts[1], payload[0]))
-    coef, next_coef, theta_new = pl.pallas_call(
+    two = gather(pack(parts[0], parts[1], me))
+    coef, next_coef, theta_mid, total_mid = pl.pallas_call(
         functools.partial(dynamics, tiles, rows, nz),
-        out_shape=[field(length, 7, nz, ny), field(length, 7, nz, ny), field(*flat)],
+        out_shape=[field(length, 7, nz, ny), field(length, 7, nz, ny), field(length, nz, ny), field(length, 1, nz, ny)],
         in_specs=[VMEM] * tiles,
-        out_specs=[VMEM] * 3,
-        scratch_shapes=[scratch(length, nz, ny), scratch(length, 1, nz, ny), scratch(length, 1, nz, ny)],
+        out_specs=[VMEM] * 4,
+        scratch_shapes=[scratch(length, 1, nz, ny)],
         compiler_params=params(),
         name="dynamics",
     )(*small)
@@ -251,6 +262,15 @@
 
     done_one = work(one, parts[0])
     done_two = work(two, parts[1])
+    theta_new = pl.pallas_call(
+        functools.partial(finish, rows, nz),
+        out_shape=field(*flat),
+        in_specs=[VMEM] * 3 + [HBM],
+        out_specs=VMEM,
+        scratch_shapes=[scratch(length, 1, nz, ny)] * 2,
+        compiler_params=params(),
+        name="finish",
+    )(theta_mid, total_mid, next_coef, done_one[0])
     back = [piece for done in (done_one, done_two) for piece in [done[0]] + [shift(done[step], step) for step in range(1, tiles)]]
     out = pl.pallas_call(
         functools.partial(assemble, tiles, parts),

time: 50.5 us -> 49.8 us (0.986)
  waiting for transfers between devices: 8.66 us -> 5.32 us
  starting transfers between devices: 29.6 us -> 32.3 us
    ppermute x15, waiting for transfers between devices: 8.65 us -> 5.31 us  [shift(): lax.ppermute(value, 'tile', [(i, (i + step) % tiles) for i in range(tiles)])]
    ppermute x15, starting transfers between devices: 26.6 us -> 29.3 us  [shift(): lax.ppermute(value, 'tile', [(i, (i + step) % tiles) for i in range(tiles)])]
    pallas_call x1, Pallas kernels: 1.93 us -> 0.75 us  [per_device(): pl.pallas_call(functools.partial(dynamics, tiles, rows, nz), out_shape=[f...]
    pallas_call x0 -> x1, Pallas kernels: none -> 1.14 us  [per_device(): pl.pallas_call(functools.partial(finish, rows, nz), out_shape=field(*flat...]
  transfers between devices with their start and end apart: 18 -> 18, of which waited for: 4 -> 3; matrix products, arithmetic and copies ran while one was open for 0% -> 0% of each run, Pallas kernels for 16% -> 16%
where the time goes in v7:
time: 49.8 us; the launch traced here: 49.7 us
  starting transfers between devices  32.3 us (65%)
  Pallas kernels  10.6 us (21%)
  waiting for transfers between devices  5.32 us (11%)
  between operations  1.46 us (3%)
    ppermute x15, starting transfers between devices, shift(): lax.ppermute(value, 'tile', [(i, (i + step) % tiles) for i in range(tiles)])  29.3 us
    pallas_call x2, Pallas kernels, work(): pl.pallas_call(functools.partial(both, tiles, part, rows, nz), out_shape=...  5.8 us
    ppermute x15, waiting for transfers between devices, shift(): lax.ppermute(value, 'tile', [(i, (i + step) % tiles) for i in range(tiles)])  5.31 us
    ppermute x3, starting transfers between devices, swap(): lax.ppermute(value, axis, [(i, i ^ hop) for i in range(lax.axis_size(axis...  3.06 us
    pallas_call x1, Pallas kernels, per_device(): pl.pallas_call(functools.partial(weigh, slots), out_shape=field(*flat), i...  1.85 us
    pallas_call x1, Pallas kernels, per_device(): pl.pallas_call(functools.partial(finish, rows, nz), out_shape=field(*flat...  1.14 us
  transfers between devices with their start and end apart: 18, of which 3 were waited for; matrix products, arithmetic and copies ran while one was open for 0% of the time, Pallas kernels for 16%

profile of v7, /device:TPU:0, one launch (start us, length us, event | category | flops | bytes accessed | tf_op | source)
XLA Modules:
  0.0 49.7 jit_solution(6843160615892015681)
XLA Ops:
  0.6 0.0 copy-start
  1.4 1.8 %weigh.1 = f32[32,128]{1,0:T(8,128)} custom-call(s32[1,1]{1,0:T(1,128)S(6)} %copy.7.counts_ref, s32[1,48]{1,0:T(1,128)} %flags_ref.1, f32[1,48]{1,0:T(1,128)} %kappa_ref.1, f32[48,32,128]{2,1,0:T(8,128)} %bitcast.7), custom_call_target="tpu_custom_call" | custom-call | tf_op jit(solution)/shard_map/weigh/pallas_call | solution.py:217
  3.2 2.4 %collective-permute-start.2 = (f32[32,128]{1,0:T(8,128)}, f32[32,128]{1,0:T(8,128)S(1)}, u32[]{:S(2)}, u32[]{:S(2)}) collective-permute-start(f32[32,128]{1,0:T(8,128)} %weigh.1), channel_id=1, source_target_pairs={{0,3},{1,2},{2,1},{3,0},{4,7},{5,6},{6,5},{7,4},{8,11},{9,10},{10,... | collective-permute-start | bytes 49160 | tf_op jit(solution)/shard_map/ppermute | solution.py:193
  5.6 0.6 %collective-permute-start.1 = (f32[32,128]{1,0:T(8,128)}, f32[32,128]{1,0:T(8,128)S(1)}, u32[]{:S(2)}, u32[]{:S(2)}) collective-permute-start(f32[32,128]{1,0:T(8,128)} %weigh.1), channel_id=1, source_target_pairs={{0,2},{1,3},{2,0},{3,1},{4,6},{5,7},{6,4},{7,5},{8,10},{9,11},{10,... | collective-permute-start | bytes 49160 | tf_op jit(solution)/shard_map/ppermute | solution.py:193
  6.2 0.1 collective-permute-start
  6.3 0.0 copy-done
  6.3 0.0 copy-start.1
  6.3 3.9 %collective-permute-start.6 = (f32[6,32,128]{2,1,0:T(8,128)S(1)}, f32[6,32,128]{2,1,0:T(8,128)S(1)}, u32[]{:S(2)}, u32[]{:S(2)}) collective-permute-start(f32[6,32,128]{2,1,0:T(8,128)S(1)} %get-tuple-element.26), channel_id=1, source_target_pairs={{0,12},{4,0},{8,4},{12,8},{1,13},{5,1},{9,5},{13,9},{2,14},{6,2},{... | collective-permute-start | bytes 294920 | tf_op jit(solution)/shard_map/ppermute | solution.py:210
  10.2 0.0 collective-permute-start.7
  10.2 0.0 collective-permute-done.2
  10.2 0.0 copy-start.2
  10.2 1.0 %collective-permute-start.8 = (f32[6,32,128]{2,1,0:T(8,128)S(1)}, f32[6,32,128]{2,1,0:T(8,128)S(1)}, u32[]{:S(2)}, u32[]{:S(2)}) collective-permute-start(f32[6,32,128]{2,1,0:T(8,128)S(1)} %get-tuple-element.28), channel_id=1, source_target_pairs={{0,4},{4,8},{8,12},{12,0},{1,5},{5,9},{9,13},{13,1},{2,6},{6,10},{... | collective-permute-start | bytes 294920 | tf_op jit(solution)/shard_map/ppermute | solution.py:210
  11.2 0.0 collective-permute-done.1
  11.2 0.0 collective-permute-done
  11.2 0.0 copy-done.1
  11.3 0.0 copy-done.2
  11.3 2.9 %collective-permute-start.3 = (f32[2,32,128]{2,1,0:T(8,128)S(1)}, f32[2,32,128]{2,1,0:T(8,128)S(1)}, u32[]{:S(2)}, u32[]{:S(2)}) collective-permute-start(f32[2,32,128]{2,1,0:T(8,128)S(1)} %pad_maximum_fusion.refs_0_), channel_id=1, source_target_pairs={{0,12},{4,0},{8,4},{12,8},{1,13},{5,1},{9,5},{13,9},{2,14},{6,2},{... | collective-permute-start | bytes 98312 | tf_op jit(solution)/shard_map/ppermute | solution.py:210
  14.2 1.1 %collective-permute-start.4 = (f32[2,32,128]{2,1,0:T(8,128)S(1)}, f32[2,32,128]{2,1,0:T(8,128)S(1)}, u32[]{:S(2)}, u32[]{:S(2)}) collective-permute-start(f32[2,32,128]{2,1,0:T(8,128)S(1)} %pad_maximum_fusion.refs_0_), channel_id=1, source_target_pairs={{0,8},{4,12},{8,0},{12,4},{1,9},{5,13},{9,1},{13,5},{2,10},{6,14},... | collective-permute-start | bytes 98312 | tf_op jit(solution)/shard_map/ppermute | solution.py:210
  15.3 2.6 %collective-permute-done.3.refs_1_ = f32[2,32,128]{2,1,0:T(8,128)S(1)} collective-permute-done((f32[2,32,128]{2,1,0:T(8,128)S(1)}, f32[2,32,128]{2,1,0:T(8,128)S(1)}, u32[]{:S(2)}, u32[]{:S(2)}) %collective-permute-start.3) | collective-permute-done | bytes 32800 | tf_op jit(solution)/shard_map/ppermute | solution.py:210
  17.9 3.9 %collective-permute-start.5 = (f32[2,32,128]{2,1,0:T(8,128)S(1)}, f32[2,32,128]{2,1,0:T(8,128)S(1)}, u32[]{:S(2)}, u32[]{:S(2)}) collective-permute-start(f32[2,32,128]{2,1,0:T(8,128)S(1)} %pad_maximum_fusion.refs_0_), channel_id=1, source_target_pairs={{0,4},{4,8},{8,12},{12,0},{1,5},{5,9},{9,13},{13,1},{2,6},{6,10},{... | collective-permute-start | bytes 98312 | tf_op jit(solution)/shard_map/ppermute | solution.py:210
  21.9 0.0 collective-permute-done.4.refs_2_
  21.9 3.1 %collective-permute-start.12 = (f32[6,32,128]{2,1,0:T(8,128)S(1)}, f32[6,32,128]{2,1,0:T(8,128)S(1)}, u32[]{:S(2)}, u32[]{:S(2)}) collective-permute-start(f32[6,32,128]{2,1,0:T(8,128)S(1)} %get-tuple-element.35), channel_id=1, source_target_pairs={{0,12},{4,0},{8,4},{12,8},{1,13},{5,1},{9,5},{13,9},{2,14},{6,2},{... | collective-permute-start | bytes 294920 | tf_op jit(solution)/shard_map/ppermute | solution.py:210
  24.9 0.0 collective-permute-done.5.refs_3_
  24.9 0.2 collective-permute-start.13
  25.2 0.8 %dynamics.1 = (f32[16,7,8,128]{3,2,1,0:T(8,128)S(1)}, f32[16,7,8,128]{3,2,1,0:T(8,128)S(1)}, f32[16,8,128]{2,1,0:T(8,128)S(1)}, f32[16,1,8,128]{3,2,1,0:T(8,128)S(1)}) custom-call(f32[2,32,128]{2,1,0:T(8,128)S(1)} %pad_maximum_fusion.refs_0_, f32[2,32,128]{2,1,0:T(8,128)S(1)} %collective-permute-done.3.refs_1_, ...), custom_call_target="tpu_custom_call" | custom-call | tf_op jit(solution)/shard_map/dynamics/pallas_call | solution.py:242
  25.9 0.0 collective-permute-done.6.refs_1_
  25.9 1.7 %collective-permute-start.14 = (f32[6,32,128]{2,1,0:T(8,128)S(1)}, f32[6,32,128]{2,1,0:T(8,128)S(1)}, u32[]{:S(2)}, u32[]{:S(2)}) collective-permute-start(f32[6,32,128]{2,1,0:T(8,128)S(1)} %get-tuple-element.37), channel_id=1, source_target_pairs={{0,4},{4,8},{8,12},{12,0},{1,5},{5,9},{9,13},{13,1},{2,6},{6,10},{... | collective-permute-start | bytes 294920 | tf_op jit(solution)/shard_map/ppermute | solution.py:210
  27.6 0.0 collective-permute-done.7.refs_2_
  27.6 0.0 collective-permute-done.8.refs_3_
  27.6 2.9 %both.2 = (f32[6,32,128]{2,1,0:T(8,128)S(1)}, f32[6,32,128]{2,1,0:T(8,128)S(1)}, f32[6,32,128]{2,1,0:T(8,128)S(1)}, f32[6,32,128]{2,1,0:T(8,128)S(1)}) custom-call(f32[6,32,128]{2,1,0:T(8,128)S(1)} %get-tuple-element.25.refs_0_, f32[6,32,128]{2,1,0:T(8,128)S(1)} %collective-permute-done.6.refs_1_, f32[6,32,128]{2,1,0:T(8,128)S(1)} %collective-permute-done.7.refs_2_, ...), custom_call_target="tpu_custom_call" | custom-call | tf_op jit(solution)/shard_map/both/pallas_call | solution.py:253
  30.5 1.7 %collective-permute-start.9 = (f32[6,32,128]{2,1,0:T(8,128)S(1)}, f32[6,32,128]{2,1,0:T(8,128)S(1)}, u32[]{:S(2)}, u32[]{:S(2)}) collective-permute-start(f32[6,32,128]{2,1,0:T(8,128)S(1)} %get-tuple-element.31), channel_id=1, source_target_pairs={{0,4},{4,8},{8,12},{12,0},{1,5},{5,9},{9,13},{13,1},{2,6},{6,10},{... | collective-permute-start | bytes 294920 | tf_op jit(solution)/shard_map/ppermute | solution.py:210
  32.2 1.1 %collective-permute-start.10 = (f32[6,32,128]{2,1,0:T(8,128)S(1)}, f32[6,32,128]{2,1,0:T(8,128)S(1)}, u32[]{:S(2)}, u32[]{:S(2)}) collective-permute-start(f32[6,32,128]{2,1,0:T(8,128)S(1)} %get-tuple-element.32), channel_id=1, source_target_pairs={{0,8},{4,12},{8,0},{12,4},{1,9},{5,13},{9,1},{13,5},{2,10},{6,14},... | collective-permute-start | bytes 294920 | tf_op jit(solution)/shard_map/ppermute | solution.py:210
  33.4 0.0 collective-permute-done.12.refs_1_
  33.4 2.0 %collective-permute-start.11 = (f32[6,32,128]{2,1,0:T(8,128)S(1)}, f32[6,32,128]{2,1,0:T(8,128)S(1)}, u32[]{:S(2)}, u32[]{:S(2)}) collective-permute-start(f32[6,32,128]{2,1,0:T(8,128)S(1)} %get-tuple-element.33), channel_id=1, source_target_pairs={{0,12},{4,0},{8,4},{12,8},{1,13},{5,1},{9,5},{13,9},{2,14},{6,2},{... | collective-permute-start | bytes 294920 | tf_op jit(solution)/shard_map/ppermute | solution.py:210
  35.4 0.1 collective-permute-done.13.refs_2_
  35.5 0.0 collective-permute-done.14.refs_3_
  35.5 2.9 %both.3 = (f32[6,32,128]{2,1,0:T(8,128)S(1)}, f32[6,32,128]{2,1,0:T(8,128)S(1)}, f32[6,32,128]{2,1,0:T(8,128)S(1)}, f32[6,32,128]{2,1,0:T(8,128)S(1)}) custom-call(f32[6,32,128]{2,1,0:T(8,128)S(1)} %get-tuple-element.34.refs_0_, f32[6,32,128]{2,1,0:T(8,128)S(1)} %collective-permute-done.12.refs_1_, f32[6,32,128]{2,1,0:T(8,128)S(1)} %collective-permute-done.13.refs_2_, ...), custom_call_target="tpu_custom_call" | custom-call | tf_op jit(solution)/shard_map/both/pallas_call | solution.py:253
  38.4 0.7 %collective-permute-start.15 = (f32[6,32,128]{2,1,0:T(8,128)S(1)}, f32[6,32,128]{2,1,0:T(8,128)S(1)}, u32[]{:S(2)}, u32[]{:S(2)}) collective-permute-start(f32[6,32,128]{2,1,0:T(8,128)S(1)} %get-tuple-element.39), channel_id=1, source_target_pairs={{0,4},{4,8},{8,12},{12,0},{1,5},{5,9},{9,13},{13,1},{2,6},{6,10},{... | collective-permute-start | bytes 294920 | tf_op jit(solution)/shard_map/ppermute | solution.py:210
  39.1 3.1 %collective-permute-start.16 = (f32[6,32,128]{2,1,0:T(8,128)S(1)}, f32[6,32,128]{2,1,0:T(8,128)S(1)}, u32[]{:S(2)}, u32[]{:S(2)}) collective-permute-start(f32[6,32,128]{2,1,0:T(8,128)S(1)} %get-tuple-element.40), channel_id=1, source_target_pairs={{0,8},{4,12},{8,0},{12,4},{1,9},{5,13},{9,1},{13,5},{2,10},{6,14},... | collective-permute-start | bytes 294920 | tf_op jit(solution)/shard_map/ppermute | solution.py:210
  42.2 0.0 collective-permute-done.9.refs_1_
  42.2 2.8 %collective-permute-start.17 = (f32[6,32,128]{2,1,0:T(8,128)S(1)}, f32[6,32,128]{2,1,0:T(8,128)S(1)}, u32[]{:S(2)}, u32[]{:S(2)}) collective-permute-start(f32[6,32,128]{2,1,0:T(8,128)S(1)} %get-tuple-element.41), channel_id=1, source_target_pairs={{0,12},{4,0},{8,4},{12,8},{1,13},{5,1},{9,5},{13,9},{2,14},{6,2},{... | collective-permute-start | bytes 294920 | tf_op jit(solution)/shard_map/ppermute | solution.py:210
  45.1 1.1 %finish.1 = f32[32,128]{1,0:T(8,128)} custom-call(f32[16,8,128]{2,1,0:T(8,128)S(1)} %get-tuple-element.22.theta_ref, f32[16,1,8,128]{3,2,1,0:T(8,128)S(1)} %get-tuple-element.23.total_ref, f32[16,7,8,128]{3,2,1,0:T(8,128)S(1)} %get-tuple-element.24.refs_5_.next_ref, f32[6,32,128]{2,1,0:T(8,128)S(1)} %get-tuple-element.30.after_ref.refs_0_), custom_call_target="tpu_custom_call" | custom-call | tf_op jit(solution)/shard_map/finish/pallas_call | solution.py:265
  46.2 0.0 collective-permute-done.10.refs_2_
  46.2 0.0 collective-permute-done.11.refs_3_
  46.2 0.0 collective-permute-done.15.refs_5_
  46.2 2.5 %collective-permute-done.16.refs_6_ = f32[6,32,128]{2,1,0:T(8,128)S(1)} collective-permute-done((f32[6,32,128]{2,1,0:T(8,128)S(1)}, f32[6,32,128]{2,1,0:T(8,128)S(1)}, u32[]{:S(2)}, u32[]{:S(2)}) %collective-permute-start.16) | collective-permute-done | bytes 98336 | tf_op jit(solution)/shard_map/ppermute | solution.py:210
  48.7 0.0 collective-permute-done.17.refs_7_
  48.7 0.9 %assemble.1 = f32[48,32,128]{2,1,0:T(8,128)} custom-call(s32[1]{0:T(128)} %bitcast.3.me_ref.after_ref, f32[6,32,128]{2,1,0:T(8,128)S(1)} %get-tuple-element.30.after_ref.refs_0_, f32[6,32,128]{2,1,0:T(8,128)S(1)} %collective-permute-done.9.refs_1_, f32[6,32,128]{2,1,0:T(8,128)S(1)} %collective-permute-done.10.refs_2_, ...), custom_call_target="tpu_custom_call" | custom-call | tf_op jit(solution)/shard_map/assemble/pallas_call | solution.py:275
  (4 shorter events, 0.1 us)
Async XLA Ops:
  0.6 5.6 %copy-start = (f32[1,48,8,4,128]{4,3,2,1,0:T(4,128)S(1)}, f32[1,48,8,4,128]{4,3,2,1,0:T(4,128)}, u32[]{:S(2)}) copy-start(f32[1,48,8,4,128]{4,3,2,1,0:T(4,128)} %param.6) | copy-start | bytes 2359300
  3.2 7.0 %collective-permute-start.2 = (f32[32,128]{1,0:T(8,128)}, f32[32,128]{1,0:T(8,128)S(1)}, u32[]{:S(2)}, u32[]{:S(2)}) collective-permute-start(f32[32,128]{1,0:T(8,128)} %weigh.1), channel_id=1, source_target_pairs={{0,3},{1,2},{2,1},{3,0},{4,7},{5,6},{6,5},{7,4},{8,11},{9,10},{10,... | collective-permute-start | bytes 49160 | tf_op jit(solution)/shard_map/ppermute | solution.py:193
  5.6 5.7 %collective-permute-start.1 = (f32[32,128]{1,0:T(8,128)}, f32[32,128]{1,0:T(8,128)S(1)}, u32[]{:S(2)}, u32[]{:S(2)}) collective-permute-start(f32[32,128]{1,0:T(8,128)} %weigh.1), channel_id=1, source_target_pairs={{0,2},{1,3},{2,0},{3,1},{4,6},{5,7},{6,4},{7,5},{8,10},{9,11},{10,... | collective-permute-start | bytes 49160 | tf_op jit(solution)/shard_map/ppermute | solution.py:193
  6.2 5.1 %collective-permute-start = (f32[32,128]{1,0:T(8,128)}, f32[32,128]{1,0:T(8,128)S(1)}, u32[]{:S(2)}, u32[]{:S(2)}) collective-permute-start(f32[32,128]{1,0:T(8,128)} %weigh.1), channel_id=1, source_target_pairs={{0,1},{1,0},{2,3},{3,2},{4,5},{5,4},{6,7},{7,6},{8,9},{9,8},{10,11... | collective-permute-start | bytes 49160 | tf_op jit(solution)/shard_map/ppermute | solution.py:193
  6.3 5.0 %copy-start.1 = (f32[32,128]{1,0:T(8,128)S(1)}, f32[32,128]{1,0:T(8,128)}, u32[]{:S(2)}) copy-start(f32[32,128]{1,0:T(8,128)} %weigh.1) | copy-start | bytes 49156
  6.3 19.6 %collective-permute-start.6 = (f32[6,32,128]{2,1,0:T(8,128)S(1)}, f32[6,32,128]{2,1,0:T(8,128)S(1)}, u32[]{:S(2)}, u32[]{:S(2)}) collective-permute-start(f32[6,32,128]{2,1,0:T(8,128)S(1)} %get-tuple-element.26), channel_id=1, source_target_pairs={{0,12},{4,0},{8,4},{12,8},{1,13},{5,1},{9,5},{13,9},{2,14},{6,2},{... | collective-permute-start | bytes 294920 | tf_op jit(solution)/shard_map/ppermute | solution.py:210
  10.2 17.4 %collective-permute-start.7 = (f32[6,32,128]{2,1,0:T(8,128)S(1)}, f32[6,32,128]{2,1,0:T(8,128)S(1)}, u32[]{:S(2)}, u32[]{:S(2)}) collective-permute-start(f32[6,32,128]{2,1,0:T(8,128)S(1)} %get-tuple-element.27), channel_id=1, source_target_pairs={{0,8},{4,12},{8,0},{12,4},{1,9},{5,13},{9,1},{13,5},{2,10},{6,14},... | collective-permute-start | bytes 294920 | tf_op jit(solution)/shard_map/ppermute | solution.py:210
  10.2 1.0 %copy-start.2 = (f32[8,4,128]{2,1,0:T(4,128)S(1)}, f32[8,4,128]{2,1,0:T(4,128)}, u32[]{:S(2)}) copy-start(f32[8,4,128]{2,1,0:T(4,128)} %param.5) | copy-start | bytes 49156
  10.2 17.4 %collective-permute-start.8 = (f32[6,32,128]{2,1,0:T(8,128)S(1)}, f32[6,32,128]{2,1,0:T(8,128)S(1)}, u32[]{:S(2)}, u32[]{:S(2)}) collective-permute-start(f32[6,32,128]{2,1,0:T(8,128)S(1)} %get-tuple-element.28), channel_id=1, source_target_pairs={{0,4},{4,8},{8,12},{12,0},{1,5},{5,9},{9,13},{13,1},{2,6},{6,10},{... | collective-permute-start | bytes 294920 | tf_op jit(solution)/shard_map/ppermute | solution.py:210
  11.3 6.6 %collective-permute-start.3 = (f32[2,32,128]{2,1,0:T(8,128)S(1)}, f32[2,32,128]{2,1,0:T(8,128)S(1)}, u32[]{:S(2)}, u32[]{:S(2)}) collective-permute-start(f32[2,32,128]{2,1,0:T(8,128)S(1)} %pad_maximum_fusion.refs_0_), channel_id=1, source_target_pairs={{0,12},{4,0},{8,4},{12,8},{1,13},{5,1},{9,5},{13,9},{2,14},{6,2},{... | collective-permute-start | bytes 98312 | tf_op jit(solution)/shard_map/ppermute | solution.py:210
  14.2 7.7 %collective-permute-start.4 = (f32[2,32,128]{2,1,0:T(8,128)S(1)}, f32[2,32,128]{2,1,0:T(8,128)S(1)}, u32[]{:S(2)}, u32[]{:S(2)}) collective-permute-start(f32[2,32,128]{2,1,0:T(8,128)S(1)} %pad_maximum_fusion.refs_0_), channel_id=1, source_target_pairs={{0,8},{4,12},{8,0},{12,4},{1,9},{5,13},{9,1},{13,5},{2,10},{6,14},... | collective-permute-start | bytes 98312 | tf_op jit(solution)/shard_map/ppermute | solution.py:210
  17.9 7.0 %collective-permute-start.5 = (f32[2,32,128]{2,1,0:T(8,128)S(1)}, f32[2,32,128]{2,1,0:T(8,128)S(1)}, u32[]{:S(2)}, u32[]{:S(2)}) collective-permute-start(f32[2,32,128]{2,1,0:T(8,128)S(1)} %pad_maximum_fusion.refs_0_), channel_id=1, source_target_pairs={{0,4},{4,8},{8,12},{12,0},{1,5},{5,9},{9,13},{13,1},{2,6},{6,10},{... | collective-permute-start | bytes 98312 | tf_op jit(solution)/shard_map/ppermute | solution.py:210
  21.9 11.5 %collective-permute-start.12 = (f32[6,32,128]{2,1,0:T(8,128)S(1)}, f32[6,32,128]{2,1,0:T(8,128)S(1)}, u32[]{:S(2)}, u32[]{:S(2)}) collective-permute-start(f32[6,32,128]{2,1,0:T(8,128)S(1)} %get-tuple-element.35), channel_id=1, source_target_pairs={{0,12},{4,0},{8,4},{12,8},{1,13},{5,1},{9,5},{13,9},{2,14},{6,2},{... | collective-permute-start | bytes 294920 | tf_op jit(solution)/shard_map/ppermute | solution.py:210
  24.9 10.6 %collective-permute-start.13 = (f32[6,32,128]{2,1,0:T(8,128)S(1)}, f32[6,32,128]{2,1,0:T(8,128)S(1)}, u32[]{:S(2)}, u32[]{:S(2)}) collective-permute-start(f32[6,32,128]{2,1,0:T(8,128)S(1)} %get-tuple-element.36), channel_id=1, source_target_pairs={{0,8},{4,12},{8,0},{12,4},{1,9},{5,13},{9,1},{13,5},{2,10},{6,14},... | collective-permute-start | bytes 294920 | tf_op jit(solution)/shard_map/ppermute | solution.py:210
  25.9 9.6 %collective-permute-start.14 = (f32[6,32,128]{2,1,0:T(8,128)S(1)}, f32[6,32,128]{2,1,0:T(8,128)S(1)}, u32[]{:S(2)}, u32[]{:S(2)}) collective-permute-start(f32[6,32,128]{2,1,0:T(8,128)S(1)} %get-tuple-element.37), channel_id=1, source_target_pairs={{0,4},{4,8},{8,12},{12,0},{1,5},{5,9},{9,13},{13,1},{2,6},{6,10},{... | collective-permute-start | bytes 294920 | tf_op jit(solution)/shard_map/ppermute | solution.py:210
  30.5 11.7 %collective-permute-start.9 = (f32[6,32,128]{2,1,0:T(8,128)S(1)}, f32[6,32,128]{2,1,0:T(8,128)S(1)}, u32[]{:S(2)}, u32[]{:S(2)}) collective-permute-start(f32[6,32,128]{2,1,0:T(8,128)S(1)} %get-tuple-element.31), channel_id=1, source_target_pairs={{0,4},{4,8},{8,12},{12,0},{1,5},{5,9},{9,13},{13,1},{2,6},{6,10},{... | collective-permute-start | bytes 294920 | tf_op jit(solution)/shard_map/ppermute | solution.py:210
  32.2 14.0 %collective-permute-start.10 = (f32[6,32,128]{2,1,0:T(8,128)S(1)}, f32[6,32,128]{2,1,0:T(8,128)S(1)}, u32[]{:S(2)}, u32[]{:S(2)}) collective-permute-start(f32[6,32,128]{2,1,0:T(8,128)S(1)} %get-tuple-element.32), channel_id=1, source_target_pairs={{0,8},{4,12},{8,0},{12,4},{1,9},{5,13},{9,1},{13,5},{2,10},{6,14},... | collective-permute-start | bytes 294920 | tf_op jit(solution)/shard_map/ppermute | solution.py:210
  33.4 12.9 %collective-permute-start.11 = (f32[6,32,128]{2,1,0:T(8,128)S(1)}, f32[6,32,128]{2,1,0:T(8,128)S(1)}, u32[]{:S(2)}, u32[]{:S(2)}) collective-permute-start(f32[6,32,128]{2,1,0:T(8,128)S(1)} %get-tuple-element.33), channel_id=1, source_target_pairs={{0,12},{4,0},{8,4},{12,8},{1,13},{5,1},{9,5},{13,9},{2,14},{6,2},{... | collective-permute-start | bytes 294920 | tf_op jit(solution)/shard_map/ppermute | solution.py:210
  38.4 7.8 %collective-permute-start.15 = (f32[6,32,128]{2,1,0:T(8,128)S(1)}, f32[6,32,128]{2,1,0:T(8,128)S(1)}, u32[]{:S(2)}, u32[]{:S(2)}) collective-permute-start(f32[6,32,128]{2,1,0:T(8,128)S(1)} %get-tuple-element.39), channel_id=1, source_target_pairs={{0,4},{4,8},{8,12},{12,0},{1,5},{5,9},{9,13},{13,1},{2,6},{6,10},{... | collective-permute-start | bytes 294920 | tf_op jit(solution)/shard_map/ppermute | solution.py:210
  39.1 9.7 %collective-permute-start.16 = (f32[6,32,128]{2,1,0:T(8,128)S(1)}, f32[6,32,128]{2,1,0:T(8,128)S(1)}, u32[]{:S(2)}, u32[]{:S(2)}) collective-permute-start(f32[6,32,128]{2,1,0:T(8,128)S(1)} %get-tuple-element.40), channel_id=1, source_target_pairs={{0,8},{4,12},{8,0},{12,4},{1,9},{5,13},{9,1},{13,5},{2,10},{6,14},... | collective-permute-start | bytes 294920 | tf_op jit(solution)/shard_map/ppermute | solution.py:210
  42.2 6.5 %collective-permute-start.17 = (f32[6,32,128]{2,1,0:T(8,128)S(1)}, f32[6,32,128]{2,1,0:T(8,128)S(1)}, u32[]{:S(2)}, u32[]{:S(2)}) collective-permute-start(f32[6,32,128]{2,1,0:T(8,128)S(1)} %get-tuple-element.41), channel_id=1, source_target_pairs={{0,12},{4,0},{8,4},{12,8},{1,13},{5,1},{9,5},{13,9},{2,14},{6,2},{... | collective-permute-start | bytes 294920 | tf_op jit(solution)/shard_map/ppermute | solution.py:210
